TPU v7x, 32 devices: a whole 2x2x4 slice. The times are simulated.
32 devices in a mesh: groups: 2 (over y), seq: 4 (over z), head: 2 (over x), rep: 2 (over core).
Axes of the slice: x: 2, y: 2, z: 4, core: 2. Of those that a mesh axis runs over, the one named last changes fastest.
Arguments:
- queries: bfloat16 [32, 128, 1280], P(('groups', 'seq', 'rep'), None, 'head'), parts along dimension 0, may hold values from -5.5 to 5.5
- response_keys: bfloat16 [32, 128, 256], P(('groups', 'seq', 'rep'), None, 'head'), parts along dimension 0, may hold values from -6 to 6
- response_values: bfloat16 [32, 128, 256], P(('groups', 'seq', 'rep'), None, 'head'), parts along dimension 0, may hold values from -14 to 14
- grad_out: bfloat16 [32, 128, 1280], P(('groups', 'seq', 'rep'), None, 'head'), parts along dimension 0, may hold values from -6 to 6
- prompt_keys: bfloat16 [4096, 256], P(('groups', 'seq'), 'head'), parts along dimension 0, may hold values from -5.5 to 5.5
- prompt_values: bfloat16 [4096, 256], P(('groups', 'seq'), 'head'), parts along dimension 0, may hold values from -14 to 14
- packing: int32 [32], P('groups'), parts along dimension 0, may hold values from 0 to 15, each once
- lengths: int32 [32], P(('groups', 'seq', 'rep')), parts along dimension 0, may hold values from 1 to 128
- tree_mask: int32 [32, 2], P(('groups', 'seq', 'rep')), parts along dimension 0, may hold values from 0 to 1, as said below
Outputs:
- attended: bfloat16 [32, 128, 1280], P(('groups', 'seq', 'rep'), None, 'head'), parts along dimension 0
- grad_queries: bfloat16 [32, 128, 1280], P(('groups', 'seq', 'rep'), None, 'head'), parts along dimension 0
- grad_keys: bfloat16 [32, 128, 256], P(('groups', 'seq', 'rep'), None, 'head'), parts along dimension 0
- grad_values: bfloat16 [32, 128, 256], P(('groups', 'seq', 'rep'), None, 'head'), parts along dimension 0
- prompt_grads: float32 [2, 4096, 256], P(None, ('groups', 'seq'), 'head'), parts along dimension 1
There are 2 independent parts, one for each index of `groups`. A program takes and returns all parts, laid end to end along the dimension named above; each array names one. Nothing has to cross between parts.
Inputs may be any that keep to these rules, and one draw needn't show every extreme that they name: `tree_mask`: row s of each aligned block of 2 rows has 1 in column s and in the columns of its ancestors along a parent chain of earlier segments of the block, 0 elsewhere.
All inputs are finite; a program needn't handle non-finite values.
Results may differ from a plain program's by a relative error of at most 0.012.
The roundings to bfloat16 on the way count: a program that leaves them out, or rounds other values in their place, can miss the bound.
Values may be sent and summed in bfloat16 or wider, within the bound.
No kernel may reach another device: no remote copies, remote signals or barrier semaphores. Data moves between devices by JAX's collectives and lax.ppermute only.
A program may use at most 64 MiB of HBM per device.

v0:
```python
import jax
import jax.numpy as jnp
from jax import lax
from jax.sharding import PartitionSpec as P


def relay_rows(query_part, key_part, value_part, grad_part, packing):
    banded = (
        lax.all_to_all(query_part, ("seq", "rep"), split_axis=1, concat_axis=0, tiled=True),
        lax.all_to_all(key_part, ("seq", "rep"), split_axis=1, concat_axis=0, tiled=True),
        lax.all_to_all(value_part, ("seq", "rep"), split_axis=1, concat_axis=0, tiled=True),
        lax.all_to_all(grad_part, ("seq", "rep"), split_axis=1, concat_axis=0, tiled=True),
    )
    picked = tuple((jnp.take(entry, packing, axis=0) for entry in banded))
    moved = (
        lax.all_to_all(picked[0], ("seq", "rep"), split_axis=0, concat_axis=1, tiled=True),
        lax.all_to_all(picked[1], ("seq", "rep"), split_axis=0, concat_axis=1, tiled=True),
        lax.all_to_all(picked[2], ("seq", "rep"), split_axis=0, concat_axis=1, tiled=True),
        lax.all_to_all(picked[3], ("seq", "rep"), split_axis=0, concat_axis=1, tiled=True),
    )
    return moved


def per_device(
    queries,
    response_keys,
    response_values,
    grad_out,
    prompt_keys,
    prompt_values,
    packing,
    lengths,
    tree_mask,
):
    seg_count = lengths.shape[0]
    head_size = prompt_keys.shape[1]
    group_heads = queries.shape[2] // head_size
    softmax_scale = head_size ** (-0.5)
    moved = relay_rows(queries, response_keys, response_values, grad_out, packing)
    seg_length = moved[0].shape[1]
    row_count = seg_count * seg_length
    query_rows = moved[0].reshape(row_count, group_heads * head_size)
    key_rows = moved[1].reshape(row_count, head_size)
    value_rows = moved[2].reshape(row_count, head_size)
    grad_rows = moved[3].reshape(row_count, group_heads * head_size)
    full_keys, full_values = (
        lax.all_gather(prompt_keys, "seq", axis=0, tiled=True),
        lax.all_gather(prompt_values, "seq", axis=0, tiled=True),
    )
    position = jnp.arange(row_count)
    slot_of = position // seg_length
    within = position % seg_length
    slot_hot = (slot_of[:, None] == jnp.arange(seg_count)[None, :]).astype(jnp.int32)
    row_length = jnp.dot(slot_hot, lengths)
    live_rows = within < row_length
    live_float = live_rows.astype(jnp.float32)
    live_bf = live_rows.astype(jnp.bfloat16)
    tree_pairs = jnp.dot(jnp.dot(slot_hot, tree_mask), slot_hot.T)
    visible = (tree_pairs == 1) & live_rows[None, :]
    visible = visible & (
        (slot_of[:, None] != slot_of[None, :]) | (within[None, :] <= within[:, None])
    )
    attended_list = []
    grad_query_list = []
    tree_key_acc = jnp.zeros((row_count, head_size), jnp.float32)
    tree_value_acc = jnp.zeros((row_count, head_size), jnp.float32)
    prompt_key_acc = jnp.zeros(full_keys.shape, jnp.float32)
    prompt_value_acc = jnp.zeros(full_keys.shape, jnp.float32)
    for head_index in range(group_heads):
        query_head = query_rows[:, head_index * head_size : (head_index + 1) * head_size]
        grad_head = (
            grad_rows[:, head_index * head_size : (head_index + 1) * head_size] * live_bf[:, None]
        )
        prompt_scores = (
            jnp.dot(query_head, full_keys.T, preferred_element_type=jnp.float32) * softmax_scale
        )
        tree_scores = (
            jnp.dot(query_head, key_rows.T, preferred_element_type=jnp.float32) * softmax_scale
        )
        tree_scores = jnp.where(visible, tree_scores, -1e30)
        row_max = jnp.maximum(jnp.max(prompt_scores, axis=-1), jnp.max(tree_scores, axis=-1))
        prompt_exp = jnp.exp(prompt_scores - row_max[:, None])
        tree_exp = jnp.exp(tree_scores - row_max[:, None])
        denominator = jnp.sum(prompt_exp, axis=-1) + jnp.sum(tree_exp, axis=-1)
        prompt_probs = prompt_exp / denominator[:, None]
        tree_probs = tree_exp / denominator[:, None]
        prompt_round = prompt_probs.astype(jnp.bfloat16)
        tree_round = tree_probs.astype(jnp.bfloat16)
        weighted = jnp.dot(prompt_round, full_values, preferred_element_type=jnp.float32)
        weighted = weighted + jnp.dot(tree_round, value_rows, preferred_element_type=jnp.float32)
        attended_head = (weighted * live_float[:, None]).astype(jnp.bfloat16)
        delta = jnp.sum(grad_head.astype(jnp.float32) * attended_head.astype(jnp.float32), axis=-1)
        prompt_dprob = jnp.dot(grad_head, full_values.T, preferred_element_type=jnp.float32)
        tree_dprob = jnp.dot(grad_head, value_rows.T, preferred_element_type=jnp.float32)
        prompt_dscore = (prompt_probs * (prompt_dprob - delta[:, None])).astype(jnp.bfloat16)
        tree_dscore = (tree_probs * (tree_dprob - delta[:, None])).astype(jnp.bfloat16)
        grad_query = jnp.dot(prompt_dscore, full_keys, preferred_element_type=jnp.float32)
        grad_query = grad_query + jnp.dot(tree_dscore, key_rows, preferred_element_type=jnp.float32)
        grad_query_list.append((softmax_scale * grad_query).astype(jnp.bfloat16))
        attended_list.append(attended_head)
        tree_key_acc = tree_key_acc + jnp.dot(
            tree_dscore.T, query_head, preferred_element_type=jnp.float32
        )
        tree_value_acc = tree_value_acc + jnp.dot(
            tree_round.T, grad_head, preferred_element_type=jnp.float32
        )
        prompt_key_acc = prompt_key_acc + jnp.dot(
            prompt_dscore.T, query_head, preferred_element_type=jnp.float32
        )
        prompt_value_acc = prompt_value_acc + jnp.dot(
            prompt_round.T, grad_head, preferred_element_type=jnp.float32
        )
    attended = jnp.concatenate(attended_list, axis=-1).reshape(
        seg_count, seg_length, group_heads * head_size
    )
    grad_queries = jnp.concatenate(grad_query_list, axis=-1).reshape(
        seg_count, seg_length, group_heads * head_size
    )
    grad_keys = (
        (softmax_scale * tree_key_acc)
        .astype(jnp.bfloat16)
        .reshape(seg_count, seg_length, head_size)
    )
    grad_values = tree_value_acc.astype(jnp.bfloat16).reshape(seg_count, seg_length, head_size)
    prompt_key_acc = softmax_scale * prompt_key_acc
    summed_keys, summed_values = lax.psum((prompt_key_acc, prompt_value_acc), ("seq", "rep"))
    share_rows = summed_keys.shape[0] // lax.axis_size("seq")
    share_start = lax.axis_index("seq") * share_rows
    own_keys = lax.dynamic_slice_in_dim(summed_keys, share_start, share_rows, 0)
    own_values = lax.dynamic_slice_in_dim(summed_values, share_start, share_rows, 0)
    prompt_grads = jnp.stack([own_keys, own_values])
    return (attended, grad_queries, grad_keys, grad_values, prompt_grads)


def solution(mesh):
    in_specs = (
        P(("groups", "seq", "rep"), None, "head"),
        P(("groups", "seq", "rep"), None, "head"),
        P(("groups", "seq", "rep"), None, "head"),
        P(("groups", "seq", "rep"), None, "head"),
        P(("groups", "seq"), "head"),
        P(("groups", "seq"), "head"),
        P("groups"),
        P(("groups", "seq", "rep")),
        P(("groups", "seq", "rep"), None),
    )
    out_specs = (
        P(("groups", "seq", "rep"), None, "head"),
        P(("groups", "seq", "rep"), None, "head"),
        P(("groups", "seq", "rep"), None, "head"),
        P(("groups", "seq", "rep"), None, "head"),
        P(None, ("groups", "seq"), "head"),
    )
    return jax.shard_map(
        per_device, mesh=mesh, in_specs=in_specs, out_specs=out_specs, check_vma=False
    )
```

profile of v0, /device:TPU:0, one launch (start us, length us, event | category | flops | bytes accessed | tf_op | source)
XLA Modules:
  0.0 258.7 jit_solution(14727381347529049941)
XLA Ops:
  7.2 1.5 copy.79
  8.8 6.3 %all-to-all-start.2 = ((bf16[2,128,128]{2,0,1:T(2,128)(2,1)}), bf16[2,128,128]{2,0,1:T(2,128)(2,1)S(1)}, u32[]{:S(2)}, u32[]{:S(2)}) async-start(bf16[2,128,128]{2,0,1:T(2,128)(2,1)} %copy.79), calls=%async_computation.2 | async-start | bytes 131072 | tf_op jit(solution)/shard_map/all_to_all | solution.py:10
  15.1 1.5 copy.83
  16.6 4.4 %all-to-all-done.2 = bf16[2,128,128]{2,0,1:T(2,128)(2,1)S(1)} async-done(((bf16[2,128,128]{2,0,1:T(2,128)(2,1)}), bf16[2,128,128]{2,0,1:T(2,128)(2,1)S(1)}, u32[]{:S(2)}, u32[]{:S(2)}) %all-to-all-start.2) | async-done | bytes 65568 | tf_op jit(solution)/shard_map/all_to_all | solution.py:10
  21.0 3.4 %all-to-all-start.4 = ((bf16[2,128,128]{2,0,1:T(2,128)(2,1)}), bf16[2,128,128]{2,0,1:T(2,128)(2,1)S(1)}, u32[]{:S(2)}, u32[]{:S(2)}) async-start(bf16[2,128,128]{2,0,1:T(2,128)(2,1)} %copy.83), calls=%async_computation.4 | async-start | bytes 131072 | tf_op jit(solution)/shard_map/all_to_all | solution.py:11
  24.4 2.0 copy.75
  26.4 3.8 %all-to-all-done.4 = bf16[2,128,128]{2,0,1:T(2,128)(2,1)S(1)} async-done(((bf16[2,128,128]{2,0,1:T(2,128)(2,1)}), bf16[2,128,128]{2,0,1:T(2,128)(2,1)S(1)}, u32[]{:S(2)}, u32[]{:S(2)}) %all-to-all-start.4) | async-done | bytes 65568 | tf_op jit(solution)/shard_map/all_to_all | solution.py:11
  30.2 3.4 %all-to-all-start = ((bf16[2,128,640]{2,0,1:T(2,128)(2,1)}), bf16[2,128,640]{2,0,1:T(2,128)(2,1)S(1)}, u32[]{:S(2)}, u32[]{:S(2)}) async-start(bf16[2,128,640]{2,0,1:T(2,128)(2,1)} %copy.75), calls=%async_computation | async-start | bytes 655360 | tf_op jit(solution)/shard_map/all_to_all | solution.py:9
  33.6 2.0 copy.87
  35.7 9.0 %all-to-all-done = bf16[2,128,640]{2,0,1:T(2,128)(2,1)S(1)} async-done(((bf16[2,128,640]{2,0,1:T(2,128)(2,1)}), bf16[2,128,640]{2,0,1:T(2,128)(2,1)S(1)}, u32[]{:S(2)}, u32[]{:S(2)}) %all-to-all-start) | async-done | bytes 327712 | tf_op jit(solution)/shard_map/all_to_all | solution.py:9
  44.7 3.4 %all-to-all-start.6 = ((bf16[2,128,640]{2,0,1:T(2,128)(2,1)}), bf16[2,128,640]{2,0,1:T(2,128)(2,1)S(1)}, u32[]{:S(2)}, u32[]{:S(2)}) async-start(bf16[2,128,640]{2,0,1:T(2,128)(2,1)} %copy.87), calls=%async_computation.6 | async-start | bytes 655360 | tf_op jit(solution)/shard_map/all_to_all | solution.py:12
  49.7 0.7 broadcast_select_fusion.2
  50.4 8.8 %all-to-all-done.6 = bf16[2,128,640]{2,0,1:T(2,128)(2,1)S(1)} async-done(((bf16[2,128,640]{2,0,1:T(2,128)(2,1)}), bf16[2,128,640]{2,0,1:T(2,128)(2,1)S(1)}, u32[]{:S(2)}, u32[]{:S(2)}) %all-to-all-start.6) | async-done | bytes 327712 | tf_op jit(solution)/shard_map/all_to_all | solution.py:12
  59.2 3.4 %all-to-all-start.5 = ((bf16[16,16,128]{2,1,0:T(8,128)(2,1)}), bf16[16,16,128]{2,1,0:T(8,128)(2,1)S(1)}, u32[]{:S(2)}, u32[]{:S(2)}) async-start(bf16[16,16,128]{2,1,0:T(8,128)(2,1)} %get-tuple-element.43), calls=%async_computation.5 | async-start | bytes 131072 | tf_op jit(solution)/shard_map/all_to_all | solution.py:18
  64.6 3.8 %all-to-all-done.5 = bf16[16,16,128]{2,1,0:T(8,128)(2,1)S(1)} async-done(((bf16[16,16,128]{2,1,0:T(8,128)(2,1)}), bf16[16,16,128]{2,1,0:T(8,128)(2,1)S(1)}, u32[]{:S(2)}, u32[]{:S(2)}) %all-to-all-start.5) | async-done | bytes 65568 | tf_op jit(solution)/shard_map/all_to_all | solution.py:18
  68.4 3.4 %all-to-all-start.3 = ((bf16[16,16,128]{2,1,0:T(8,128)(2,1)}), bf16[16,16,128]{2,1,0:T(8,128)(2,1)S(1)}, u32[]{:S(2)}, u32[]{:S(2)}) async-start(bf16[16,16,128]{2,1,0:T(8,128)(2,1)} %get-tuple-element.44), calls=%async_computation.3 | async-start | bytes 131072 | tf_op jit(solution)/shard_map/all_to_all | solution.py:17
  71.8 1.0 broadcast_select_fusion
  72.8 4.9 %all-to-all-done.3 = bf16[16,16,128]{2,1,0:T(8,128)(2,1)S(1)} async-done(((bf16[16,16,128]{2,1,0:T(8,128)(2,1)}), bf16[16,16,128]{2,1,0:T(8,128)(2,1)S(1)}, u32[]{:S(2)}, u32[]{:S(2)}) %all-to-all-start.3) | async-done | bytes 65568 | tf_op jit(solution)/shard_map/all_to_all | solution.py:17
  77.6 3.4 %all-to-all-start.1 = ((bf16[16,16,640]{2,1,0:T(8,128)(2,1)}), bf16[16,16,640]{2,1,0:T(8,128)(2,1)S(1)}, u32[]{:S(2)}, u32[]{:S(2)}) async-start(bf16[16,16,640]{2,1,0:T(8,128)(2,1)} %get-tuple-element.42), calls=%async_computation.1 | async-start | bytes 655360 | tf_op jit(solution)/shard_map/all_to_all | solution.py:16
  81.1 20.7 %all_gather.6 = bf16[2048,128]{1,0:T(8,128)(2,1)S(1)} all-gather(bf16[512,128]{1,0:T(8,128)(2,1)S(1)} %copy-done.35), channel_id=1, replica_groups=mesh['groups'=2,'seq'=4,'head'=2,'rep'=2] {'seq'}, dimensions={0}, use_global_device_ids=true | all-gather | bytes 655360 | tf_op jit(solution)/shard_map/all_gather | solution.py:47
  101.8 16.0 %all_gather.7 = bf16[2048,128]{1,0:T(8,128)(2,1)S(1)} all-gather(bf16[512,128]{1,0:T(8,128)(2,1)S(1)} %copy-done.36), channel_id=1, replica_groups=mesh['groups'=2,'seq'=4,'head'=2,'rep'=2] {'seq'}, dimensions={0}, use_global_device_ids=true | all-gather | bytes 655360 | tf_op jit(solution)/shard_map/all_gather | solution.py:48
  119.0 4.1 %all-to-all-start.7 = ((bf16[16,16,640]{2,1,0:T(8,128)(2,1)}), bf16[16,16,640]{2,1,0:T(8,128)(2,1)}, u32[]{:S(2)}, u32[]{:S(2)}) async-start(bf16[16,16,640]{2,1,0:T(8,128)(2,1)} %get-tuple-element.41), calls=%async_computation.7 | async-start | bytes 655360 | tf_op jit(solution)/shard_map/all_to_all | solution.py:19
  123.6 1.4 fusion.192
  125.1 1.5 fusion.194
  126.6 1.5 fusion.196
  128.1 2.3 fusion.197
  130.4 2.4 fusion.195
  132.8 2.3 fusion.193
  135.1 2.3 fusion.191
  138.5 0.7 fusion.99
  139.2 1.5 fusion.198
  141.2 1.0 copy.90
  142.2 0.7 fusion.188
  142.9 1.6 copy.122
  144.5 1.6 copy.125
  146.1 1.6 copy.124
  147.6 1.6 copy.123
  149.2 1.6 copy.126
  150.8 0.8 max.39
  151.6 1.0 fusion.93
  152.7 2.2 fusion.20
  154.8 0.7 max.38
  157.8 0.7 copy-done.3
  159.9 0.7 copy-done.4
  164.5 0.8 fusion.32
  165.4 0.7 fusion.6
  166.1 0.8 fusion.33
  166.9 0.7 fusion.7
  167.7 0.8 fusion.34
  168.5 0.7 fusion.8
  169.7 0.7 fusion.5
  171.1 0.7 fusion.9
  174.5 0.7 convolution_add_fusion.3
  175.9 0.7 convolution_add_fusion.1
  176.6 1.6 convolution_add_fusion
  180.3 1.5 fusion.10
  184.2 0.9 copy.119
  185.1 0.7 copy.121
  185.9 0.9 copy.120
  187.5 0.8 fusion.63
  188.3 60.8 %all-reduce.3.cloned.1.call-done = (f32[2048,128]{1,0:T(8,128)}, f32[2048,128]{1,0:T(8,128)}) async-done(((f32[2048,128]{1,0:T(8,128)}, f32[2048,128]{1,0:T(8,128)}), (f32[2048,128]{1,0:T(8,128)}, f32[2048,128]{1,0:T(8,128)})) %all-reduce.3.cloned.1.call-update) | async-done | bytes 2097168 | tf_op jit(solution)/shard_map/psum | solution.py:126
  249.1 1.0 dynamic-slice_bitcast_fusion
  250.0 1.0 dynamic-slice_bitcast_fusion.1
  251.0 0.8 pad_maximum_fusion
  (202 shorter events, 23.3 us)
Async XLA Ops:
  7.2 110.6 %copy-start = (s32[2,2]{1,0:T(2,128)S(1)}, s32[2,2]{1,0:T(2,128)}, u32[]{:S(2)}) copy-start(s32[2,2]{1,0:T(2,128)} %param.21) | copy-start | bytes 52
  7.2 28.5 %copy-start.58 = (s32[16]{0:T(128)S(1)}, s32[16]{0:T(128)}, u32[]{:S(2)}) copy-start(s32[16]{0:T(128)} %param.19) | copy-start | bytes 196
  7.2 41.0 %copy-start.59 = (s32[2]{0:T(128)S(1)}, s32[2]{0:T(128)}, u32[]{:S(2)}) copy-start(s32[2]{0:T(128)} %param.20) | copy-start | bytes 28
  8.8 12.2 %all-to-all-start.2 = ((bf16[2,128,128]{2,0,1:T(2,128)(2,1)}), bf16[2,128,128]{2,0,1:T(2,128)(2,1)S(1)}, u32[]{:S(2)}, u32[]{:S(2)}) async-start(bf16[2,128,128]{2,0,1:T(2,128)(2,1)} %copy.79), calls=%async_computation.2 | async-start | bytes 131072 | tf_op jit(solution)/shard_map/all_to_all | solution.py:10
  21.0 9.2 %all-to-all-start.4 = ((bf16[2,128,128]{2,0,1:T(2,128)(2,1)}), bf16[2,128,128]{2,0,1:T(2,128)(2,1)S(1)}, u32[]{:S(2)}, u32[]{:S(2)}) async-start(bf16[2,128,128]{2,0,1:T(2,128)(2,1)} %copy.83), calls=%async_computation.4 | async-start | bytes 131072 | tf_op jit(solution)/shard_map/all_to_all | solution.py:11
  30.2 14.5 %all-to-all-start = ((bf16[2,128,640]{2,0,1:T(2,128)(2,1)}), bf16[2,128,640]{2,0,1:T(2,128)(2,1)S(1)}, u32[]{:S(2)}, u32[]{:S(2)}) async-start(bf16[2,128,640]{2,0,1:T(2,128)(2,1)} %copy.75), calls=%async_computation | async-start | bytes 655360 | tf_op jit(solution)/shard_map/all_to_all | solution.py:9
  44.7 14.5 %all-to-all-start.6 = ((bf16[2,128,640]{2,0,1:T(2,128)(2,1)}), bf16[2,128,640]{2,0,1:T(2,128)(2,1)S(1)}, u32[]{:S(2)}, u32[]{:S(2)}) async-start(bf16[2,128,640]{2,0,1:T(2,128)(2,1)} %copy.87), calls=%async_computation.6 | async-start | bytes 655360 | tf_op jit(solution)/shard_map/all_to_all | solution.py:12
  59.2 9.2 %all-to-all-start.5 = ((bf16[16,16,128]{2,1,0:T(8,128)(2,1)}), bf16[16,16,128]{2,1,0:T(8,128)(2,1)S(1)}, u32[]{:S(2)}, u32[]{:S(2)}) async-start(bf16[16,16,128]{2,1,0:T(8,128)(2,1)} %get-tuple-element.43), calls=%async_computation.5 | async-start | bytes 131072 | tf_op jit(solution)/shard_map/all_to_all | solution.py:18
  63.9 17.2 %copy-start.35 = (bf16[512,128]{1,0:T(8,128)(2,1)S(1)}, bf16[512,128]{1,0:T(8,128)(2,1)}, u32[]{:S(2)}) copy-start(bf16[512,128]{1,0:T(8,128)(2,1)} %param.17) | copy-start | bytes 393220
  63.9 37.9 %copy-start.36 = (bf16[512,128]{1,0:T(8,128)(2,1)S(1)}, bf16[512,128]{1,0:T(8,128)(2,1)}, u32[]{:S(2)}) copy-start(bf16[512,128]{1,0:T(8,128)(2,1)} %param.18) | copy-start | bytes 393220
  68.4 9.2 %all-to-all-start.3 = ((bf16[16,16,128]{2,1,0:T(8,128)(2,1)}), bf16[16,16,128]{2,1,0:T(8,128)(2,1)S(1)}, u32[]{:S(2)}, u32[]{:S(2)}) async-start(bf16[16,16,128]{2,1,0:T(8,128)(2,1)} %get-tuple-element.44), calls=%async_computation.3 | async-start | bytes 131072 | tf_op jit(solution)/shard_map/all_to_all | solution.py:17
  77.6 41.4 %all-to-all-start.1 = ((bf16[16,16,640]{2,1,0:T(8,128)(2,1)}), bf16[16,16,640]{2,1,0:T(8,128)(2,1)S(1)}, u32[]{:S(2)}, u32[]{:S(2)}) async-start(bf16[16,16,640]{2,1,0:T(8,128)(2,1)} %get-tuple-element.42), calls=%async_computation.1 | async-start | bytes 655360 | tf_op jit(solution)/shard_map/all_to_all | solution.py:16
  119.0 22.1 %all-to-all-start.7 = ((bf16[16,16,640]{2,1,0:T(8,128)(2,1)}), bf16[16,16,640]{2,1,0:T(8,128)(2,1)}, u32[]{:S(2)}, u32[]{:S(2)}) async-start(bf16[16,16,640]{2,1,0:T(8,128)(2,1)} %get-tuple-element.41), calls=%async_computation.7 | async-start | bytes 655360 | tf_op jit(solution)/shard_map/all_to_all | solution.py:19
  123.1 125.9 %all-reduce.3.cloned.1.call-start = ((), (), s32[]{:S(2)}) async-start(), calls=%async_computation.8 | async-start | bytes 4194304 | tf_op jit(solution)/shard_map/psum | solution.py:126
  123.6 14.9 %copy-start.5 = (f32[256,256]{0,1:T(8,128)}, f32[256,256]{0,1:T(8,128)S(1)}, u32[]{:S(2)}) copy-start(f32[256,256]{0,1:T(8,128)S(1)} %get-tuple-element.48) | copy-start | bytes 786436
  138.5 2.2 copy-start.43
  150.8 4.7 %copy-start.11 = (f32[256,256]{0,1:T(8,128)S(1)}, f32[256,256]{0,1:T(8,128)}, u32[]{:S(2)}) copy-start(f32[256,256]{0,1:T(8,128)} %get-tuple-element.66) | copy-start | bytes 786436
  150.8 4.8 %copy-start.2 = (f32[256,2048]{1,0:T(8,128)S(1)}, f32[256,2048]{1,0:T(8,128)}, u32[]{:S(2)}) copy-start(f32[256,2048]{1,0:T(8,128)} %get-tuple-element.64) | copy-start | bytes 6291460
  152.6 3.4 %copy-start.1 = (f32[256,2048]{1,0:T(8,128)S(1)}, f32[256,2048]{1,0:T(8,128)}, u32[]{:S(2)}) copy-start(f32[256,2048]{1,0:T(8,128)} %get-tuple-element.70) | copy-start | bytes 6291460
  155.5 20.4 %copy-start.37 = (f32[256]{0:T(256)}, f32[256]{0:T(256)S(1)}, u32[]{:S(2)}) copy-start(f32[256]{0:T(256)S(1)} %max.38) | copy-start | bytes 3076
  156.0 20.5 %copy-start.50 = (f32[256]{0:T(256)}, f32[256]{0:T(256)S(1)}, u32[]{:S(2)}) copy-start(f32[256]{0:T(256)S(1)} %add.161) | copy-start | bytes 3076
  156.7 19.2 %copy-start.52 = (f32[256]{0:T(256)}, f32[256]{0:T(256)S(1)}, u32[]{:S(2)}) copy-start(f32[256]{0:T(256)S(1)} %add.159) | copy-start | bytes 3076
  156.7 1.0 copy-start.13
  156.8 1.7 copy-start.3
  157.5 17.7 %copy-start.39 = (f32[256]{0:T(256)}, f32[256]{0:T(256)S(1)}, u32[]{:S(2)}) copy-start(f32[256]{0:T(256)S(1)} %max.37) | copy-start | bytes 3076
  158.9 16.3 %copy-start.54 = (f32[256]{0:T(256)}, f32[256]{0:T(256)S(1)}, u32[]{:S(2)}) copy-start(f32[256]{0:T(256)S(1)} %add.157) | copy-start | bytes 3076
  158.9 1.0 copy-start.15
  158.9 1.7 copy-start.4
  159.6 14.9 %copy-start.41 = (f32[256]{0:T(256)}, f32[256]{0:T(256)S(1)}, u32[]{:S(2)}) copy-start(f32[256]{0:T(256)S(1)} %max.36) | copy-start | bytes 3076
  161.0 13.5 %copy-start.56 = (f32[256]{0:T(256)}, f32[256]{0:T(256)S(1)}, u32[]{:S(2)}) copy-start(f32[256]{0:T(256)S(1)} %add.155) | copy-start | bytes 3076
  161.7 0.9 copy-start.9
  161.7 0.9 copy-start.34
  161.7 0.9 copy-start.49
  162.2 1.4 copy-start.17
  163.1 0.9 copy-start.7
  163.1 0.9 copy-start.26
  163.1 0.9 copy-start.28
  163.1 0.9 copy-start.30
  163.1 1.0 copy-start.32
  168.5 0.9 copy-start.6
  168.5 1.0 copy-start.44
  169.6 3.1 %copy-start.22 = (bf16[256,256]{0,1:T(8,128)(2,1)}, bf16[256,256]{0,1:T(8,128)(2,1)S(1)}, u32[]{:S(2)}) copy-start(bf16[256,256]{0,1:T(8,128)(2,1)S(1)} %fusion.31) | copy-start | bytes 393220
  180.2 1.5 copy-start.23
  180.2 1.7 copy-start.21
  180.3 2.0 copy-start.20
  180.3 2.2 copy-start.19
  182.7 1.3 copy-start.8
  182.7 1.3 copy-start.10
  182.9 1.3 copy-start.25
  183.0 3.8 %copy-start.16 = (f32[256,256]{0,1:T(8,128)S(1)}, f32[256,256]{0,1:T(8,128)}, u32[]{:S(2)}) copy-start(f32[256,256]{0,1:T(8,128)} %get-tuple-element.54) | copy-start | bytes 786436
  183.0 3.8 %copy-start.33 = (bf16[256,128]{0,1:T(8,128)(2,1)S(1)}, bf16[256,128]{0,1:T(8,128)(2,1)}, u32[]{:S(2)}) copy-start(bf16[256,128]{0,1:T(8,128)(2,1)} %copy.123) | copy-start | bytes 196612
  183.0 3.8 %copy-start.42 = (f32[256]{0:T(256)S(1)}, f32[256]{0:T(256)}, u32[]{:S(2)}) copy-start(f32[256]{0:T(256)} %copy-done.41) | copy-start | bytes 3076
  183.0 3.8 %copy-start.57 = (f32[256]{0:T(256)S(1)}, f32[256]{0:T(256)}, u32[]{:S(2)}) copy-start(f32[256]{0:T(256)} %copy-done.56) | copy-start | bytes 3076
  183.2 3.7 %copy-start.14 = (f32[256,256]{0,1:T(8,128)S(1)}, f32[256,256]{0,1:T(8,128)}, u32[]{:S(2)}) copy-start(f32[256,256]{0,1:T(8,128)} %get-tuple-element.60) | copy-start | bytes 786436
  183.2 3.7 %copy-start.31 = (bf16[256,128]{0,1:T(8,128)(2,1)S(1)}, bf16[256,128]{0,1:T(8,128)(2,1)}, u32[]{:S(2)}) copy-start(bf16[256,128]{0,1:T(8,128)(2,1)} %copy.124) | copy-start | bytes 196612
  183.3 3.7 %copy-start.40 = (f32[256]{0:T(256)S(1)}, f32[256]{0:T(256)}, u32[]{:S(2)}) copy-start(f32[256]{0:T(256)} %copy-done.39) | copy-start | bytes 3076
  183.3 3.7 %copy-start.55 = (f32[256]{0:T(256)S(1)}, f32[256]{0:T(256)}, u32[]{:S(2)}) copy-start(f32[256]{0:T(256)} %copy-done.54) | copy-start | bytes 3076
  184.0 3.2 %copy-start.12 = (f32[256,256]{0,1:T(8,128)S(1)}, f32[256,256]{0,1:T(8,128)}, u32[]{:S(2)}) copy-start(f32[256,256]{0,1:T(8,128)} %get-tuple-element.66) | copy-start | bytes 786436
  184.0 3.2 %copy-start.27 = (bf16[256,128]{0,1:T(8,128)(2,1)S(1)}, bf16[256,128]{0,1:T(8,128)(2,1)}, u32[]{:S(2)}) copy-start(bf16[256,128]{0,1:T(8,128)(2,1)} %copy.125) | copy-start | bytes 196612
  184.0 3.2 %copy-start.38 = (f32[256]{0:T(256)S(1)}, f32[256]{0:T(256)}, u32[]{:S(2)}) copy-start(f32[256]{0:T(256)} %copy-done.37) | copy-start | bytes 3076
  184.0 3.2 %copy-start.53 = (f32[256]{0:T(256)S(1)}, f32[256]{0:T(256)}, u32[]{:S(2)}) copy-start(f32[256]{0:T(256)} %copy-done.52) | copy-start | bytes 3076
  185.1 2.3 copy-start.18
  185.1 2.3 copy-start.29
  185.1 2.3 copy-start.51
  (5 other events, 3.5 us)
Sparse Core Ops, SparseCore 0:
  183.1 65.9 all-reduce.2
where the time goes:
time: 260 us; the launch traced here: 259 us
  waiting for transfers between devices  95.5 us (37%)
  matrix products  41.3 us (16%)
  blocking collectives  36.7 us (14%)
  starting transfers between devices  31 us (12%)
  local copies, waits for them, and re-layouts  27.7 us (11%)
  between operations  15.3 us (6%)
  other arithmetic  11.2 us (4%)
    psum x1, waiting for transfers between devices, per_device(): lax.psum((prompt_key_acc, prompt_value_acc), ('seq', 'rep'))  60.8 us
    unnamed x132, local copies, waits for them, and re-layouts  20.8 us
    all_gather x1, blocking collectives, per_device(): lax.all_gather(prompt_keys, 'seq', axis=0, tiled=True)  20.7 us
    all_gather x1, blocking collectives, per_device(): lax.all_gather(prompt_values, 'seq', axis=0, tiled=True)  16 us
    dot_general x5, matrix products, per_device(): jnp.dot(query_head, full_keys.T, preferred_element_type=jnp.float32)  9.88 us
    all_to_all x1, waiting for transfers between devices, relay_rows(): lax.all_to_all(query_part, ('seq', 'rep'), split_axis=1, concat_axis=0, t...  9.01 us
    all_to_all x1, waiting for transfers between devices, relay_rows(): lax.all_to_all(grad_part, ('seq', 'rep'), split_axis=1, concat_axis=0, ti...  8.81 us
    all_to_all x1, starting transfers between devices, relay_rows(): lax.all_to_all(key_part, ('seq', 'rep'), split_axis=1, concat_axis=0, til...  6.33 us
  transfers between devices with their start and end apart: 9, of which 7 were waited for; matrix products, arithmetic and copies ran while one was open for 13% of the time, Pallas kernels for 0%

commit v1 on v0

v1 whole, which is shorter than its diff:
```python
import functools

import jax
import jax.numpy as jnp
from jax import lax
from jax.experimental import pallas as pl
from jax.experimental.pallas import tpu as pltpu
from jax.sharding import PartitionSpec as P

LINE = ("seq", "rep")
NT = (((1,), (1,)), ((), ()))
NN = (((1,), (0,)), ((), ()))
LOG2E = 1.4426950408889634
VMEM = pl.BlockSpec(memory_space=pltpu.VMEM)
SMEM = pl.BlockSpec(memory_space=pltpu.SMEM)
PARAMS = pltpu.CompilerParams(vmem_limit_bytes=56 * 1024 * 1024)


def dot(left, right, dims):
    return lax.dot_general(left, right, dims, preferred_element_type=jnp.float32)


def pack_kernel(band, piece, q_ref, k_ref, v_ref, g_ref, pk_ref, pv_ref, out_ref):
    core = lax.axis_index("rep")
    devices = out_ref.shape[0]
    head_size = k_ref.shape[2]
    for dest in range(devices):
        start = pl.multiple_of((dest % 2) * 2 * piece + core * piece, 16)
        out_ref[dest, :piece, :] = pk_ref[pl.ds(start, piece), :]
        out_ref[dest, piece : 2 * piece, :] = pv_ref[pl.ds(start, piece), :]
        row = 2 * piece
        for source in (k_ref, v_ref, q_ref, g_ref):
            for tile in range(source.shape[2] // head_size):
                for slot in range(source.shape[0]):
                    out_ref[dest, row : row + band, :] = source[
                        slot, dest * band : (dest + 1) * band, tile * head_size : (tile + 1) * head_size
                    ]
                    row += band


def pack_plain(band, piece, q, k, v, g, pk, pv):
    slots, length, head_size = k.shape
    devices = length // band
    rows = jnp.concatenate([k, v, q, g], axis=2)
    tiles = rows.shape[2] // head_size
    rows = rows.reshape(slots, devices, band, tiles, head_size).transpose(1, 3, 0, 2, 4)
    rows = rows.reshape(devices, tiles * slots * band, head_size)
    core = lax.axis_index("rep")
    quarters = jnp.stack([pk, pv]).reshape(2, 2, 2, piece, head_size)
    quarters = lax.dynamic_index_in_dim(quarters, core, 2, keepdims=False)
    quarters = quarters.transpose(1, 0, 2, 3).reshape(2, 2 * piece, head_size)
    quarters = jnp.broadcast_to(quarters[None], (devices // 2, 2, 2 * piece, head_size))
    return jnp.concatenate([quarters.reshape(devices, 2 * piece, head_size), rows], axis=1)


def pick_kernel(band, skip, tiles, packing_ref, in_ref, out_ref):
    slots = 2
    for target in range(out_ref.shape[0] * slots):
        chosen = packing_ref[target]
        device = chosen // slots
        slot = chosen % slots
        for tile in range(tiles):
            out_ref[target // slots, tile * slots + target % slots] = in_ref[device, skip + tile * slots + slot]


def attend_kernel(
    band, piece, heads, natural, length_ref, tree_ref, rows_ref, own_ref, other_ref,
    att_ref, gq_ref, gk_ref, gv_ref, keep_ref, send_ref, keys, values, key_acc, value_acc,
):
    core = lax.axis_index("rep")
    head_size = rows_ref.shape[2]
    blocks = rows_ref.shape[0]
    high = rows_ref.shape[1] // (2 + 2 * heads)
    rows = blocks * high
    seg_length = rows // 2
    prompt = keys.shape[0] - rows
    scale = head_size ** (-0.5)

    def tile_of(index):
        return rows_ref[:, index * high : (index + 1) * high, :].reshape(rows, head_size)

    for source in range(own_ref.shape[0]):
        base = (source // 2) * 4 * piece + (source % 2) * piece
        for ref, half in ((own_ref, core), (other_ref, 1 - core)):
            start = pl.multiple_of(base + half * 2 * piece, 16)
            keys[pl.ds(start, piece), :] = ref[source, :piece, :]
            values[pl.ds(start, piece), :] = ref[source, piece:, :]
    keys[prompt:, :] = tile_of(0)
    values[prompt:, :] = tile_of(1)

    def place(shape, axis):
        index = lax.broadcasted_iota(jnp.int32, shape, axis)
        slot = (index % (2 * band)) // band
        return slot, (index // (2 * band)) * band + index % band

    row_slot, row_at = place((rows, rows), 0)
    col_slot, col_at = place((rows, rows), 1)
    first, second = length_ref[0], length_ref[1]
    tree = jnp.where(
        row_slot == 0,
        jnp.where(col_slot == 0, tree_ref[0, 0], tree_ref[0, 1]),
        jnp.where(col_slot == 0, tree_ref[1, 0], tree_ref[1, 1]),
    )
    visible = (
        (tree == 1)
        & (col_at < jnp.where(col_slot == 0, first, second))
        & ((row_slot != col_slot) | (col_at <= row_at))
    )
    slot, at = place((rows, head_size), 0)
    live = (at < jnp.where(slot == 0, first, second)).astype(jnp.float32)
    live_bf = live.astype(jnp.bfloat16)
    all_keys = keys[...]
    all_values = values[...]

    def put(ref, value, column):
        if natural:
            for block in range(blocks):
                for one in range(2):
                    start = block * high + one * band
                    ref[one, block * band : (block + 1) * band, column * head_size : (column + 1) * head_size] = value[
                        start : start + band, :
                    ]
        else:
            ref[column] = value

    for head in range(heads):
        query = tile_of(2 + head)
        grad = tile_of(2 + heads + head) * live_bf
        scores = dot(query, all_keys, NT)
        prompt_scores = scores[:, :prompt]
        tree_scores = jnp.where(visible, scores[:, prompt:], -1e30)
        top = jnp.maximum(
            jnp.max(prompt_scores, axis=1, keepdims=True), jnp.max(tree_scores, axis=1, keepdims=True)
        )
        scores = jnp.concatenate([prompt_scores, tree_scores], axis=1)
        powers = jnp.exp2((scores - top) * (scale * LOG2E))
        probs = powers * (1.0 / jnp.sum(powers, axis=1, keepdims=True))
        probs_b = probs.astype(jnp.bfloat16)
        attended = (dot(probs_b, all_values, NN) * live).astype(jnp.bfloat16)
        put(att_ref, attended, head)
        delta = jnp.sum(grad.astype(jnp.float32) * attended.astype(jnp.float32), axis=1, keepdims=True)
        dscore = (probs * (dot(grad, all_values, NT) - delta)).astype(jnp.bfloat16)
        put(gq_ref, (dot(dscore, all_keys, NN) * scale).astype(jnp.bfloat16), head)
        key_part = dot(query.T, dscore, NN)
        value_part = dot(grad.T, probs_b, NN)
        if head == 0:
            key_acc[...] = key_part
            value_acc[...] = value_part
        else:
            key_acc[...] += key_part
            value_acc[...] += value_part
    put(gk_ref, (key_acc[:, prompt:] * scale).T.astype(jnp.bfloat16), 0)
    put(gv_ref, value_acc[:, prompt:].T.astype(jnp.bfloat16), 0)

    @pl.when(core == 0)
    def _():
        keep_ref[...] = key_acc[:, :prompt] * scale
        send_ref[...] = value_acc[:, :prompt]

    @pl.when(core != 0)
    def _():
        keep_ref[...] = value_acc[:, :prompt]
        send_ref[...] = key_acc[:, :prompt] * scale


def swap_cores(value):
    return lax.ppermute(value, "rep", [(0, 1), (1, 0)])


def per_device(
    queries, response_keys, response_values, grad_out, prompt_keys, prompt_values, packing, lengths, tree_mask
):
    slots, seg_length, head_size = response_keys.shape
    heads = queries.shape[2] // head_size
    tiles = 2 + 2 * heads
    chips = lax.axis_size("seq")
    devices = chips * lax.axis_size("rep")
    band = seg_length // devices
    share = prompt_keys.shape[0]
    piece = share // 4
    prompt = share * chips
    rows = slots * seg_length
    natural = band % 16 == 0
    bf16 = jnp.bfloat16

    sources = (queries, response_keys, response_values, grad_out, prompt_keys, prompt_values)
    message_rows = 2 * piece + tiles * slots * band
    if natural:
        message = pl.pallas_call(
            functools.partial(pack_kernel, band, piece),
            out_shape=jax.ShapeDtypeStruct((devices, message_rows, head_size), bf16),
            in_specs=[VMEM] * 6,
            out_specs=VMEM,
            compiler_params=PARAMS,
            name="pack",
        )(*sources)
    else:
        message = pack_plain(band, piece, *sources)
    banded = lax.all_to_all(message, LINE, split_axis=0, concat_axis=0)
    prompt_own = banded[:, : 2 * piece, :]
    prompt_other = swap_cores(prompt_own)
    if natural:
        picked = pl.pallas_call(
            functools.partial(pick_kernel, band, 2 * piece // band, tiles),
            out_shape=jax.ShapeDtypeStruct((devices, tiles * slots, band, head_size), bf16),
            in_specs=[SMEM, VMEM],
            out_specs=VMEM,
            compiler_params=PARAMS,
            name="pick",
        )(packing, banded.reshape(devices, message_rows // band, band, head_size))
        moved = lax.all_to_all(picked, LINE, split_axis=0, concat_axis=0)
        moved = moved.reshape(devices, tiles * slots * band, head_size)
    else:
        held = banded[:, 2 * piece :, :].reshape(devices, tiles, slots, band, head_size)
        held = held.transpose(0, 2, 1, 3, 4).reshape(devices * slots, tiles, band, head_size)
        picked = jnp.take(held, packing, axis=0).reshape(devices, slots, tiles, band, head_size)
        moved = lax.all_to_all(picked, LINE, split_axis=0, concat_axis=0)
        moved = moved.transpose(2, 0, 1, 3, 4).reshape(1, tiles * rows, head_size)

    if natural:
        wide, narrow = (slots, seg_length, heads * head_size), (slots, seg_length, head_size)
    else:
        wide, narrow = (heads, rows, head_size), (1, rows, head_size)
    attended, grad_queries, grad_keys, grad_values, keep, send = pl.pallas_call(
        functools.partial(attend_kernel, band, piece, heads, natural),
        out_shape=[
            jax.ShapeDtypeStruct(wide, bf16),
            jax.ShapeDtypeStruct(wide, bf16),
            jax.ShapeDtypeStruct(narrow, bf16),
            jax.ShapeDtypeStruct(narrow, bf16),
            jax.ShapeDtypeStruct((head_size, prompt), jnp.float32),
            jax.ShapeDtypeStruct((head_size, prompt), jnp.float32),
        ],
        in_specs=[SMEM, SMEM, VMEM, VMEM, VMEM],
        out_specs=[VMEM] * 6,
        scratch_shapes=[
            pltpu.VMEM((prompt + rows, head_size), bf16),
            pltpu.VMEM((prompt + rows, head_size), bf16),
            pltpu.VMEM((head_size, prompt + rows), jnp.float32),
            pltpu.VMEM((head_size, prompt + rows), jnp.float32),
        ],
        compiler_params=PARAMS,
        name="attend",
    )(lengths, tree_mask, moved, prompt_own, prompt_other)
    if not natural:

        def restore(value):
            value = value.reshape(-1, devices, slots, band, head_size).transpose(2, 1, 3, 0, 4)
            return value.reshape(slots, seg_length, -1)

        attended, grad_queries, grad_keys, grad_values = (
            restore(value) for value in (attended, grad_queries, grad_keys, grad_values)
        )

    total = keep + swap_cores(send)
    parts = total.reshape(head_size, chips, share).transpose(1, 0, 2).astype(bf16)
    gathered = lax.all_to_all(parts, "seq", split_axis=0, concat_axis=0)
    own = jnp.sum(gathered.astype(jnp.float32), axis=0).T
    other = swap_cores(own)
    core = lax.axis_index("rep")
    prompt_grads = jnp.stack([jnp.where(core == 0, own, other), jnp.where(core == 0, other, own)])
    return attended, grad_queries, grad_keys, grad_values, prompt_grads


def solution(mesh):
    segments = P(("groups", "seq", "rep"), None, "head")
    in_specs = (
        segments,
        segments,
        segments,
        segments,
        P(("groups", "seq"), "head"),
        P(("groups", "seq"), "head"),
        P("groups"),
        P(("groups", "seq", "rep")),
        P(("groups", "seq", "rep"), None),
    )
    out_specs = (segments, segments, segments, segments, P(None, ("groups", "seq"), "head"))
    return jax.shard_map(per_device, mesh=mesh, in_specs=in_specs, out_specs=out_specs, check_vma=False)
```

time: 260 us -> 108 us (0.42)
  waiting for transfers between devices: 95.5 us -> 23.7 us
  matrix products: 41.3 us -> 0 us
  starting transfers between devices: 31 us -> 4.08 us
  local copies, waits for them, and re-layouts: 27.7 us -> 2.99 us
  blocking collectives: 36.7 us -> 56.1 us
  Pallas kernels: 0 us -> 18.8 us
  between operations: 15.3 us -> 0.7 us
  other arithmetic: 11.2 us -> 1.48 us
    psum x1 -> x0, waiting for transfers between devices: 60.8 us -> none  [per_device(): lax.psum((prompt_key_acc, prompt_value_acc), ('seq', 'rep'))]
    all_to_all x0 -> x2, blocking collectives: none -> 56.1 us  [the longest x1 38.6 us: per_device(): banded = lax.all_to_all(message, LINE, split_axis=0, concat_axis=0)]
    dot_general x62 -> x0, matrix products: 41.3 us -> none  [the longest x5 9.88 us: per_device(): jnp.dot(query_head, full_keys.T, preferred_element_type=jnp.float32)]
    all_gather x2 -> x0, blocking collectives: 36.7 us -> none  [the longest x1 20.7 us: per_device(): lax.all_gather(prompt_keys, 'seq', axis=0, tiled=True)]
    all_to_all x8 -> x1, starting transfers between devices: 30.8 us -> 3.55 us  [per_device(): moved = lax.all_to_all(picked, LINE, split_axis=0, concat_axis=0)]
    unnamed x132 -> x7, local copies, waits for them, and re-layouts: 20.8 us -> 1.87 us
    pallas_call x0 -> x3, Pallas kernels: none -> 18.8 us  [the longest x1 14 us: per_device(): pl.pallas_call(functools.partial(attend_kernel, band, piece, heads, natur...]
    all_to_all x8 -> x1, waiting for transfers between devices: 34.7 us -> 17.8 us  [per_device(): moved = lax.all_to_all(picked, LINE, split_axis=0, concat_axis=0)]
  transfers between devices with their start and end apart: 9 -> 4, of which waited for: 7 -> 4; matrix products, arithmetic and copies ran while one was open for 13% -> 1% of each run, Pallas kernels for 0% -> 0%
where the time goes in v1:
time: 108 us
  blocking collectives  56.1 us (52%)
  waiting for transfers between devices  23.7 us (22%)
  Pallas kernels  18.8 us (17%)
  starting transfers between devices  4.08 us (4%)
  local copies, waits for them, and re-layouts  2.99 us (3%)
  other arithmetic  1.48 us (1%)
    all_to_all x1, blocking collectives, per_device(): banded = lax.all_to_all(message, LINE, split_axis=0, concat_axis=0)  38.6 us
    all_to_all x1, waiting for transfers between devices, per_device(): moved = lax.all_to_all(picked, LINE, split_axis=0, concat_axis=0)  17.8 us
    all_to_all x1, blocking collectives, per_device(): gathered = lax.all_to_all(parts, 'seq', split_axis=0, concat_axis=0)  17.5 us
    pallas_call x1, Pallas kernels, per_device(): pl.pallas_call(functools.partial(attend_kernel, band, piece, heads, natur...  14 us
    ppermute x3, waiting for transfers between devices, swap_cores(): return lax.ppermute(value, 'rep', [(0, 1), (1, 0)])  5.92 us
    all_to_all x1, starting transfers between devices, per_device(): moved = lax.all_to_all(picked, LINE, split_axis=0, concat_axis=0)  3.55 us
    pallas_call x1, Pallas kernels, per_device(): pl.pallas_call(functools.partial(pack_kernel, band, piece), out_shape=jax...  2.46 us
    pallas_call x1, Pallas kernels, per_device(): pl.pallas_call(functools.partial(pick_kernel, band, 2 * piece // band, ti...  2.35 us
  transfers between devices with their start and end apart: 4, of which 4 were waited for; matrix products, arithmetic and copies ran while one was open for 1% of the time, Pallas kernels for 0%

profile of v1, /device:TPU:0, one launch (start us, length us, event | category | flops | bytes accessed | tf_op | source)
XLA Modules:
  0.0 107.9 jit_solution(17525973362804192873)
XLA Ops:
  0.6 2.5 %pack.1 = bf16[8,640,128]{2,1,0:T(8,128)(2,1)} custom-call(bf16[2,128,640]{2,1,0:T(8,128)(2,1)} %q_ref.1, bf16[2,128,128]{2,1,0:T(8,128)(2,1)} %k_ref.1, bf16[2,128,128]{2,1,0:T(8,128)(2,1)} %v_ref.1, bf16[2,128,640]{2,1,0:T(8,128)(2,1)} %g_ref.1, bf16[512,128]{1,0:T(8,128)(2,1)} %pk_ref.1, bf16[512,128]{1,0:T(8,128)(2,1)} %pv_ref.1), custom_call_target="tpu_custom_call" | custom-call | tf_op jit(solution)/shard_map/pack/pallas_call | solution.py:189
  3.1 38.6 %all_to_all.15 = bf16[8,640,128]{2,1,0:T(8,128)(2,1)} all-to-all(bf16[8,640,128]{2,1,0:T(8,128)(2,1)} %pack.1), channel_id=1, replica_groups=mesh['groups'=2,'seq'=4,'head'=2,'rep'=2] {'seq','rep'}, dimensions={0} | all-to-all | bytes 2621440 | tf_op jit(solution)/shard_map/all_to_all | solution.py:199
  41.7 2.3 %pick.1 = bf16[8,24,16,128]{3,2,1,0:T(8,128)(2,1)} custom-call(s32[16]{0:T(128)} %packing_ref.1, bf16[8,40,16,128]{3,2,1,0:T(8,128)(2,1)} %bitcast.16), custom_call_target="tpu_custom_call" | custom-call | tf_op jit(solution)/shard_map/pick/pallas_call | solution.py:203
  44.1 3.5 %all-to-all-start.1 = ((bf16[8,24,16,128]{3,2,1,0:T(8,128)(2,1)}), bf16[8,24,16,128]{3,2,1,0:T(8,128)(2,1)S(1)}, u32[]{:S(2)}, u32[]{:S(2)}) async-start(bf16[8,24,16,128]{3,2,1,0:T(8,128)(2,1)} %pick.1), calls=%async_computation.1 | async-start | bytes 1572864 | tf_op jit(solution)/shard_map/all_to_all | solution.py:211
  47.6 1.1 %slice.4.own_ref = bf16[8,256,128]{2,1,0:T(8,128)(2,1)S(1)} slice(bf16[8,640,128]{2,1,0:T(8,128)(2,1)} %all_to_all.15), slice={[0:8], [0:256], [0:128]} | slice | bytes 1048576 | tf_op jit(solution)/shard_map/slice | solution.py:200
  48.7 0.0 copy-start.1
  48.7 0.5 collective-permute-start
  49.2 1.5 %collective-permute-done.other_ref = bf16[8,256,128]{2,1,0:T(8,128)(2,1)S(1)} collective-permute-done((bf16[8,256,128]{2,1,0:T(8,128)(2,1)S(1)}, bf16[8,256,128]{2,1,0:T(8,128)(2,1)S(1)}, u32[]{:S(2)}, u32[]{:S(2)}) %collective-permute-start) | collective-permute-done | bytes 524320 | tf_op jit(solution)/shard_map/ppermute | solution.py:167
  50.7 0.0 copy-start.2
  50.7 17.8 %all-to-all-done.1 = bf16[8,24,16,128]{3,2,1,0:T(8,128)(2,1)S(1)} async-done(((bf16[8,24,16,128]{3,2,1,0:T(8,128)(2,1)}), bf16[8,24,16,128]{3,2,1,0:T(8,128)(2,1)S(1)}, u32[]{:S(2)}, u32[]{:S(2)}) %all-to-all-start.1) | async-done | bytes 786464 | tf_op jit(solution)/shard_map/all_to_all | solution.py:211
  68.5 0.0 copy-start
  68.5 0.0 copy-done.1
  68.5 0.0 copy-done.2
  68.5 0.9 copy-done
  69.4 14.0 %attend.1 = (bf16[2,128,640]{2,1,0:T(8,128)(2,1)}, bf16[2,128,640]{2,1,0:T(8,128)(2,1)}, bf16[2,128,128]{2,1,0:T(8,128)(2,1)}, bf16[2,128,128]{2,1,0:T(8,128)(2,...) custom-call(s32[2]{0:T(128)} %length_ref.1, s32[2,2]{1,0:T(2,128)} %tree_ref.1, bf16[8,384,128]{2,1,0:T(8,128)(2,1)} %bitcast.17, ...), custom_call_target="tpu_custom_call" | custom-call | tf_op jit(solution)/shard_map/attend/pallas_call | solution.py:224
  83.4 0.0 collective-permute-start.1
  83.4 2.9 %collective-permute-done.1 = f32[128,2048]{1,0:T(8,128)S(1)} collective-permute-done((f32[128,2048]{1,0:T(8,128)}, f32[128,2048]{1,0:T(8,128)S(1)}, u32[]{:S(2)}, u32[]{:S(2)}) %collective-permute-start.1) | collective-permute-done | bytes 1048608 | tf_op jit(solution)/shard_map/ppermute | solution.py:167
  86.3 1.3 %add_convert_fusion = bf16[128,2048]{1,0:T(8,128)(2,1)S(1)} fusion(f32[128,2048]{1,0:T(8,128)} %get-tuple-element.15, f32[128,2048]{1,0:T(8,128)S(1)} %collective-permute-done.1), kind=kLoop, calls=%fused_computation.1 | loop fusion | flops 524288 | bytes 2621440 | tf_op jit(solution)/shard_map/convert_element_type | solution.py:256
  87.7 17.5 %all_to_all.16 = bf16[4,128,512]{2,1,0:T(8,128)(2,1)S(1)} all-to-all(bf16[4,128,512]{2,1,0:T(8,128)(2,1)S(1)} %bitcast.19), channel_id=1, replica_groups=mesh['groups'=2,'seq'=4,'head'=2,'rep'=2] {'seq'}, dimensions={0} | all-to-all | bytes 1048576 | tf_op jit(solution)/shard_map/all_to_all | solution.py:257
  105.1 0.1 convert_reduce_fusion
  105.2 0.1 collective-permute-start.2
  105.3 1.5 %collective-permute-done.2 = f32[512,128]{0,1:T(8,128)S(1)} collective-permute-done((f32[512,128]{0,1:T(8,128)S(1)}, f32[512,128]{0,1:T(8,128)S(1)}, u32[]{:S(2)}, u32[]{:S(2)}) %collective-permute-start.2) | collective-permute-done | bytes 262176 | tf_op jit(solution)/shard_map/ppermute | solution.py:167
  106.9 1.0 copy.16
  (3 shorter events, 0.1 us)
Async XLA Ops:
  44.1 24.4 %all-to-all-start.1 = ((bf16[8,24,16,128]{3,2,1,0:T(8,128)(2,1)}), bf16[8,24,16,128]{3,2,1,0:T(8,128)(2,1)S(1)}, u32[]{:S(2)}, u32[]{:S(2)}) async-start(bf16[8,24,16,128]{3,2,1,0:T(8,128)(2,1)} %pick.1), calls=%async_computation.1 | async-start | bytes 1572864 | tf_op jit(solution)/shard_map/all_to_all | solution.py:211
  48.7 19.8 %copy-start.1 = (bf16[8,256,128]{2,1,0:T(8,128)(2,1)}, bf16[8,256,128]{2,1,0:T(8,128)(2,1)S(1)}, u32[]{:S(2)}) copy-start(bf16[8,256,128]{2,1,0:T(8,128)(2,1)S(1)} %slice.4.own_ref) | copy-start | bytes 1572868
  48.7 2.0 %collective-permute-start = (bf16[8,256,128]{2,1,0:T(8,128)(2,1)S(1)}, bf16[8,256,128]{2,1,0:T(8,128)(2,1)S(1)}, u32[]{:S(2)}, u32[]{:S(2)}) collective-permute-start(bf16[8,256,128]{2,1,0:T(8,128)(2,1)S(1)} %slice.4.own_ref), channel_id=1, source_target_pairs={{0,1},{1,0},{2,3},{3,2},{4,5},{5,4},{6,7},{7,6},{8,9},{9,8},{10,11... | collective-permute-start | bytes 1572872 | tf_op jit(solution)/shard_map/ppermute | solution.py:167
  50.7 17.8 %copy-start.2 = (bf16[8,256,128]{2,1,0:T(8,128)(2,1)}, bf16[8,256,128]{2,1,0:T(8,128)(2,1)S(1)}, u32[]{:S(2)}) copy-start(bf16[8,256,128]{2,1,0:T(8,128)(2,1)S(1)} %collective-permute-done.other_ref) | copy-start | bytes 1572868
  68.5 0.9 copy-start
  83.4 2.9 %collective-permute-start.1 = (f32[128,2048]{1,0:T(8,128)}, f32[128,2048]{1,0:T(8,128)S(1)}, u32[]{:S(2)}, u32[]{:S(2)}) collective-permute-start(f32[128,2048]{1,0:T(8,128)} %get-tuple-element.16), channel_id=1, source_target_pairs={{0,1},{1,0},{2,3},{3,2},{4,5},{5,4},{6,7},{7,6},{8,9},{9,8},{10,11... | collective-permute-start | bytes 3145736 | tf_op jit(solution)/shard_map/ppermute | solution.py:167
  105.2 1.6 %collective-permute-start.2 = (f32[512,128]{0,1:T(8,128)S(1)}, f32[512,128]{0,1:T(8,128)S(1)}, u32[]{:S(2)}, u32[]{:S(2)}) collective-permute-start(f32[512,128]{0,1:T(8,128)S(1)} %bitcast.20), channel_id=1, source_target_pairs={{0,1},{1,0},{2,3},{3,2},{4,5},{5,4},{6,7},{7,6},{8,9},{9,8},{10,11... | collective-permute-start | bytes 786440 | tf_op jit(solution)/shard_map/ppermute | solution.py:167

commit v2 on v1

v2 whole, which is shorter than its diff:
```python
import functools

import jax
import jax.numpy as jnp
from jax import lax
from jax.experimental import pallas as pl
from jax.experimental.pallas import tpu as pltpu
from jax.sharding import PartitionSpec as P

NT = (((1,), (1,)), ((), ()))
NN = (((1,), (0,)), ((), ()))
LOG2E = 1.4426950408889634
SPLIT = (5,)
VMEM = pl.BlockSpec(memory_space=pltpu.VMEM)
SMEM = pl.BlockSpec(memory_space=pltpu.SMEM)
SMALL = pltpu.CompilerParams(vmem_limit_bytes=8 * 1024 * 1024)
LARGE = pltpu.CompilerParams(vmem_limit_bytes=36 * 1024 * 1024)


def dot(left, right, dims):
    return lax.dot_general(left, right, dims, preferred_element_type=jnp.float32)


def chunk_tiles(split):
    chunks, head = [], 0
    for count in split:
        part = [(0, 0), (1, 0)] if head == 0 else []
        part += [(2, one) for one in range(head, head + count)] + [(3, one) for one in range(head, head + count)]
        chunks.append(part)
        head += count
    return chunks


def pack_kernel(band, chunks, k_ref, v_ref, q_ref, g_ref, *outs):
    me = lax.axis_index("seq")
    sources = (k_ref, v_ref, q_ref, g_ref)
    size = k_ref.shape[2]
    chips = len(outs) // len(chunks)
    for number, chunk in enumerate(chunks):
        for far in range(chips):
            out = outs[number * chips + far]
            start = pl.multiple_of((me ^ far) * band, 16)
            row = 0
            for source, tile in chunk:
                for slot in range(k_ref.shape[0]):
                    out[row : row + band, :] = sources[source][
                        slot, pl.ds(start, band), tile * size : (tile + 1) * size
                    ]
                    row += band


def pick_kernel(band, chips, packing_ref, *refs):
    pieces, outs, held = refs[: 2 * chips], refs[2 * chips : 3 * chips], refs[3 * chips]
    me = lax.axis_index("seq")
    core = lax.axis_index("rep")
    for number, piece in enumerate(pieces):
        held[number] = piece[...]
    tiles = outs[0].shape[0] // (2 * band)
    for far in range(chips):
        for slot in range(2):
            chosen = packing_ref[((me ^ far) * 2 + core) * 2 + slot]
            device = chosen // 2
            number = ((device // 2) ^ me) + chips * ((device % 2) ^ core)
            for tile in range(tiles):
                start = pl.multiple_of(tile * 2 * band + (chosen % 2) * band, 16)
                row = tile * 2 * band + slot * band
                outs[far][row : row + band, :] = held[number, pl.ds(start, band), :]


def attend_kernel(
    band, heads, head_from, last, xor, natural, own_count, row_count, length_ref, tree_ref, *refs
):
    refs = list(refs)

    def take(count):
        taken = refs[:count]
        del refs[:count]
        return taken

    first = head_from == 0
    key_rows = take(row_count)
    head_rows = key_rows if first else take(row_count)
    own_refs, other_refs = take(own_count), take(own_count)
    before = [] if first else take(4)
    att_ref, gq_ref = take(2)
    results = take(4 if last else 2)
    keys, values, key_acc, value_acc = take(4)
    core = lax.axis_index("rep")
    me = lax.axis_index("seq") if xor else 0
    size = key_rows[0].shape[1]
    high = 2 * band if xor else key_acc.shape[1] - sum(ref.shape[0] for ref in own_refs)
    rows = high * row_count
    prompt = keys.shape[0] - rows
    share = prompt // own_count
    scale = size ** (-0.5)

    def tile_of(source, index):
        parts = [ref[index * high : (index + 1) * high, :] for ref in source]
        return parts[0] if len(parts) == 1 else jnp.concatenate(parts, axis=0)

    @pl.when(core == 0)
    def _():
        for number in range(own_count):
            keys[number * share : (number + 1) * share, :] = own_refs[number][...]
            values[number * share : (number + 1) * share, :] = other_refs[number][...]

    @pl.when(core != 0)
    def _():
        for number in range(own_count):
            keys[number * share : (number + 1) * share, :] = other_refs[number][...]
            values[number * share : (number + 1) * share, :] = own_refs[number][...]

    keys[prompt:, :] = tile_of(key_rows, 0)
    values[prompt:, :] = tile_of(key_rows, 1)

    def place(shape, axis):
        index = lax.broadcasted_iota(jnp.int32, shape, axis)
        slot = (index % (2 * band)) // band
        return slot, ((index // (2 * band)) ^ me) * band + index % band

    row_slot, row_at = place((rows, rows), 0)
    col_slot, col_at = place((rows, rows), 1)
    length_a, length_b = length_ref[0], length_ref[1]
    tree = jnp.where(
        row_slot == 0,
        jnp.where(col_slot == 0, tree_ref[0, 0], tree_ref[0, 1]),
        jnp.where(col_slot == 0, tree_ref[1, 0], tree_ref[1, 1]),
    )
    visible = (
        (tree == 1)
        & (col_at < jnp.where(col_slot == 0, length_a, length_b))
        & ((row_slot != col_slot) | (col_at <= row_at))
    )
    slot, at = place((rows, size), 0)
    live = (at < jnp.where(slot == 0, length_a, length_b)).astype(jnp.float32)
    live_bf = live.astype(jnp.bfloat16)
    all_keys = keys[...]
    all_values = values[...]

    def put(ref, value, column):
        if natural:
            for number in range(row_count):
                for one in range(2):
                    start = number * high + one * band
                    at = pl.multiple_of((number ^ me) * band, 16)
                    ref[one, pl.ds(at, band), column * size : (column + 1) * size] = value[start : start + band, :]
        else:
            ref[column] = value

    if not first:
        if natural:
            att_ref[:, :, : head_from * size] = before[0][...]
            gq_ref[:, :, : head_from * size] = before[1][...]
        else:
            att_ref[:head_from] = before[0][...]
            gq_ref[:head_from] = before[1][...]
    for head in range(heads):
        offset = 2 if first else 0
        query = tile_of(head_rows, offset + head)
        grad = tile_of(head_rows, offset + heads + head) * live_bf
        scores = dot(query, all_keys, NT)
        prompt_scores = scores[:, :prompt]
        tree_scores = jnp.where(visible, scores[:, prompt:], -1e30)
        top = jnp.maximum(
            jnp.max(prompt_scores, axis=1, keepdims=True), jnp.max(tree_scores, axis=1, keepdims=True)
        )
        scores = jnp.concatenate([prompt_scores, tree_scores], axis=1)
        powers = jnp.exp2((scores - top) * (scale * LOG2E))
        probs = powers * (1.0 / jnp.sum(powers, axis=1, keepdims=True))
        probs_b = probs.astype(jnp.bfloat16)
        attended = (dot(probs_b, all_values, NN) * live).astype(jnp.bfloat16)
        put(att_ref, attended, head_from + head)
        delta = jnp.sum(grad.astype(jnp.float32) * attended.astype(jnp.float32), axis=1, keepdims=True)
        dscore = (probs * (dot(grad, all_values, NT) - delta)).astype(jnp.bfloat16)
        put(gq_ref, (dot(dscore, all_keys, NN) * scale).astype(jnp.bfloat16), head_from + head)
        key_part = dot(query.T, dscore, NN)
        value_part = dot(grad.T, probs_b, NN)
        if head == 0 and first:
            key_acc[...] = key_part
            value_acc[...] = value_part
        elif head == 0:
            key_acc[...] = before[2][...] + key_part
            value_acc[...] = before[3][...] + value_part
        else:
            key_acc[...] += key_part
            value_acc[...] += value_part
    if not last:
        results[0][...] = key_acc[...]
        results[1][...] = value_acc[...]
        return
    gk_ref, gv_ref, keep_ref, send_ref = results
    put(gk_ref, (key_acc[:, prompt:] * scale).T.astype(jnp.bfloat16), 0)
    put(gv_ref, value_acc[:, prompt:].T.astype(jnp.bfloat16), 0)

    @pl.when(core == 0)
    def _():
        for number in range(own_count):
            keep_ref[number] = key_acc[:, number * share : (number + 1) * share] * scale
            send_ref[number] = value_acc[:, number * share : (number + 1) * share]

    @pl.when(core != 0)
    def _():
        for number in range(own_count):
            keep_ref[number] = value_acc[:, number * share : (number + 1) * share]
            send_ref[number] = key_acc[:, number * share : (number + 1) * share] * scale


def swap_cores(value):
    return lax.ppermute(value, "rep", [(0, 1), (1, 0)])


def to_far(value, far):
    return lax.ppermute(value, "seq", [(chip, chip ^ far) for chip in range(lax.axis_size("seq"))])


def spread(parts):
    order = sorted(range(1, len(parts)), key=lambda far: -(far & 2) - (far == 3))
    got = {far: to_far(parts[far], far) for far in order}
    return [parts[0]] + [got[far] for far in range(1, len(parts))]


def per_device(
    queries, response_keys, response_values, grad_out, prompt_keys, prompt_values, packing, lengths, tree_mask
):
    slots, seg_length, size = response_keys.shape
    heads = queries.shape[2] // size
    chips = lax.axis_size("seq")
    band = seg_length // chips
    share = prompt_keys.shape[0]
    prompt = share * chips
    rows = slots * seg_length
    core = lax.axis_index("rep")
    xor = band % 16 == 0 and chips in (2, 4, 8)
    natural = xor
    bf16 = jnp.bfloat16
    split = SPLIT if sum(SPLIT) == heads else (heads,)
    chunks = chunk_tiles(split)
    sources = (response_keys, response_values, queries, grad_out)

    prompt_mine = jnp.where(core == 0, prompt_keys, prompt_values)
    if xor:
        packed = pl.pallas_call(
            functools.partial(pack_kernel, band, chunks),
            out_shape=[
                jax.ShapeDtypeStruct((len(chunk) * slots * band, size), bf16) for chunk in chunks for _ in range(chips)
            ],
            in_specs=[VMEM] * 4,
            out_specs=[VMEM] * (chips * len(chunks)),
            compiler_params=SMALL,
            name="pack",
        )(*sources)
        rows_in = []
        for number, chunk in enumerate(chunks):
            mine = spread(packed[number * chips : (number + 1) * chips])
            theirs = [swap_cores(piece) for piece in mine]
            picked = pl.pallas_call(
                functools.partial(pick_kernel, band, chips),
                out_shape=[jax.ShapeDtypeStruct((len(chunk) * slots * band, size), bf16)] * chips,
                in_specs=[SMEM] + [VMEM] * (2 * chips),
                out_specs=[VMEM] * chips,
                scratch_shapes=[pltpu.VMEM((2 * chips, len(chunk) * slots * band, size), bf16)],
                compiler_params=SMALL,
                name="pick",
            )(packing, *mine, *theirs)
            rows_in.append(spread(picked))
        prompt_own = spread([prompt_mine] * chips)
        prompt_other = [swap_cores(piece) for piece in prompt_own]
    else:
        rows_in = []
        for chunk in chunks:
            tiles = [sources[source][:, :, tile * size : (tile + 1) * size] for source, tile in chunk]
            piece = jnp.stack(tiles, axis=2).reshape(slots, chips, band, len(chunk), size).transpose(1, 0, 3, 2, 4)
            mine = lax.all_to_all(piece, "seq", split_axis=0, concat_axis=0)
            theirs = swap_cores(mine)
            both = jnp.stack([jnp.where(core == 0, mine, theirs), jnp.where(core == 0, theirs, mine)], axis=1)
            both = both.reshape(chips * 2 * slots, len(chunk), band, size)
            wanted = packing.reshape(chips, 2, slots)
            wanted = lax.dynamic_index_in_dim(wanted, core, 1, keepdims=False)
            picked = jnp.take(both, wanted.reshape(-1), axis=0).reshape(chips, slots, len(chunk), band, size)
            moved = lax.all_to_all(picked, "seq", split_axis=0, concat_axis=0)
            rows_in.append([moved.transpose(2, 0, 1, 3, 4).reshape(len(chunk) * rows, size)])
        prompt_own = [lax.all_gather(prompt_mine, "seq", axis=0, tiled=True)]
        prompt_other = [swap_cores(prompt_own[0])]

    carried = []
    own_count, row_count = len(prompt_own), len(rows_in[0])
    head_from = 0
    for number, count in enumerate(split):
        last = number == len(split) - 1
        done = head_from + count
        wide = (slots, seg_length, done * size) if natural else (done, rows, size)
        narrow = (slots, seg_length, size) if natural else (1, rows, size)
        out_shape = [jax.ShapeDtypeStruct(wide, bf16)] * 2
        if last:
            out_shape += [jax.ShapeDtypeStruct(narrow, bf16)] * 2
            out_shape += [jax.ShapeDtypeStruct((own_count, size, prompt // own_count), jnp.float32)] * 2
        else:
            out_shape += [jax.ShapeDtypeStruct((size, prompt + rows), jnp.float32)] * 2
        operands = [*rows_in[0], *(rows_in[number] if number else []), *prompt_own, *prompt_other, *carried]
        work = 2 * 6 * count * rows * (prompt + rows) * size
        carried = pl.pallas_call(
            functools.partial(attend_kernel, band, count, head_from, last, xor, natural, own_count, row_count),
            out_shape=out_shape,
            in_specs=[SMEM, SMEM] + [VMEM] * len(operands),
            out_specs=[VMEM] * len(out_shape),
            scratch_shapes=[
                pltpu.VMEM((prompt + rows, size), bf16),
                pltpu.VMEM((prompt + rows, size), bf16),
                pltpu.VMEM((size, prompt + rows), jnp.float32),
                pltpu.VMEM((size, prompt + rows), jnp.float32),
            ],
            compiler_params=LARGE,
            cost_estimate=pl.CostEstimate(
                flops=2 * work, bytes_accessed=1 << 20, transcendentals=count * rows * (prompt + rows)
            ),
            name="attend",
        )(lengths, tree_mask, *operands)
        head_from = done
    attended, grad_queries, grad_keys, grad_values, keep, send = carried
    if not natural:

        def restore(value):
            value = value.reshape(-1, chips, slots, band, size).transpose(2, 1, 3, 0, 4)
            return value.reshape(slots, seg_length, -1)

        attended, grad_queries, grad_keys, grad_values = (
            restore(value) for value in (attended, grad_queries, grad_keys, grad_values)
        )

    received = swap_cores(send)
    if xor:
        total = [keep[number] + received[number] for number in range(chips)]
        arrived = spread([total[0]] + [part.astype(bf16) for part in total[1:]])
        own = sum(part.astype(jnp.float32) for part in arrived).T
    else:
        total = (keep + received).reshape(size, chips, share).transpose(1, 0, 2).astype(bf16)
        arrived = lax.all_to_all(total, "seq", split_axis=0, concat_axis=0)
        own = jnp.sum(arrived.astype(jnp.float32), axis=0).T
    other = swap_cores(own)
    prompt_grads = jnp.stack([jnp.where(core == 0, own, other), jnp.where(core == 0, other, own)])
    return attended, grad_queries, grad_keys, grad_values, prompt_grads


def solution(mesh):
    segments = P(("groups", "seq", "rep"), None, "head")
    in_specs = (
        segments,
        segments,
        segments,
        segments,
        P(("groups", "seq"), "head"),
        P(("groups", "seq"), "head"),
        P("groups"),
        P(("groups", "seq", "rep")),
        P(("groups", "seq", "rep"), None),
    )
    out_specs = (segments, segments, segments, segments, P(None, ("groups", "seq"), "head"))
    return jax.shard_map(per_device, mesh=mesh, in_specs=in_specs, out_specs=out_specs, check_vma=False)
```

time: 108 us -> 93.2 us (0.86)
  blocking collectives: 56.1 us -> 0 us
  starting transfers between devices: 4.08 us -> 26.3 us
  waiting for transfers between devices: 23.7 us -> 45.1 us
  Pallas kernels: 18.8 us -> 13.3 us
  other arithmetic: 1.48 us -> 3.09 us
  local copies, waits for them, and re-layouts: 2.99 us -> 4.28 us
    all_to_all x2 -> x0, blocking collectives: 56.1 us -> none  [the longest x1 38.6 us: per_device(): banded = lax.all_to_all(message, LINE, split_axis=0, concat_axis=0)]
    ppermute x0 -> x12, waiting for transfers between devices: none -> 40.1 us  [to_far(): lax.ppermute(value, 'seq', [(chip, chip ^ far) for chip in range(lax.axis...]
    ppermute x0 -> x12, starting transfers between devices: none -> 24.8 us  [to_far(): lax.ppermute(value, 'seq', [(chip, chip ^ far) for chip in range(lax.axis...]
    all_to_all x1 -> x0, waiting for transfers between devices: 17.8 us -> none  [per_device(): moved = lax.all_to_all(picked, LINE, split_axis=0, concat_axis=0)]
    pallas_call x3, Pallas kernels: 18.8 us -> 13.3 us  [the longest x1 12.4 us: per_device(): pl.pallas_call(functools.partial(attend_kernel, band, count, head_from, l...]
    all_to_all x1 -> x0, starting transfers between devices: 3.55 us -> none  [per_device(): moved = lax.all_to_all(picked, LINE, split_axis=0, concat_axis=0)]
    unnamed x7 -> x18, local copies, waits for them, and re-layouts: 1.87 us -> 3.64 us
    slice x1 -> x0, local copies, waits for them, and re-layouts: 1.08 us -> none  [per_device(): prompt_own = banded[:, :2 * piece, :]]
  transfers between devices with their start and end apart: 4 -> 22, of which waited for: 4 -> 13; matrix products, arithmetic and copies ran while one was open for 1% -> 0% of each run, Pallas kernels for 0% -> 1%
where the time goes in v2:
time: 93.2 us; the launch traced here: 92.9 us
  waiting for transfers between devices  45.1 us (48%)
  starting transfers between devices  26.3 us (28%)
  Pallas kernels  13.3 us (14%)
  local copies, waits for them, and re-layouts  4.28 us (5%)
  other arithmetic  3.09 us (3%)
    ppermute x12, waiting for transfers between devices, to_far(): lax.ppermute(value, 'seq', [(chip, chip ^ far) for chip in range(lax.axis...  40.1 us
    ppermute x12, starting transfers between devices, to_far(): lax.ppermute(value, 'seq', [(chip, chip ^ far) for chip in range(lax.axis...  24.8 us
    pallas_call x1, Pallas kernels, per_device(): pl.pallas_call(functools.partial(attend_kernel, band, count, head_from, l...  12.4 us
    ppermute x10, waiting for transfers between devices, swap_cores(): return lax.ppermute(value, 'rep', [(0, 1), (1, 0)])  5 us
    unnamed x18, local copies, waits for them, and re-layouts  3.64 us
  transfers between devices with their start and end apart: 22, of which 13 were waited for; matrix products, arithmetic and copies ran while one was open for 0% of the time, Pallas kernels for 1%

profile of v2, /device:TPU:0, one launch (start us, length us, event | category | flops | bytes accessed | tf_op | source)
XLA Modules:
  0.0 92.9 jit_solution(10088154134081400843)
XLA Ops:
  0.6 0.0 copy-start
  0.6 1.0 %copy-done = bf16[2,128,640]{2,1,0:T(8,128)(2,1)S(1)} copy-done((bf16[2,128,640]{2,1,0:T(8,128)(2,1)S(1)}, bf16[2,128,640]{2,1,0:T(8,128)(2,1)}, u32[]{:S(2)}) %copy-start) | copy-done | bytes 327704
  1.6 0.0 copy-start.1
  1.6 1.0 %copy-done.1 = bf16[2,128,640]{2,1,0:T(8,128)(2,1)S(1)} copy-done((bf16[2,128,640]{2,1,0:T(8,128)(2,1)S(1)}, bf16[2,128,640]{2,1,0:T(8,128)(2,1)}, u32[]{:S(2)}) %copy-start.1) | copy-done | bytes 327704
  2.6 0.8 copy-done.2
  3.4 0.8 copy-done.3
  4.3 0.1 pack.1
  4.4 3.1 %collective-permute-start = (bf16[768,128]{1,0:T(8,128)(2,1)S(1)}, bf16[768,128]{1,0:T(8,128)(2,1)S(1)}, u32[]{:S(2)}, u32[]{:S(2)}) collective-permute-start(bf16[768,128]{1,0:T(8,128)(2,1)S(1)} %get-tuple-element.20), channel_id=1, source_target_pairs={{0,4},{4,0},{8,12},{12,8},{1,5},{5,1},{9,13},{13,9},{2,6},{6,2},{1... | collective-permute-start | bytes 589832 | tf_op jit(solution)/shard_map/ppermute | solution.py:213
  7.5 2.6 %collective-permute-start.1 = (bf16[768,128]{1,0:T(8,128)(2,1)S(1)}, bf16[768,128]{1,0:T(8,128)(2,1)S(1)}, u32[]{:S(2)}, u32[]{:S(2)}) collective-permute-start(bf16[768,128]{1,0:T(8,128)(2,1)S(1)} %get-tuple-element.21), channel_id=1, source_target_pairs={{0,8},{4,12},{8,0},{12,4},{1,9},{5,13},{9,1},{13,5},{2,10},{6,14},... | collective-permute-start | bytes 589832 | tf_op jit(solution)/shard_map/ppermute | solution.py:213
  10.1 0.0 collective-permute-start.2
  10.1 0.0 collective-permute-start.3
  10.1 0.0 copy-done.7
  10.1 0.0 copy-done.8
  10.1 0.0 copy-start.4
  10.1 3.9 %collective-permute-start.12 = (bf16[512,128]{1,0:T(8,128)(2,1)S(1)}, bf16[512,128]{1,0:T(8,128)(2,1)S(1)}, u32[]{:S(2)}, u32[]{:S(2)}) collective-permute-start(bf16[512,128]{1,0:T(8,128)(2,1)S(1)} %broadcast_select_fusion.refs_4_), channel_id=1, source_target_pairs={{0,12},{4,8},{8,4},{12,0},{1,13},{5,9},{9,5},{13,1},{2,14},{6,10},... | collective-permute-start | bytes 393224 | tf_op jit(solution)/shard_map/ppermute | solution.py:213
  14.0 1.8 %collective-permute-done.refs_1_ = bf16[768,128]{1,0:T(8,128)(2,1)S(1)} collective-permute-done((bf16[768,128]{1,0:T(8,128)(2,1)S(1)}, bf16[768,128]{1,0:T(8,128)(2,1)S(1)}, u32[]{:S(2)}, u32[]{:S(2)}) %collective-permute-start) | collective-permute-done | bytes 196640 | tf_op jit(solution)/shard_map/ppermute | solution.py:213
  15.8 0.0 collective-permute-start.4
  15.8 11.6 %collective-permute-done.1.refs_2_ = bf16[768,128]{1,0:T(8,128)(2,1)S(1)} collective-permute-done((bf16[768,128]{1,0:T(8,128)(2,1)S(1)}, bf16[768,128]{1,0:T(8,128)(2,1)S(1)}, u32[]{:S(2)}, u32[]{:S(2)}) %collective-permute-start.1) | collective-permute-done | bytes 196640 | tf_op jit(solution)/shard_map/ppermute | solution.py:213
  27.4 0.0 collective-permute-start.5
  27.4 0.0 collective-permute-done.2.refs_3_
  27.4 0.5 collective-permute-start.6
  28.0 0.0 collective-permute-done.12.refs_7_
  28.0 0.1 collective-permute-start.13
  28.0 0.0 collective-permute-done.3.refs_4_
  28.0 6.6 %collective-permute-start.11 = (bf16[512,128]{1,0:T(8,128)(2,1)S(1)}, bf16[512,128]{1,0:T(8,128)(2,1)S(1)}, u32[]{:S(2)}, u32[]{:S(2)}) collective-permute-start(bf16[512,128]{1,0:T(8,128)(2,1)S(1)} %broadcast_select_fusion.refs_4_), channel_id=1, source_target_pairs={{0,8},{4,12},{8,0},{12,4},{1,9},{5,13},{9,1},{13,5},{2,10},{6,14},... | collective-permute-start | bytes 393224 | tf_op jit(solution)/shard_map/ppermute | solution.py:213
  34.6 0.0 collective-permute-done.4.refs_5_
  34.6 0.0 collective-permute-start.10
  34.6 0.0 collective-permute-done.5.refs_6_
  34.6 0.3 collective-permute-start.16
  34.9 0.0 collective-permute-done.6.refs_7_
  34.9 0.0 copy-done.4
  34.9 0.8 pick.1
  35.8 1.8 %collective-permute-start.7 = (bf16[768,128]{1,0:T(8,128)(2,1)S(1)}, bf16[768,128]{1,0:T(8,128)(2,1)S(1)}, u32[]{:S(2)}, u32[]{:S(2)}) collective-permute-start(bf16[768,128]{1,0:T(8,128)(2,1)S(1)} %get-tuple-element.24), channel_id=1, source_target_pairs={{0,4},{4,0},{8,12},{12,8},{1,5},{5,1},{9,13},{13,9},{2,6},{6,2},{1... | collective-permute-start | bytes 589832 | tf_op jit(solution)/shard_map/ppermute | solution.py:213
  37.6 0.0 collective-permute-done.13.refs_8_
  37.6 0.3 collective-permute-start.8
  37.9 4.0 %collective-permute-done.11.refs_6_ = bf16[512,128]{1,0:T(8,128)(2,1)S(1)} collective-permute-done((bf16[512,128]{1,0:T(8,128)(2,1)S(1)}, bf16[512,128]{1,0:T(8,128)(2,1)S(1)}, u32[]{:S(2)}, u32[]{:S(2)}) %collective-permute-start.11) | collective-permute-done | bytes 131104 | tf_op jit(solution)/shard_map/ppermute | solution.py:213
  41.9 1.4 %collective-permute-start.9 = (bf16[768,128]{1,0:T(8,128)(2,1)S(1)}, bf16[768,128]{1,0:T(8,128)(2,1)S(1)}, u32[]{:S(2)}, u32[]{:S(2)}) collective-permute-start(bf16[768,128]{1,0:T(8,128)(2,1)S(1)} %get-tuple-element.26), channel_id=1, source_target_pairs={{0,12},{4,8},{8,4},{12,0},{1,13},{5,9},{9,5},{13,1},{2,14},{6,10},... | collective-permute-start | bytes 589832 | tf_op jit(solution)/shard_map/ppermute | solution.py:213
  43.2 3.6 %collective-permute-done.10.refs_5_ = bf16[512,128]{1,0:T(8,128)(2,1)S(1)} collective-permute-done((bf16[512,128]{1,0:T(8,128)(2,1)S(1)}, bf16[512,128]{1,0:T(8,128)(2,1)S(1)}, u32[]{:S(2)}, u32[]{:S(2)}) %collective-permute-start.10) | collective-permute-done | bytes 131104 | tf_op jit(solution)/shard_map/ppermute | solution.py:213
  46.8 0.0 collective-permute-start.15
  46.8 0.0 collective-permute-done.16.refs_11_
  46.8 0.5 collective-permute-start.14
  47.3 0.8 collective-permute-done.15.refs_10_
  48.2 0.2 collective-permute-done.14.refs_9_
  48.3 2.0 %collective-permute-done.7.refs_1_ = bf16[768,128]{1,0:T(8,128)(2,1)S(1)} collective-permute-done((bf16[768,128]{1,0:T(8,128)(2,1)S(1)}, bf16[768,128]{1,0:T(8,128)(2,1)S(1)}, u32[]{:S(2)}, u32[]{:S(2)}) %collective-permute-start.7) | collective-permute-done | bytes 196640 | tf_op jit(solution)/shard_map/ppermute | solution.py:213
  50.3 0.0 collective-permute-done.8.refs_2_
  50.3 5.1 %collective-permute-done.9.refs_3_ = bf16[768,128]{1,0:T(8,128)(2,1)S(1)} collective-permute-done((bf16[768,128]{1,0:T(8,128)(2,1)S(1)}, bf16[768,128]{1,0:T(8,128)(2,1)S(1)}, u32[]{:S(2)}, u32[]{:S(2)}) %collective-permute-start.9) | collective-permute-done | bytes 196640 | tf_op jit(solution)/shard_map/ppermute | solution.py:213
  55.5 0.0 copy-done.5
  55.5 0.0 copy-done.6
  55.5 12.4 %attend.1 = (bf16[2,128,640]{2,1,0:T(8,128)(2,1)}, bf16[2,128,640]{2,1,0:T(8,128)(2,1)}, bf16[2,128,128]{2,1,0:T(8,128)(2,1)}, bf16[2,128,128]{2,1,0:T(8,128)(2,...) custom-call(s32[2]{0:T(128)S(1)} %copy-done.6, s32[2,2]{1,0:T(2,128)S(1)} %copy-done.5, ...), custom_call_target="tpu_custom_call" | custom-call | flops 9059696640 | bytes 1048576 | tf_op jit(solution)/shard_map/attend/pallas_call | solution.py:301
  67.9 0.3 copy.15
  68.2 0.1 collective-permute-start.17
  68.3 0.3 copy.14
  68.6 2.4 %collective-permute-done.17 = f32[4,128,512]{1,2,0:T(8,128)} collective-permute-done((f32[4,128,512]{1,2,0:T(8,128)S(1)}, f32[4,128,512]{1,2,0:T(8,128)}, u32[]{:S(2)}, u32[]{:S(2)}) %collective-permute-start.17) | collective-permute-done | bytes 1048608 | tf_op jit(solution)/shard_map/ppermute | solution.py:209
  71.0 1.2 %fusion.8 = (bf16[128,512]{0,1:T(8,128)(2,1)S(1)}, bf16[128,512]{0,1:T(8,128)(2,1)S(1)}, bf16[128,512]{0,1:T(8,128)(2,1)S(1)}) fusion(f32[4,128,512]{1,2,0:T(8,128)} %collective-permute-done.17, f32[4,128,512]{1,2,0:T(8,128)S(1)} %copy.14), kind=kLoop, calls=%fused_computation.15 | loop fusion | flops 393216 | bytes 1966080 | tf_op jit(solution)/shard_map/convert_element_type | solution.py:333
  72.2 3.7 %collective-permute-start.18 = (bf16[128,512]{0,1:T(8,128)(2,1)S(1)}, bf16[128,512]{0,1:T(8,128)(2,1)S(1)}, u32[]{:S(2)}, u32[]{:S(2)}) collective-permute-start(bf16[128,512]{0,1:T(8,128)(2,1)S(1)} %get-tuple-element.33), channel_id=1, source_target_pairs={{0,4},{4,0},{8,12},{12,8},{1,5},{5,1},{9,13},{13,9},{2,6},{6,2},{1... | collective-permute-start | bytes 393224 | tf_op jit(solution)/shard_map/ppermute | solution.py:213
  75.9 1.4 %collective-permute-start.20 = (bf16[128,512]{0,1:T(8,128)(2,1)S(1)}, bf16[128,512]{0,1:T(8,128)(2,1)S(1)}, u32[]{:S(2)}, u32[]{:S(2)}) collective-permute-start(bf16[128,512]{0,1:T(8,128)(2,1)S(1)} %get-tuple-element.34), channel_id=1, source_target_pairs={{0,12},{4,8},{8,4},{12,0},{1,13},{5,9},{9,5},{13,1},{2,14},{6,10},... | collective-permute-start | bytes 393224 | tf_op jit(solution)/shard_map/ppermute | solution.py:213
  77.3 0.2 collective-permute-start.19
  77.4 2.3 %collective-permute-done.18 = bf16[128,512]{0,1:T(8,128)(2,1)S(1)} collective-permute-done((bf16[128,512]{0,1:T(8,128)(2,1)S(1)}, bf16[128,512]{0,1:T(8,128)(2,1)S(1)}, u32[]{:S(2)}, u32[]{:S(2)}) %collective-permute-start.18) | collective-permute-done | bytes 131104 | tf_op jit(solution)/shard_map/ppermute | solution.py:213
  79.8 4.5 %collective-permute-done.20 = bf16[128,512]{0,1:T(8,128)(2,1)S(1)} collective-permute-done((bf16[128,512]{0,1:T(8,128)(2,1)S(1)}, bf16[128,512]{0,1:T(8,128)(2,1)S(1)}, u32[]{:S(2)}, u32[]{:S(2)}) %collective-permute-start.20) | collective-permute-done | bytes 131104 | tf_op jit(solution)/shard_map/ppermute | solution.py:213
  84.3 5.1 %collective-permute-done.19 = bf16[128,512]{0,1:T(8,128)(2,1)S(1)} collective-permute-done((bf16[128,512]{0,1:T(8,128)(2,1)S(1)}, bf16[128,512]{0,1:T(8,128)(2,1)S(1)}, u32[]{:S(2)}, u32[]{:S(2)}) %collective-permute-start.19) | collective-permute-done | bytes 131104 | tf_op jit(solution)/shard_map/ppermute | solution.py:213
  89.4 1.0 %fusion.7 = f32[512,128]{1,0:T(8,128)S(1)} fusion(f32[4,128,512]{1,2,0:T(8,128)} %collective-permute-done.17, f32[4,128,512]{1,2,0:T(8,128)S(1)} %copy.14, bf16[128,512]{0,1:T(8,128)(2,1)S(1)} %collective-permute-done.20, bf16[128,512]{0,1:T(8,128)(2,1)S(1)} %collective-permute-done.19, bf16[128,512]{0,1:T(8,128)(2,1)S(1)} %collective-permute-done.18), kind=kLoop, calls=%fused_computation.12 | loop fusion | flops 458752 | bytes 1179648 | tf_op jit(solution)/shard_map/transpose | solution.py:334
  90.4 0.1 collective-permute-start.21
  90.5 1.5 %collective-permute-done.21 = f32[512,128]{1,0:T(8,128)S(1)} collective-permute-done((f32[512,128]{1,0:T(8,128)S(1)}, f32[512,128]{1,0:T(8,128)S(1)}, u32[]{:S(2)}, u32[]{:S(2)}) %collective-permute-start.21) | collective-permute-done | bytes 262176 | tf_op jit(solution)/shard_map/ppermute | solution.py:209
  92.1 0.8 pad_maximum_fusion
  (8 shorter events, 0.1 us)
Async XLA Ops:
  0.6 1.0 %copy-start = (bf16[2,128,640]{2,1,0:T(8,128)(2,1)S(1)}, bf16[2,128,640]{2,1,0:T(8,128)(2,1)}, u32[]{:S(2)}) copy-start(bf16[2,128,640]{2,1,0:T(8,128)(2,1)} %q_ref.1) | copy-start | bytes 983044
  1.6 1.0 %copy-start.1 = (bf16[2,128,640]{2,1,0:T(8,128)(2,1)S(1)}, bf16[2,128,640]{2,1,0:T(8,128)(2,1)}, u32[]{:S(2)}) copy-start(bf16[2,128,640]{2,1,0:T(8,128)(2,1)} %g_ref.1) | copy-start | bytes 983044
  2.6 0.8 copy-start.2
  3.4 0.8 copy-start.3
  4.3 5.8 %copy-start.7 = (bf16[512,128]{1,0:T(8,128)(2,1)S(1)}, bf16[512,128]{1,0:T(8,128)(2,1)}, u32[]{:S(2)}) copy-start(bf16[512,128]{1,0:T(8,128)(2,1)} %param.13) | copy-start | bytes 393220
  4.3 5.8 %copy-start.8 = (bf16[512,128]{1,0:T(8,128)(2,1)S(1)}, bf16[512,128]{1,0:T(8,128)(2,1)}, u32[]{:S(2)}) copy-start(bf16[512,128]{1,0:T(8,128)(2,1)} %param.14) | copy-start | bytes 393220
  4.4 11.4 %collective-permute-start = (bf16[768,128]{1,0:T(8,128)(2,1)S(1)}, bf16[768,128]{1,0:T(8,128)(2,1)S(1)}, u32[]{:S(2)}, u32[]{:S(2)}) collective-permute-start(bf16[768,128]{1,0:T(8,128)(2,1)S(1)} %get-tuple-element.20), channel_id=1, source_target_pairs={{0,4},{4,0},{8,12},{12,8},{1,5},{5,1},{9,13},{13,9},{2,6},{6,2},{1... | collective-permute-start | bytes 589832 | tf_op jit(solution)/shard_map/ppermute | solution.py:213
  7.5 20.0 %collective-permute-start.1 = (bf16[768,128]{1,0:T(8,128)(2,1)S(1)}, bf16[768,128]{1,0:T(8,128)(2,1)S(1)}, u32[]{:S(2)}, u32[]{:S(2)}) collective-permute-start(bf16[768,128]{1,0:T(8,128)(2,1)S(1)} %get-tuple-element.21), channel_id=1, source_target_pairs={{0,8},{4,12},{8,0},{12,4},{1,9},{5,13},{9,1},{13,5},{2,10},{6,14},... | collective-permute-start | bytes 589832 | tf_op jit(solution)/shard_map/ppermute | solution.py:213
  10.1 17.4 %collective-permute-start.2 = (bf16[768,128]{1,0:T(8,128)(2,1)S(1)}, bf16[768,128]{1,0:T(8,128)(2,1)S(1)}, u32[]{:S(2)}, u32[]{:S(2)}) collective-permute-start(bf16[768,128]{1,0:T(8,128)(2,1)S(1)} %get-tuple-element.22), channel_id=1, source_target_pairs={{0,12},{4,8},{8,4},{12,0},{1,13},{5,9},{9,5},{13,1},{2,14},{6,10},... | collective-permute-start | bytes 589832 | tf_op jit(solution)/shard_map/ppermute | solution.py:213
  10.1 18.0 %collective-permute-start.3 = (bf16[768,128]{1,0:T(8,128)(2,1)S(1)}, bf16[768,128]{1,0:T(8,128)(2,1)S(1)}, u32[]{:S(2)}, u32[]{:S(2)}) collective-permute-start(bf16[768,128]{1,0:T(8,128)(2,1)S(1)} %get-tuple-element.19.refs_0_), channel_id=1, source_target_pairs={{0,1},{1,0},{2,3},{3,2},{4,5},{5,4},{6,7},{7,6},{8,9},{9,8},{10,11... | collective-permute-start | bytes 589832 | tf_op jit(solution)/shard_map/ppermute | solution.py:209
  10.1 24.8 %copy-start.4 = (s32[16]{0:T(128)S(1)}, s32[16]{0:T(128)}, u32[]{:S(2)}) copy-start(s32[16]{0:T(128)} %packing_ref.1) | copy-start | bytes 196
  10.1 17.8 %collective-permute-start.12 = (bf16[512,128]{1,0:T(8,128)(2,1)S(1)}, bf16[512,128]{1,0:T(8,128)(2,1)S(1)}, u32[]{:S(2)}, u32[]{:S(2)}) collective-permute-start(bf16[512,128]{1,0:T(8,128)(2,1)S(1)} %broadcast_select_fusion.refs_4_), channel_id=1, source_target_pairs={{0,12},{4,8},{8,4},{12,0},{1,13},{5,9},{9,5},{13,1},{2,14},{6,10},... | collective-permute-start | bytes 393224 | tf_op jit(solution)/shard_map/ppermute | solution.py:213
  15.8 18.8 %collective-permute-start.4 = (bf16[768,128]{1,0:T(8,128)(2,1)S(1)}, bf16[768,128]{1,0:T(8,128)(2,1)S(1)}, u32[]{:S(2)}, u32[]{:S(2)}) collective-permute-start(bf16[768,128]{1,0:T(8,128)(2,1)S(1)} %collective-permute-done.refs_1_), channel_id=1, source_target_pairs={{0,1},{1,0},{2,3},{3,2},{4,5},{5,4},{6,7},{7,6},{8,9},{9,8},{10,11... | collective-permute-start | bytes 589832 | tf_op jit(solution)/shard_map/ppermute | solution.py:209
  27.4 7.2 %collective-permute-start.5 = (bf16[768,128]{1,0:T(8,128)(2,1)S(1)}, bf16[768,128]{1,0:T(8,128)(2,1)S(1)}, u32[]{:S(2)}, u32[]{:S(2)}) collective-permute-start(bf16[768,128]{1,0:T(8,128)(2,1)S(1)} %collective-permute-done.1.refs_2_), channel_id=1, source_target_pairs={{0,1},{1,0},{2,3},{3,2},{4,5},{5,4},{6,7},{7,6},{8,9},{9,8},{10,11... | collective-permute-start | bytes 589832 | tf_op jit(solution)/shard_map/ppermute | solution.py:209
  27.4 7.5 %collective-permute-start.6 = (bf16[768,128]{1,0:T(8,128)(2,1)S(1)}, bf16[768,128]{1,0:T(8,128)(2,1)S(1)}, u32[]{:S(2)}, u32[]{:S(2)}) collective-permute-start(bf16[768,128]{1,0:T(8,128)(2,1)S(1)} %collective-permute-done.2.refs_3_), channel_id=1, source_target_pairs={{0,1},{1,0},{2,3},{3,2},{4,5},{5,4},{6,7},{7,6},{8,9},{9,8},{10,11... | collective-permute-start | bytes 589832 | tf_op jit(solution)/shard_map/ppermute | solution.py:209
  28.0 9.6 %collective-permute-start.13 = (bf16[512,128]{1,0:T(8,128)(2,1)S(1)}, bf16[512,128]{1,0:T(8,128)(2,1)S(1)}, u32[]{:S(2)}, u32[]{:S(2)}) collective-permute-start(bf16[512,128]{1,0:T(8,128)(2,1)S(1)} %broadcast_select_fusion.refs_4_), channel_id=1, source_target_pairs={{0,1},{1,0},{2,3},{3,2},{4,5},{5,4},{6,7},{7,6},{8,9},{9,8},{10,11... | collective-permute-start | bytes 393224 | tf_op jit(solution)/shard_map/ppermute | solution.py:209
  28.0 13.8 %collective-permute-start.11 = (bf16[512,128]{1,0:T(8,128)(2,1)S(1)}, bf16[512,128]{1,0:T(8,128)(2,1)S(1)}, u32[]{:S(2)}, u32[]{:S(2)}) collective-permute-start(bf16[512,128]{1,0:T(8,128)(2,1)S(1)} %broadcast_select_fusion.refs_4_), channel_id=1, source_target_pairs={{0,8},{4,12},{8,0},{12,4},{1,9},{5,13},{9,1},{13,5},{2,10},{6,14},... | collective-permute-start | bytes 393224 | tf_op jit(solution)/shard_map/ppermute | solution.py:213
  34.6 12.2 %collective-permute-start.10 = (bf16[512,128]{1,0:T(8,128)(2,1)S(1)}, bf16[512,128]{1,0:T(8,128)(2,1)S(1)}, u32[]{:S(2)}, u32[]{:S(2)}) collective-permute-start(bf16[512,128]{1,0:T(8,128)(2,1)S(1)} %broadcast_select_fusion.refs_4_), channel_id=1, source_target_pairs={{0,4},{4,0},{8,12},{12,8},{1,5},{5,1},{9,13},{13,9},{2,6},{6,2},{1... | collective-permute-start | bytes 393224 | tf_op jit(solution)/shard_map/ppermute | solution.py:213
  34.6 12.2 %collective-permute-start.16 = (bf16[512,128]{1,0:T(8,128)(2,1)S(1)}, bf16[512,128]{1,0:T(8,128)(2,1)S(1)}, u32[]{:S(2)}, u32[]{:S(2)}) collective-permute-start(bf16[512,128]{1,0:T(8,128)(2,1)S(1)} %collective-permute-done.12.refs_7_), channel_id=1, source_target_pairs={{0,1},{1,0},{2,3},{3,2},{4,5},{5,4},{6,7},{7,6},{8,9},{9,8},{10,11... | collective-permute-start | bytes 393224 | tf_op jit(solution)/shard_map/ppermute | solution.py:209
  35.8 14.6 %collective-permute-start.7 = (bf16[768,128]{1,0:T(8,128)(2,1)S(1)}, bf16[768,128]{1,0:T(8,128)(2,1)S(1)}, u32[]{:S(2)}, u32[]{:S(2)}) collective-permute-start(bf16[768,128]{1,0:T(8,128)(2,1)S(1)} %get-tuple-element.24), channel_id=1, source_target_pairs={{0,4},{4,0},{8,12},{12,8},{1,5},{5,1},{9,13},{13,9},{2,6},{6,2},{1... | collective-permute-start | bytes 589832 | tf_op jit(solution)/shard_map/ppermute | solution.py:213
  37.6 12.7 %collective-permute-start.8 = (bf16[768,128]{1,0:T(8,128)(2,1)S(1)}, bf16[768,128]{1,0:T(8,128)(2,1)S(1)}, u32[]{:S(2)}, u32[]{:S(2)}) collective-permute-start(bf16[768,128]{1,0:T(8,128)(2,1)S(1)} %get-tuple-element.25), channel_id=1, source_target_pairs={{0,8},{4,12},{8,0},{12,4},{1,9},{5,13},{9,1},{13,5},{2,10},{6,14},... | collective-permute-start | bytes 589832 | tf_op jit(solution)/shard_map/ppermute | solution.py:213
  41.9 13.6 %copy-start.5 = (s32[2,2]{1,0:T(2,128)S(1)}, s32[2,2]{1,0:T(2,128)}, u32[]{:S(2)}) copy-start(s32[2,2]{1,0:T(2,128)} %tree_ref.1) | copy-start | bytes 52
  41.9 13.6 %copy-start.6 = (s32[2]{0:T(128)S(1)}, s32[2]{0:T(128)}, u32[]{:S(2)}) copy-start(s32[2]{0:T(128)} %length_ref.1) | copy-start | bytes 28
  41.9 13.6 %collective-permute-start.9 = (bf16[768,128]{1,0:T(8,128)(2,1)S(1)}, bf16[768,128]{1,0:T(8,128)(2,1)S(1)}, u32[]{:S(2)}, u32[]{:S(2)}) collective-permute-start(bf16[768,128]{1,0:T(8,128)(2,1)S(1)} %get-tuple-element.26), channel_id=1, source_target_pairs={{0,12},{4,8},{8,4},{12,0},{1,13},{5,9},{9,5},{13,1},{2,14},{6,10},... | collective-permute-start | bytes 589832 | tf_op jit(solution)/shard_map/ppermute | solution.py:213
  46.8 1.3 %collective-permute-start.15 = (bf16[512,128]{1,0:T(8,128)(2,1)S(1)}, bf16[512,128]{1,0:T(8,128)(2,1)S(1)}, u32[]{:S(2)}, u32[]{:S(2)}) collective-permute-start(bf16[512,128]{1,0:T(8,128)(2,1)S(1)} %collective-permute-done.11.refs_6_), channel_id=1, source_target_pairs={{0,1},{1,0},{2,3},{3,2},{4,5},{5,4},{6,7},{7,6},{8,9},{9,8},{10,11... | collective-permute-start | bytes 393224 | tf_op jit(solution)/shard_map/ppermute | solution.py:209
  46.8 1.5 %collective-permute-start.14 = (bf16[512,128]{1,0:T(8,128)(2,1)S(1)}, bf16[512,128]{1,0:T(8,128)(2,1)S(1)}, u32[]{:S(2)}, u32[]{:S(2)}) collective-permute-start(bf16[512,128]{1,0:T(8,128)(2,1)S(1)} %collective-permute-done.10.refs_5_), channel_id=1, source_target_pairs={{0,1},{1,0},{2,3},{3,2},{4,5},{5,4},{6,7},{7,6},{8,9},{9,8},{10,11... | collective-permute-start | bytes 393224 | tf_op jit(solution)/shard_map/ppermute | solution.py:209
  68.2 2.9 %collective-permute-start.17 = (f32[4,128,512]{1,2,0:T(8,128)S(1)}, f32[4,128,512]{1,2,0:T(8,128)}, u32[]{:S(2)}, u32[]{:S(2)}) collective-permute-start(f32[4,128,512]{1,2,0:T(8,128)S(1)} %copy.15), channel_id=1, source_target_pairs={{0,1},{1,0},{2,3},{3,2},{4,5},{5,4},{6,7},{7,6},{8,9},{9,8},{10,11... | collective-permute-start | bytes 3145736 | tf_op jit(solution)/shard_map/ppermute | solution.py:209
  72.2 7.5 %collective-permute-start.18 = (bf16[128,512]{0,1:T(8,128)(2,1)S(1)}, bf16[128,512]{0,1:T(8,128)(2,1)S(1)}, u32[]{:S(2)}, u32[]{:S(2)}) collective-permute-start(bf16[128,512]{0,1:T(8,128)(2,1)S(1)} %get-tuple-element.33), channel_id=1, source_target_pairs={{0,4},{4,0},{8,12},{12,8},{1,5},{5,1},{9,13},{13,9},{2,6},{6,2},{1... | collective-permute-start | bytes 393224 | tf_op jit(solution)/shard_map/ppermute | solution.py:213
  75.9 8.4 %collective-permute-start.20 = (bf16[128,512]{0,1:T(8,128)(2,1)S(1)}, bf16[128,512]{0,1:T(8,128)(2,1)S(1)}, u32[]{:S(2)}, u32[]{:S(2)}) collective-permute-start(bf16[128,512]{0,1:T(8,128)(2,1)S(1)} %get-tuple-element.34), channel_id=1, source_target_pairs={{0,12},{4,8},{8,4},{12,0},{1,13},{5,9},{9,5},{13,1},{2,14},{6,10},... | collective-permute-start | bytes 393224 | tf_op jit(solution)/shard_map/ppermute | solution.py:213
  77.3 12.1 %collective-permute-start.19 = (bf16[128,512]{0,1:T(8,128)(2,1)S(1)}, bf16[128,512]{0,1:T(8,128)(2,1)S(1)}, u32[]{:S(2)}, u32[]{:S(2)}) collective-permute-start(bf16[128,512]{0,1:T(8,128)(2,1)S(1)} %get-tuple-element.35), channel_id=1, source_target_pairs={{0,8},{4,12},{8,0},{12,4},{1,9},{5,13},{9,1},{13,5},{2,10},{6,14},... | collective-permute-start | bytes 393224 | tf_op jit(solution)/shard_map/ppermute | solution.py:213
  90.4 1.6 %collective-permute-start.21 = (f32[512,128]{1,0:T(8,128)S(1)}, f32[512,128]{1,0:T(8,128)S(1)}, u32[]{:S(2)}, u32[]{:S(2)}) collective-permute-start(f32[512,128]{1,0:T(8,128)S(1)} %fusion.7), channel_id=1, source_target_pairs={{0,1},{1,0},{2,3},{3,2},{4,5},{5,4},{6,7},{7,6},{8,9},{9,8},{10,11... | collective-permute-start | bytes 786440 | tf_op jit(solution)/shard_map/ppermute | solution.py:209

commit v3 on v2

v3 whole, which is shorter than its diff:
```python
import functools

import jax
import jax.numpy as jnp
from jax import lax
from jax.experimental import pallas as pl
from jax.experimental.pallas import tpu as pltpu
from jax.sharding import PartitionSpec as P

NT = (((1,), (1,)), ((), ()))
NN = (((1,), (0,)), ((), ()))
LOG2E = 1.4426950408889634
GROUPS = (5,)
VMEM = pl.BlockSpec(memory_space=pltpu.VMEM)
HBM = pl.BlockSpec(memory_space=pltpu.HBM)
SMEM = pl.BlockSpec(memory_space=pltpu.SMEM)
SMALL = pltpu.CompilerParams(vmem_limit_bytes=8 * 1024 * 1024)
FULL = pltpu.CompilerParams(vmem_limit_bytes=56 * 1024 * 1024)
LARGE = pltpu.CompilerParams(vmem_limit_bytes=36 * 1024 * 1024)


def dot(left, right, dims):
    return lax.dot_general(left, right, dims, preferred_element_type=jnp.float32)


def pack_kernel(band, tiles, k_hbm, v_hbm, q_hbm, g_hbm, pk_hbm, pv_hbm, *refs):
    chips = len(refs) - 5
    outs, held, sems = refs[:chips], refs[chips:-1], refs[-1]
    me = lax.axis_index("seq")
    core = lax.axis_index("rep")
    share, size = pk_hbm.shape
    rows = len(tiles) * 2 * band
    targets = [out.at[pl.ds(rows, share), :] for out in outs[:3]]
    copies = [
        pltpu.make_async_copy(source, target, sems.at[number])
        for number, (source, target) in enumerate(zip((k_hbm, v_hbm, q_hbm, g_hbm), held))
    ]
    for copy in copies:
        copy.start()

    def prompt_copies(source):
        return [pltpu.make_async_copy(source, target, sems.at[4 + far]) for far, target in enumerate(targets)]

    @pl.when(core == 0)
    def _():
        for copy in prompt_copies(pk_hbm):
            copy.start()

    @pl.when(core != 0)
    def _():
        for copy in prompt_copies(pv_hbm):
            copy.start()

    for copy in copies:
        copy.wait()
    for far, out in enumerate(outs):
        start = pl.multiple_of((me ^ far) * band, 16)
        row = 0
        for source, tile in tiles:
            for slot in range(2):
                out[row : row + band, :] = held[source][slot, pl.ds(start, band), tile * size : (tile + 1) * size]
                row += band
    for copy in prompt_copies(pk_hbm):
        copy.wait()


def pick_kernel(band, chips, counts, wanted_ref, *refs):
    pieces, outs, held = refs[: 2 * chips], refs[2 * chips : -1], refs[-1]
    me = lax.axis_index("seq")
    core = lax.axis_index("rep")
    for number, piece in enumerate(pieces):
        held[number] = piece[: held.shape[1], :]
    start = 2 * 2 * band
    for piece in (pieces[2], pieces[chips + 2]):
        passed = piece[held.shape[1] :, :]
        outs[1][start : start + passed.shape[0], :] = passed
        start += passed.shape[0]
    for far in range(chips):
        for slot in range(2):
            chosen = wanted_ref[me ^ far, slot]
            device = chosen // 2
            number = ((device // 2) ^ me) + chips * ((device % 2) ^ core)
            tile = 0
            for chunk, count in enumerate(counts):
                out = outs[chunk * chips + far]
                for one in range(count):
                    start = pl.multiple_of(tile * 2 * band + (chosen % 2) * band, 16)
                    row = one * 2 * band + slot * band
                    out[row : row + band, :] = held[number, pl.ds(start, band), :]
                    tile += 1


def combine_kernel(keep_ref, received_ref, *outs):
    for number, out in enumerate(outs):
        out[...] = (keep_ref[number] + received_ref[number].astype(jnp.float32)).astype(out.dtype)


def finish_kernel(*refs):
    mine, theirs, out_ref = refs[: len(refs) // 2], refs[len(refs) // 2 : -1], refs[-1]
    core = lax.axis_index("rep")
    for parts, place in ((mine, core), (theirs, 1 - core)):
        total = parts[0][...]
        for part in parts[1:]:
            total = total + part[...].astype(jnp.float32)
        out_ref[place] = total.T


def attend_kernel(band, heads, total_rows, bands, first, last, xor, row_count, length_ref, tree_ref, *refs):
    refs = list(refs)

    def take(count):
        taken = refs[:count]
        del refs[:count]
        return taken

    head_rows = take(len(bands))
    if first:
        pair_rows = take(row_count)
        own_parts, other_parts = take(3 if xor else 1), take(3 if xor else 1)
    else:
        keys, values, att_before, gq_before, key_before, value_before = take(6)
    att_ref, gq_ref = take(2)
    if first:
        keys, values = (refs.pop(-2), refs.pop(-1)) if last else take(2)
    core = lax.axis_index("rep")
    me = lax.axis_index("seq") if xor else 0
    size = keys.shape[1]
    prompt = keys.shape[0] - total_rows
    share = prompt // row_count
    high = total_rows // row_count
    rows = high * len(bands)
    scale = size ** (-0.5)

    def fill(keys_of, values_of):
        for target, pieces in ((keys, keys_of), (values, values_of)):
            for number, (piece, start) in enumerate(pieces):
                target[number * share : (number + 1) * share, :] = piece[start : start + share, :]

    if first:
        own_parts, other_parts = (
            [(piece, piece.shape[0] - share) for piece in parts] for parts in (own_parts, other_parts)
        )
        if xor:
            own_parts.append((pair_rows[1], 2 * high))
            other_parts.append((pair_rows[1], 2 * high + share))

        @pl.when(core == 0)
        def _():
            fill(own_parts, other_parts)

        @pl.when(core != 0)
        def _():
            fill(other_parts, own_parts)

        for number, pair in enumerate(pair_rows):
            start = prompt + number * high
            keys[start : start + high, :] = pair[:high, :]
            values[start : start + high, :] = pair[high : 2 * high, :]

    def place(shape, axis, start):
        index = lax.broadcasted_iota(jnp.int32, shape, axis) + start
        slot = (index % (2 * band)) // band
        return slot, ((index // (2 * band)) ^ me) * band + index % band

    length_a, length_b = length_ref[0], length_ref[1]
    row_slot, row_at = place((rows, total_rows), 0, bands[0] * high)
    col_slot, col_at = place((rows, total_rows), 1, 0)
    tree = jnp.where(
        row_slot == 0,
        jnp.where(col_slot == 0, tree_ref[0, 0], tree_ref[0, 1]),
        jnp.where(col_slot == 0, tree_ref[1, 0], tree_ref[1, 1]),
    )
    visible = (
        (tree == 1)
        & (col_at < jnp.where(col_slot == 0, length_a, length_b))
        & ((row_slot != col_slot) | (col_at <= row_at))
    )
    slot, at = place((rows, size), 0, bands[0] * high)
    live = (at < jnp.where(slot == 0, length_a, length_b)).astype(jnp.float32)
    live_bf = live.astype(jnp.bfloat16)
    all_keys = keys[...]
    all_values = values[...]

    def put(ref, value, head, placed):
        if not xor:
            ref[head] = value
            return
        for number, which in enumerate(placed):
            for one in range(2):
                start = number * high + one * band
                at = pl.multiple_of((which ^ me) * band, 16)
                ref[one, pl.ds(at, band), head * size : (head + 1) * size] = value[start : start + band, :]

    def rows_of(index):
        parts = [ref[index * high : (index + 1) * high, :] for ref in head_rows]
        return parts[0] if len(parts) == 1 else jnp.concatenate(parts, axis=0)

    key_total, value_total = (None, None) if first else (key_before[...], value_before[...])
    start = 0
    for count in GROUPS if sum(GROUPS) == heads else (heads,):
        query = jnp.concatenate([rows_of(start + head) for head in range(count)], axis=0)
        grad = jnp.concatenate([rows_of(heads + start + head) * live_bf for head in range(count)], axis=0)
        scores = dot(query, all_keys, NT)
        prompt_scores = scores[:, :prompt]
        tree_scores = jnp.concatenate(
            [jnp.where(visible, scores[head * rows : (head + 1) * rows, prompt:], -1e30) for head in range(count)],
            axis=0,
        )
        top = jnp.maximum(
            jnp.max(prompt_scores, axis=1, keepdims=True), jnp.max(tree_scores, axis=1, keepdims=True)
        )
        scores = jnp.concatenate([prompt_scores, tree_scores], axis=1)
        powers = jnp.exp2((scores - top) * (scale * LOG2E))
        probs = powers * (1.0 / jnp.sum(powers, axis=1, keepdims=True))
        probs_b = probs.astype(jnp.bfloat16)
        attended = dot(probs_b, all_values, NN)
        attended = jnp.concatenate(
            [(attended[head * rows : (head + 1) * rows] * live).astype(jnp.bfloat16) for head in range(count)], axis=0
        )
        delta = jnp.sum(grad.astype(jnp.float32) * attended.astype(jnp.float32), axis=1, keepdims=True)
        dscore = (probs * (dot(grad, all_values, NT) - delta)).astype(jnp.bfloat16)
        grad_query = (dot(dscore, all_keys, NN) * scale).astype(jnp.bfloat16)
        key_part = dot(query.T, dscore, NN)
        value_part = dot(grad.T, probs_b, NN)
        key_total = key_part if key_total is None else key_total + key_part
        value_total = value_part if value_total is None else value_total + value_part
        for head in range(count):
            for ref, result in ((att_ref, attended), (gq_ref, grad_query)):
                result = result[head * rows : (head + 1) * rows, :]
                if last:
                    put(ref, result, start + head, bands)
                else:
                    ref[start + head] = result
        start += count
    if not last:
        refs[0][...] = key_total
        refs[1][...] = value_total
        return
    if not first:
        for head in range(heads):
            for ref, before in ((att_ref, att_before), (gq_ref, gq_before)):
                put(ref, before[head], head, range(bands[0]))
    gk_ref, gv_ref, keep_ref, send_ref = refs
    for ref, result in ((gk_ref, key_total[:, prompt:] * scale), (gv_ref, value_total[:, prompt:])):
        put(ref, result.T.astype(jnp.bfloat16), 0, range(row_count))

    def fill_sums(key_ref, value_ref):
        for number in range(row_count):
            part = slice(number * share, (number + 1) * share)
            key_ref[number] = (key_total[:, part] * scale).astype(key_ref.dtype)
            value_ref[number] = value_total[:, part].astype(value_ref.dtype)

    @pl.when(core == 0)
    def _():
        fill_sums(keep_ref, send_ref)

    @pl.when(core != 0)
    def _():
        fill_sums(send_ref, keep_ref)


def combine_kernel(keep_ref, received_ref, *outs):
    for number, out in enumerate(outs):
        out[...] = (keep_ref[number] + received_ref[number].astype(jnp.float32)).astype(out.dtype)


def finish_kernel(*refs):
    mine, theirs, out_ref = refs[: len(refs) // 2], refs[len(refs) // 2 : -1], refs[-1]
    core = lax.axis_index("rep")
    for parts, place in ((mine, core), (theirs, 1 - core)):
        total = parts[0][...]
        for part in parts[1:]:
            total = total + part[...].astype(jnp.float32)
        out_ref[place] = total.T


def swap_cores(value):
    return lax.ppermute(value, "rep", [(0, 1), (1, 0)])


def to_far(value, far):
    return lax.ppermute(value, "seq", [(chip, chip ^ far) for chip in range(lax.axis_size("seq"))])


def spread(parts):
    order = sorted(range(1, len(parts)), key=lambda far: -(far & 2) - (far == 3))
    got = {far: to_far(parts[far], far) for far in order}
    return [parts[0]] + [got[far] for far in range(1, len(parts))]


def per_device(
    queries, response_keys, response_values, grad_out, prompt_keys, prompt_values, packing, lengths, tree_mask
):
    slots, seg_length, size = response_keys.shape
    heads = queries.shape[2] // size
    chips = lax.axis_size("seq")
    band = seg_length // chips
    share = prompt_keys.shape[0]
    prompt = share * chips
    rows = slots * seg_length
    core = lax.axis_index("rep")
    xor = band % 16 == 0 and chips == 4
    bf16 = jnp.bfloat16
    sources = (response_keys, response_values, queries, grad_out)

    wanted = lax.dynamic_index_in_dim(packing.reshape(chips, 2, slots), core, 1, keepdims=False)
    if xor:
        tiles = [(0, 0), (1, 0)] + [(source, one) for source in (2, 3) for one in range(heads)]
        counts = [2, 2 * heads]
        high = slots * band
        length = len(tiles) * high
        packed = pl.pallas_call(
            functools.partial(pack_kernel, band, tiles),
            out_shape=[jax.ShapeDtypeStruct((one, size), bf16) for one in [length + share] * 3 + [length] * (chips - 3)],
            in_specs=[HBM] * 6,
            out_specs=[VMEM] * chips,
            scratch_shapes=[pltpu.VMEM(source.shape, bf16) for source in sources] + [pltpu.SemaphoreType.DMA((7,))],
            compiler_params=FULL,
            name="pack",
        )(*sources, prompt_keys, prompt_values)
        mine = spread(packed)
        theirs = [swap_cores(piece) for piece in mine]
        picked = pl.pallas_call(
            functools.partial(pick_kernel, band, chips, counts),
            out_shape=[
                jax.ShapeDtypeStruct((count * high + (2 * share if (number, far) == (0, 1) else 0), size), bf16)
                for number, count in enumerate(counts)
                for far in range(chips)
            ],
            in_specs=[SMEM] + [VMEM] * (2 * chips),
            out_specs=[VMEM] * (chips * len(counts)),
            scratch_shapes=[pltpu.VMEM((2 * chips, len(tiles) * high, size), bf16)],
            compiler_params=SMALL,
            name="pick",
        )(wanted, *mine, *theirs)
        head_rows = spread(picked[chips:])
        pair_rows = spread(picked[:chips])
        prompt_own, prompt_other = mine[:3], theirs[:3]
    else:
        piece = jnp.concatenate(sources, axis=2)
        tiles = piece.shape[2] // size
        piece = piece.reshape(slots, chips, band, tiles, size).transpose(1, 0, 3, 2, 4)
        mine = lax.all_to_all(piece, "seq", split_axis=0, concat_axis=0)
        theirs = swap_cores(mine)
        both = jnp.stack([jnp.where(core == 0, mine, theirs), jnp.where(core == 0, theirs, mine)], axis=1)
        both = both.reshape(chips * 2 * slots, tiles, band, size)
        picked = jnp.take(both, wanted.reshape(-1), axis=0).reshape(chips, slots, tiles, band, size)
        moved = lax.all_to_all(picked, "seq", split_axis=0, concat_axis=0)
        moved = moved.transpose(2, 0, 1, 3, 4).reshape(tiles * rows, size)
        pair_rows, head_rows = [moved[: 2 * rows]], [moved[2 * rows :]]
        prompt_mine = jnp.where(core == 0, prompt_keys, prompt_values)
        prompt_own = [lax.all_gather(prompt_mine, "seq", axis=0, tiled=True)]
        prompt_other = [swap_cores(prompt_own[0])]

    row_count = len(pair_rows)
    high = rows // row_count
    every = prompt + rows
    f32 = jnp.float32
    wide = (slots, seg_length, heads * size) if xor else (heads, rows, size)
    narrow = (slots, seg_length, size) if xor else (1, rows, size)
    parts = [(0, 1), (2, 3)] if xor else [(0,)]
    carried = []
    for bands in parts:
        first, last = bands is parts[0], bands is parts[-1]
        operands = [head_rows[one] for one in bands]
        operands += [*pair_rows, *prompt_own, *prompt_other] if first else carried
        pair_shapes = [jax.ShapeDtypeStruct((every, size), bf16)] * 2
        if last:
            out_shape = [jax.ShapeDtypeStruct(shape, bf16) for shape in (wide, wide, narrow, narrow)]
            out_shape += [jax.ShapeDtypeStruct((row_count, size, prompt // row_count), dtype) for dtype in (f32, bf16)]
        else:
            out_shape = [jax.ShapeDtypeStruct((heads, high * len(bands), size), bf16)] * 2 + pair_shapes
            out_shape += [jax.ShapeDtypeStruct((size, every), f32)] * 2
        count = heads * high * len(bands) * every
        results = pl.pallas_call(
            functools.partial(attend_kernel, band, heads, rows, bands, first, last, xor, row_count),
            out_shape=out_shape,
            in_specs=[SMEM, SMEM] + [VMEM] * len(operands),
            out_specs=[VMEM] * len(out_shape),
            scratch_shapes=[pltpu.VMEM((every, size), bf16)] * 2 if first and last else [],
            compiler_params=LARGE,
            cost_estimate=pl.CostEstimate(
                flops=24 * count * size, bytes_accessed=1 << 20, transcendentals=count
            ),
            name="attend",
        )(lengths, tree_mask, *operands)
        if not last:
            att_part, gq_part, keys, values, key_part, value_part = results
            carried = [keys, values, att_part, gq_part, key_part, value_part]
    attended, grad_queries, grad_keys, grad_values, keep, send = results
    if not xor:

        def restore(value):
            value = value.reshape(-1, chips, slots, band, size).transpose(2, 1, 3, 0, 4)
            return value.reshape(slots, seg_length, -1)

        attended, grad_queries, grad_keys, grad_values = (
            restore(value) for value in (attended, grad_queries, grad_keys, grad_values)
        )

    received = swap_cores(send)
    if xor:
        block = (size, share)
        total = pl.pallas_call(
            combine_kernel,
            out_shape=[jax.ShapeDtypeStruct(block, bf16 if far else jnp.float32) for far in range(chips)],
            in_specs=[VMEM] * 2,
            out_specs=[VMEM] * chips,
            compiler_params=SMALL,
            name="combine",
        )(keep, received)
        arrived = spread(total)
        swapped = [swap_cores(part) for part in arrived]
        prompt_grads = pl.pallas_call(
            finish_kernel,
            out_shape=jax.ShapeDtypeStruct((2, share, size), jnp.float32),
            in_specs=[VMEM] * (2 * chips),
            out_specs=VMEM,
            compiler_params=SMALL,
            name="finish",
        )(*arrived, *swapped)
    else:
        total = (keep + received.astype(jnp.float32)).reshape(size, chips, share).transpose(1, 0, 2).astype(bf16)
        arrived = lax.all_to_all(total, "seq", split_axis=0, concat_axis=0)
        own = jnp.sum(arrived.astype(jnp.float32), axis=0).T
        other = swap_cores(own)
        prompt_grads = jnp.stack([jnp.where(core == 0, own, other), jnp.where(core == 0, other, own)])
    return attended, grad_queries, grad_keys, grad_values, prompt_grads


def solution(mesh):
    segments = P(("groups", "seq", "rep"), None, "head")
    in_specs = (
        segments,
        segments,
        segments,
        segments,
        P(("groups", "seq"), "head"),
        P(("groups", "seq"), "head"),
        P("groups"),
        P(("groups", "seq", "rep")),
        P(("groups", "seq", "rep"), None),
    )
    out_specs = (segments, segments, segments, segments, P(None, ("groups", "seq"), "head"))
    return jax.shard_map(per_device, mesh=mesh, in_specs=in_specs, out_specs=out_specs, check_vma=False)
```

time: 93.2 us -> 85.8 us (0.921)
  Pallas kernels: 13.3 us -> 17.4 us
  starting transfers between devices: 26.3 us -> 22.9 us
  other arithmetic: 3.09 us -> 0 us
  local copies, waits for them, and re-layouts: 4.28 us -> 1.73 us
  waiting for transfers between devices: 45.1 us -> 42.9 us
    pallas_call x3 -> x6, Pallas kernels: 13.3 us -> 17.4 us  [the longest x2 13.1 us: per_device(): pl.pallas_call(functools.partial(attend_kernel, band, heads, rows, bands,...]
    ppermute x12, starting transfers between devices: 24.8 us -> 21.9 us  [to_far(): lax.ppermute(value, 'seq', [(chip, chip ^ far) for chip in range(lax.axis...]
    unnamed x18 -> x8, local copies, waits for them, and re-layouts: 3.64 us -> 0.98 us
    ppermute x10 -> x9, waiting for transfers between devices: 5 us -> 3.58 us  [swap_cores(): return lax.ppermute(value, 'rep', [(0, 1), (1, 0)])]
    convert_element_type x1 -> x0, other arithmetic: 1.19 us -> none  [per_device(): arrived = spread([total[0]] + [part.astype(bf16) for part in total[1:]])]
    transpose x1 -> x0, other arithmetic: 1.03 us -> none  [per_device(): own = sum((part.astype(jnp.float32) for part in arrived)).T]
  transfers between devices with their start and end apart: 22 -> 21, of which waited for: 13 -> 11; matrix products, arithmetic and copies ran while one was open for 0% -> 1% of each run, Pallas kernels for 1% -> 7%
where the time goes in v3:
time: 85.8 us; the launch traced here: 85.6 us
  waiting for transfers between devices  42.9 us (50%)
  starting transfers between devices  22.9 us (27%)
  Pallas kernels  17.4 us (20%)
  local copies, waits for them, and re-layouts  1.73 us (2%)
    ppermute x12, waiting for transfers between devices, to_far(): lax.ppermute(value, 'seq', [(chip, chip ^ far) for chip in range(lax.axis...  39.3 us
    ppermute x12, starting transfers between devices, to_far(): lax.ppermute(value, 'seq', [(chip, chip ^ far) for chip in range(lax.axis...  21.9 us
    pallas_call x2, Pallas kernels, per_device(): pl.pallas_call(functools.partial(attend_kernel, band, heads, rows, bands,...  13.1 us
    ppermute x9, waiting for transfers between devices, swap_cores(): return lax.ppermute(value, 'rep', [(0, 1), (1, 0)])  3.58 us
    pallas_call x1, Pallas kernels, per_device(): pl.pallas_call(functools.partial(pack_kernel, band, tiles), out_shape=[ja...  2.34 us
  transfers between devices with their start and end apart: 21, of which 11 were waited for; matrix products, arithmetic and copies ran while one was open for 1% of the time, Pallas kernels for 7%

profile of v3, /device:TPU:0, one launch (start us, length us, event | category | flops | bytes accessed | tf_op | source)
XLA Modules:
  0.0 85.6 jit_solution(15049305355021141694)
XLA Ops:
  0.6 2.3 %pack.1 = (bf16[1280,128]{1,0:T(8,128)(2,1)}, bf16[1280,128]{1,0:T(8,128)(2,1)}, bf16[1280,128]{1,0:T(8,128)(2,1)}, bf16[768,128]{1,0:T(8,128)(2,1)}) custom-call(bf16[2,128,128]{2,1,0:T(8,128)(2,1)} %k_hbm.1, bf16[2,128,128]{2,1,0:T(8,128)(2,1)} %v_hbm.1, bf16[2,128,640]{2,1,0:T(8,128)(2,1)} %q_hbm.1, bf16[2,128,640]{2,1,0:T(8,128)(2,1)} %g_hbm.1, ...), custom_call_target="tpu_custom_call" | custom-call | tf_op jit(solution)/shard_map/pack/pallas_call | solution.py:312
  3.0 3.1 %collective-permute-start = (bf16[1280,128]{1,0:T(8,128)(2,1)}, bf16[1280,128]{1,0:T(8,128)(2,1)S(1)}, u32[]{:S(2)}, u32[]{:S(2)}) collective-permute-start(bf16[1280,128]{1,0:T(8,128)(2,1)} %get-tuple-element.34), channel_id=1, source_target_pairs={{0,4},{4,0},{8,12},{12,8},{1,5},{5,1},{9,13},{13,9},{2,6},{6,2},{1... | collective-permute-start | bytes 983048 | tf_op jit(solution)/shard_map/ppermute | solution.py:282
  6.1 2.6 %collective-permute-start.1 = (bf16[1280,128]{1,0:T(8,128)(2,1)}, bf16[1280,128]{1,0:T(8,128)(2,1)S(1)}, u32[]{:S(2)}, u32[]{:S(2)}) collective-permute-start(bf16[1280,128]{1,0:T(8,128)(2,1)} %get-tuple-element.35), channel_id=1, source_target_pairs={{0,8},{4,12},{8,0},{12,4},{1,9},{5,13},{9,1},{13,5},{2,10},{6,14},... | collective-permute-start | bytes 983048 | tf_op jit(solution)/shard_map/ppermute | solution.py:282
  8.7 0.0 collective-permute-start.2
  8.7 0.0 collective-permute-start.3
  8.7 11.6 %collective-permute-done.refs_1_.refs_7_ = bf16[1280,128]{1,0:T(8,128)(2,1)S(1)} collective-permute-done((bf16[1280,128]{1,0:T(8,128)(2,1)}, bf16[1280,128]{1,0:T(8,128)(2,1)S(1)}, u32[]{:S(2)}, u32[]{:S(2)}) %collective-permute-start) | collective-permute-done | bytes 327712 | tf_op jit(solution)/shard_map/ppermute | solution.py:282
  20.2 0.0 collective-permute-start.4
  20.2 8.8 %collective-permute-done.1.refs_2_.refs_8_ = bf16[1280,128]{1,0:T(8,128)(2,1)S(1)} collective-permute-done((bf16[1280,128]{1,0:T(8,128)(2,1)}, bf16[1280,128]{1,0:T(8,128)(2,1)S(1)}, u32[]{:S(2)}, u32[]{:S(2)}) %collective-permute-start.1) | collective-permute-done | bytes 327712 | tf_op jit(solution)/shard_map/ppermute | solution.py:282
  29.1 0.0 collective-permute-start.5
  29.1 0.0 collective-permute-done.2.refs_3_
  29.1 0.5 collective-permute-start.6
  29.6 0.7 reshape.13
  30.3 0.0 collective-permute-done.3.refs_4_.refs_9_
  30.3 0.6 collective-permute-done.6.refs_7_
  31.0 0.0 collective-permute-done.4.refs_5_.refs_10_
  31.0 0.0 collective-permute-done.5.refs_6_.refs_11_
  31.0 0.0 copy-start
  31.0 1.0 %copy-done = bf16[1280,128]{1,0:T(8,128)(2,1)S(1)} copy-done((bf16[1280,128]{1,0:T(8,128)(2,1)S(1)}, bf16[1280,128]{1,0:T(8,128)(2,1)}, u32[]{:S(2)}) %copy-start) | copy-done | bytes 327704
  31.9 0.0 copy-start.1
  32.0 0.0 copy-start.2
  32.0 0.0 copy-start.3
  32.0 0.9 pick.1
  32.8 3.0 %collective-permute-start.10 = (bf16[1152,128]{1,0:T(8,128)(2,1)S(1)}, bf16[1152,128]{1,0:T(8,128)(2,1)S(1)}, u32[]{:S(2)}, u32[]{:S(2)}) collective-permute-start(bf16[1152,128]{1,0:T(8,128)(2,1)S(1)} %get-tuple-element.42), channel_id=1, source_target_pairs={{0,4},{4,0},{8,12},{12,8},{1,5},{5,1},{9,13},{13,9},{2,6},{6,2},{1... | collective-permute-start | bytes 884744 | tf_op jit(solution)/shard_map/ppermute | solution.py:282
  35.8 0.1 collective-permute-start.9
  35.8 3.0 %collective-permute-start.11 = (bf16[128,128]{1,0:T(8,128)(2,1)S(1)}, bf16[128,128]{1,0:T(8,128)(2,1)S(1)}, u32[]{:S(2)}, u32[]{:S(2)}) collective-permute-start(bf16[128,128]{1,0:T(8,128)(2,1)S(1)} %get-tuple-element.43), channel_id=1, source_target_pairs={{0,8},{4,12},{8,0},{12,4},{1,9},{5,13},{9,1},{13,5},{2,10},{6,14},... | collective-permute-start | bytes 98312 | tf_op jit(solution)/shard_map/ppermute | solution.py:282
  38.8 1.4 %collective-permute-start.12 = (bf16[128,128]{1,0:T(8,128)(2,1)S(1)}, bf16[128,128]{1,0:T(8,128)(2,1)S(1)}, u32[]{:S(2)}, u32[]{:S(2)}) collective-permute-start(bf16[128,128]{1,0:T(8,128)(2,1)S(1)} %get-tuple-element.44), channel_id=1, source_target_pairs={{0,12},{4,8},{8,4},{12,0},{1,13},{5,9},{9,5},{13,1},{2,14},{6,10},... | collective-permute-start | bytes 98312 | tf_op jit(solution)/shard_map/ppermute | solution.py:282
  40.2 0.2 collective-permute-start.7
  40.3 7.0 %collective-permute-done.11.refs_4_ = bf16[128,128]{1,0:T(8,128)(2,1)S(1)} collective-permute-done((bf16[128,128]{1,0:T(8,128)(2,1)S(1)}, bf16[128,128]{1,0:T(8,128)(2,1)S(1)}, u32[]{:S(2)}, u32[]{:S(2)}) %collective-permute-start.11) | collective-permute-done | bytes 32800 | tf_op jit(solution)/shard_map/ppermute | solution.py:282
  47.4 2.5 %collective-permute-start.8 = (bf16[640,128]{1,0:T(8,128)(2,1)S(1)}, bf16[640,128]{1,0:T(8,128)(2,1)S(1)}, u32[]{:S(2)}, u32[]{:S(2)}) collective-permute-start(bf16[640,128]{1,0:T(8,128)(2,1)S(1)} %get-tuple-element.38), channel_id=1, source_target_pairs={{0,12},{4,8},{8,4},{12,0},{1,13},{5,9},{9,5},{13,1},{2,14},{6,10},... | collective-permute-start | bytes 491528 | tf_op jit(solution)/shard_map/ppermute | solution.py:282
  49.8 1.2 %collective-permute-done.12.refs_5_ = bf16[128,128]{1,0:T(8,128)(2,1)S(1)} collective-permute-done((bf16[128,128]{1,0:T(8,128)(2,1)S(1)}, bf16[128,128]{1,0:T(8,128)(2,1)S(1)}, u32[]{:S(2)}, u32[]{:S(2)}) %collective-permute-start.12) | collective-permute-done | bytes 32800 | tf_op jit(solution)/shard_map/ppermute | solution.py:282
  51.0 0.5 collective-permute-done.9.refs_1_
  51.5 0.0 collective-permute-done.10.refs_3_
  51.5 0.0 copy-done.1
  51.5 0.0 copy-done.2
  51.5 0.0 copy-done.3
  51.5 6.0 %attend.2 = (bf16[5,128,128]{2,1,0:T(8,128)(2,1)S(1)}, bf16[5,128,128]{2,1,0:T(8,128)(2,1)S(1)}, bf16[2304,128]{1,0:T(8,128)(2,1)S(1)}, bf16[2304,128]{1,0:T(8,1...) custom-call(s32[2]{0:T(128)S(1)} %copy-done.3, s32[2,2]{1,0:T(2,128)S(1)} %copy-done.2, ...), custom_call_target="tpu_custom_call" | custom-call | flops 4529848320 | bytes 1048576 | tf_op jit(solution)/shard_map/attend/pallas_call | solution.py:375
  57.6 0.0 collective-permute-done.7.refs_0_
  57.6 0.0 collective-permute-done.8.refs_1_
  57.6 7.0 %attend.3 = (bf16[2,128,640]{2,1,0:T(8,128)(2,1)}, bf16[2,128,640]{2,1,0:T(8,128)(2,1)}, bf16[2,128,128]{2,1,0:T(8,128)(2,1)}, bf16[2,128,128]{2,1,0:T(8,128)(2,...) custom-call(s32[2]{0:T(128)S(1)} %copy-done.3, s32[2,2]{1,0:T(2,128)S(1)} %copy-done.2, ...), custom_call_target="tpu_custom_call" | custom-call | flops 4529848320 | bytes 1048576 | tf_op jit(solution)/shard_map/attend/pallas_call | solution.py:375
  64.6 0.0 collective-permute-start.13
  64.6 1.9 %collective-permute-done.13.received_ref = bf16[4,128,512]{2,1,0:T(8,128)(2,1)S(1)} collective-permute-done((bf16[4,128,512]{2,1,0:T(8,128)(2,1)S(1)}, bf16[4,128,512]{2,1,0:T(8,128)(2,1)S(1)}, u32[]{:S(2)}, u32[]{:S(2)}) %collective-permute-start.13) | collective-permute-done | bytes 524320 | tf_op jit(solution)/shard_map/ppermute | solution.py:278
  66.5 0.1 combine.1
  66.6 3.7 %collective-permute-start.14 = (bf16[128,512]{1,0:T(8,128)(2,1)S(1)}, bf16[128,512]{1,0:T(8,128)(2,1)S(1)}, u32[]{:S(2)}, u32[]{:S(2)}) collective-permute-start(bf16[128,512]{1,0:T(8,128)(2,1)S(1)} %get-tuple-element.58), channel_id=1, source_target_pairs={{0,4},{4,0},{8,12},{12,8},{1,5},{5,1},{9,13},{13,9},{2,6},{6,2},{1... | collective-permute-start | bytes 393224 | tf_op jit(solution)/shard_map/ppermute | solution.py:282
  70.4 0.0 collective-permute-start.15
  70.4 2.4 %collective-permute-start.16 = (bf16[128,512]{1,0:T(8,128)(2,1)S(1)}, bf16[128,512]{1,0:T(8,128)(2,1)S(1)}, u32[]{:S(2)}, u32[]{:S(2)}) collective-permute-start(bf16[128,512]{1,0:T(8,128)(2,1)S(1)} %get-tuple-element.60), channel_id=1, source_target_pairs={{0,12},{4,8},{8,4},{12,0},{1,13},{5,9},{9,5},{13,1},{2,14},{6,10},... | collective-permute-start | bytes 393224 | tf_op jit(solution)/shard_map/ppermute | solution.py:282
  72.8 0.0 collective-permute-start.17
  72.8 2.5 %collective-permute-done.14.refs_1_ = bf16[128,512]{1,0:T(8,128)(2,1)S(1)} collective-permute-done((bf16[128,512]{1,0:T(8,128)(2,1)S(1)}, bf16[128,512]{1,0:T(8,128)(2,1)S(1)}, u32[]{:S(2)}, u32[]{:S(2)}) %collective-permute-start.14) | collective-permute-done | bytes 131104 | tf_op jit(solution)/shard_map/ppermute | solution.py:282
  75.4 0.0 collective-permute-start.18
  75.4 7.7 %collective-permute-done.15.refs_2_ = bf16[128,512]{1,0:T(8,128)(2,1)S(1)} collective-permute-done((bf16[128,512]{1,0:T(8,128)(2,1)S(1)}, bf16[128,512]{1,0:T(8,128)(2,1)S(1)}, u32[]{:S(2)}, u32[]{:S(2)}) %collective-permute-start.15) | collective-permute-done | bytes 131104 | tf_op jit(solution)/shard_map/ppermute | solution.py:282
  83.1 0.0 collective-permute-start.19
  83.1 0.0 collective-permute-done.16.refs_3_
  83.1 0.5 collective-permute-start.20
  83.6 0.0 collective-permute-done.18.refs_5_
  83.6 0.8 collective-permute-done.19.refs_6_
  84.4 0.2 collective-permute-done.20.refs_7_
  84.6 0.0 collective-permute-done.17.refs_4_
  84.6 1.0 %finish.1 = f32[2,512,128]{2,1,0:T(8,128)} custom-call(f32[128,512]{1,0:T(8,128)S(1)} %get-tuple-element.57.refs_0_, bf16[128,512]{1,0:T(8,128)(2,1)S(1)} %collective-permute-done.14.refs_1_, bf16[128,512]{1,0:T(8,128)(2,1)S(1)} %collective-permute-done.15.refs_2_, bf16[128,512]{1,0:T(8,128)(2,1)S(1)} %collective-permute-done.16.refs_3_, ...), custom_call_target="tpu_custom_call" | custom-call | tf_op jit(solution)/shard_map/finish/pallas_call | solution.py:414
  (1 shorter events, 0.0 us)
Async XLA Ops:
  3.0 17.3 %collective-permute-start = (bf16[1280,128]{1,0:T(8,128)(2,1)}, bf16[1280,128]{1,0:T(8,128)(2,1)S(1)}, u32[]{:S(2)}, u32[]{:S(2)}) collective-permute-start(bf16[1280,128]{1,0:T(8,128)(2,1)} %get-tuple-element.34), channel_id=1, source_target_pairs={{0,4},{4,0},{8,12},{12,8},{1,5},{5,1},{9,13},{13,9},{2,6},{6,2},{1... | collective-permute-start | bytes 983048 | tf_op jit(solution)/shard_map/ppermute | solution.py:282
  6.1 23.0 %collective-permute-start.1 = (bf16[1280,128]{1,0:T(8,128)(2,1)}, bf16[1280,128]{1,0:T(8,128)(2,1)S(1)}, u32[]{:S(2)}, u32[]{:S(2)}) collective-permute-start(bf16[1280,128]{1,0:T(8,128)(2,1)} %get-tuple-element.35), channel_id=1, source_target_pairs={{0,8},{4,12},{8,0},{12,4},{1,9},{5,13},{9,1},{13,5},{2,10},{6,14},... | collective-permute-start | bytes 983048 | tf_op jit(solution)/shard_map/ppermute | solution.py:282
  8.7 20.4 %collective-permute-start.2 = (bf16[768,128]{1,0:T(8,128)(2,1)}, bf16[768,128]{1,0:T(8,128)(2,1)S(1)}, u32[]{:S(2)}, u32[]{:S(2)}) collective-permute-start(bf16[768,128]{1,0:T(8,128)(2,1)} %get-tuple-element.36), channel_id=1, source_target_pairs={{0,12},{4,8},{8,4},{12,0},{1,13},{5,9},{9,5},{13,1},{2,14},{6,10},... | collective-permute-start | bytes 589832 | tf_op jit(solution)/shard_map/ppermute | solution.py:282
  8.7 21.7 %collective-permute-start.3 = (bf16[1280,128]{1,0:T(8,128)(2,1)}, bf16[1280,128]{1,0:T(8,128)(2,1)S(1)}, u32[]{:S(2)}, u32[]{:S(2)}) collective-permute-start(bf16[1280,128]{1,0:T(8,128)(2,1)} %get-tuple-element.33.refs_0_.refs_6_), channel_id=1, source_target_pairs={{0,1},{1,0},{2,3},{3,2},{4,5},{5,4},{6,7},{7,6},{8,9},{9,8},{10,11... | collective-permute-start | bytes 983048 | tf_op jit(solution)/shard_map/ppermute | solution.py:278
  20.2 10.7 %collective-permute-start.4 = (bf16[1280,128]{1,0:T(8,128)(2,1)S(1)}, bf16[1280,128]{1,0:T(8,128)(2,1)S(1)}, u32[]{:S(2)}, u32[]{:S(2)}) collective-permute-start(bf16[1280,128]{1,0:T(8,128)(2,1)S(1)} %collective-permute-done.refs_1_.refs_7_), channel_id=1, source_target_pairs={{0,1},{1,0},{2,3},{3,2},{4,5},{5,4},{6,7},{7,6},{8,9},{9,8},{10,11... | collective-permute-start | bytes 983048 | tf_op jit(solution)/shard_map/ppermute | solution.py:278
  29.1 1.9 %collective-permute-start.5 = (bf16[1280,128]{1,0:T(8,128)(2,1)S(1)}, bf16[1280,128]{1,0:T(8,128)(2,1)S(1)}, u32[]{:S(2)}, u32[]{:S(2)}) collective-permute-start(bf16[1280,128]{1,0:T(8,128)(2,1)S(1)} %collective-permute-done.1.refs_2_.refs_8_), channel_id=1, source_target_pairs={{0,1},{1,0},{2,3},{3,2},{4,5},{5,4},{6,7},{7,6},{8,9},{9,8},{10,11... | collective-permute-start | bytes 983048 | tf_op jit(solution)/shard_map/ppermute | solution.py:278
  29.1 1.9 %collective-permute-start.6 = (bf16[768,128]{1,0:T(8,128)(2,1)S(1)}, bf16[768,128]{1,0:T(8,128)(2,1)S(1)}, u32[]{:S(2)}, u32[]{:S(2)}) collective-permute-start(bf16[768,128]{1,0:T(8,128)(2,1)S(1)} %collective-permute-done.2.refs_3_), channel_id=1, source_target_pairs={{0,1},{1,0},{2,3},{3,2},{4,5},{5,4},{6,7},{7,6},{8,9},{9,8},{10,11... | collective-permute-start | bytes 589832 | tf_op jit(solution)/shard_map/ppermute | solution.py:278
  31.0 1.0 %copy-start = (bf16[1280,128]{1,0:T(8,128)(2,1)S(1)}, bf16[1280,128]{1,0:T(8,128)(2,1)}, u32[]{:S(2)}) copy-start(bf16[1280,128]{1,0:T(8,128)(2,1)} %get-tuple-element.33.refs_0_.refs_6_) | copy-start | bytes 983044
  31.9 19.6 %copy-start.1 = (bf16[1280,128]{1,0:T(8,128)(2,1)S(1)}, bf16[1280,128]{1,0:T(8,128)(2,1)}, u32[]{:S(2)}) copy-start(bf16[1280,128]{1,0:T(8,128)(2,1)} %get-tuple-element.33.refs_0_.refs_6_) | copy-start | bytes 983044
  32.0 19.6 %copy-start.2 = (s32[2,2]{1,0:T(2,128)S(1)}, s32[2,2]{1,0:T(2,128)}, u32[]{:S(2)}) copy-start(s32[2,2]{1,0:T(2,128)} %tree_ref.3) | copy-start | bytes 52
  32.0 19.6 %copy-start.3 = (s32[2]{0:T(128)S(1)}, s32[2]{0:T(128)}, u32[]{:S(2)}) copy-start(s32[2]{0:T(128)} %length_ref.3) | copy-start | bytes 28
  32.8 18.7 %collective-permute-start.10 = (bf16[1152,128]{1,0:T(8,128)(2,1)S(1)}, bf16[1152,128]{1,0:T(8,128)(2,1)S(1)}, u32[]{:S(2)}, u32[]{:S(2)}) collective-permute-start(bf16[1152,128]{1,0:T(8,128)(2,1)S(1)} %get-tuple-element.42), channel_id=1, source_target_pairs={{0,4},{4,0},{8,12},{12,8},{1,5},{5,1},{9,13},{13,9},{2,6},{6,2},{1... | collective-permute-start | bytes 884744 | tf_op jit(solution)/shard_map/ppermute | solution.py:282
  35.8 15.7 %collective-permute-start.9 = (bf16[640,128]{1,0:T(8,128)(2,1)S(1)}, bf16[640,128]{1,0:T(8,128)(2,1)S(1)}, u32[]{:S(2)}, u32[]{:S(2)}) collective-permute-start(bf16[640,128]{1,0:T(8,128)(2,1)S(1)} %get-tuple-element.40), channel_id=1, source_target_pairs={{0,4},{4,0},{8,12},{12,8},{1,5},{5,1},{9,13},{13,9},{2,6},{6,2},{1... | collective-permute-start | bytes 491528 | tf_op jit(solution)/shard_map/ppermute | solution.py:282
  35.8 11.5 %collective-permute-start.11 = (bf16[128,128]{1,0:T(8,128)(2,1)S(1)}, bf16[128,128]{1,0:T(8,128)(2,1)S(1)}, u32[]{:S(2)}, u32[]{:S(2)}) collective-permute-start(bf16[128,128]{1,0:T(8,128)(2,1)S(1)} %get-tuple-element.43), channel_id=1, source_target_pairs={{0,8},{4,12},{8,0},{12,4},{1,9},{5,13},{9,1},{13,5},{2,10},{6,14},... | collective-permute-start | bytes 98312 | tf_op jit(solution)/shard_map/ppermute | solution.py:282
  38.8 12.2 %collective-permute-start.12 = (bf16[128,128]{1,0:T(8,128)(2,1)S(1)}, bf16[128,128]{1,0:T(8,128)(2,1)S(1)}, u32[]{:S(2)}, u32[]{:S(2)}) collective-permute-start(bf16[128,128]{1,0:T(8,128)(2,1)S(1)} %get-tuple-element.44), channel_id=1, source_target_pairs={{0,12},{4,8},{8,4},{12,0},{1,13},{5,9},{9,5},{13,1},{2,14},{6,10},... | collective-permute-start | bytes 98312 | tf_op jit(solution)/shard_map/ppermute | solution.py:282
  40.2 17.4 %collective-permute-start.7 = (bf16[640,128]{1,0:T(8,128)(2,1)S(1)}, bf16[640,128]{1,0:T(8,128)(2,1)S(1)}, u32[]{:S(2)}, u32[]{:S(2)}) collective-permute-start(bf16[640,128]{1,0:T(8,128)(2,1)S(1)} %get-tuple-element.37), channel_id=1, source_target_pairs={{0,8},{4,12},{8,0},{12,4},{1,9},{5,13},{9,1},{13,5},{2,10},{6,14},... | collective-permute-start | bytes 491528 | tf_op jit(solution)/shard_map/ppermute | solution.py:282
  47.4 10.2 %collective-permute-start.8 = (bf16[640,128]{1,0:T(8,128)(2,1)S(1)}, bf16[640,128]{1,0:T(8,128)(2,1)S(1)}, u32[]{:S(2)}, u32[]{:S(2)}) collective-permute-start(bf16[640,128]{1,0:T(8,128)(2,1)S(1)} %get-tuple-element.38), channel_id=1, source_target_pairs={{0,12},{4,8},{8,4},{12,0},{1,13},{5,9},{9,5},{13,1},{2,14},{6,10},... | collective-permute-start | bytes 491528 | tf_op jit(solution)/shard_map/ppermute | solution.py:282
  64.6 1.9 %collective-permute-start.13 = (bf16[4,128,512]{2,1,0:T(8,128)(2,1)S(1)}, bf16[4,128,512]{2,1,0:T(8,128)(2,1)S(1)}, u32[]{:S(2)}, u32[]{:S(2)}) collective-permute-start(bf16[4,128,512]{2,1,0:T(8,128)(2,1)S(1)} %get-tuple-element.56), channel_id=1, source_target_pairs={{0,1},{1,0},{2,3},{3,2},{4,5},{5,4},{6,7},{7,6},{8,9},{9,8},{10,11... | collective-permute-start | bytes 1572872 | tf_op jit(solution)/shard_map/ppermute | solution.py:278
  66.6 8.7 %collective-permute-start.14 = (bf16[128,512]{1,0:T(8,128)(2,1)S(1)}, bf16[128,512]{1,0:T(8,128)(2,1)S(1)}, u32[]{:S(2)}, u32[]{:S(2)}) collective-permute-start(bf16[128,512]{1,0:T(8,128)(2,1)S(1)} %get-tuple-element.58), channel_id=1, source_target_pairs={{0,4},{4,0},{8,12},{12,8},{1,5},{5,1},{9,13},{13,9},{2,6},{6,2},{1... | collective-permute-start | bytes 393224 | tf_op jit(solution)/shard_map/ppermute | solution.py:282
  70.4 12.7 %collective-permute-start.15 = (bf16[128,512]{1,0:T(8,128)(2,1)S(1)}, bf16[128,512]{1,0:T(8,128)(2,1)S(1)}, u32[]{:S(2)}, u32[]{:S(2)}) collective-permute-start(bf16[128,512]{1,0:T(8,128)(2,1)S(1)} %get-tuple-element.59), channel_id=1, source_target_pairs={{0,8},{4,12},{8,0},{12,4},{1,9},{5,13},{9,1},{13,5},{2,10},{6,14},... | collective-permute-start | bytes 393224 | tf_op jit(solution)/shard_map/ppermute | solution.py:282
  70.4 12.7 %collective-permute-start.16 = (bf16[128,512]{1,0:T(8,128)(2,1)S(1)}, bf16[128,512]{1,0:T(8,128)(2,1)S(1)}, u32[]{:S(2)}, u32[]{:S(2)}) collective-permute-start(bf16[128,512]{1,0:T(8,128)(2,1)S(1)} %get-tuple-element.60), channel_id=1, source_target_pairs={{0,12},{4,8},{8,4},{12,0},{1,13},{5,9},{9,5},{13,1},{2,14},{6,10},... | collective-permute-start | bytes 393224 | tf_op jit(solution)/shard_map/ppermute | solution.py:282
  72.8 11.8 %collective-permute-start.17 = (f32[128,512]{1,0:T(8,128)S(1)}, f32[128,512]{1,0:T(8,128)S(1)}, u32[]{:S(2)}, u32[]{:S(2)}) collective-permute-start(f32[128,512]{1,0:T(8,128)S(1)} %get-tuple-element.57.refs_0_), channel_id=1, source_target_pairs={{0,1},{1,0},{2,3},{3,2},{4,5},{5,4},{6,7},{7,6},{8,9},{9,8},{10,11... | collective-permute-start | bytes 786440 | tf_op jit(solution)/shard_map/ppermute | solution.py:278
  75.4 8.3 %collective-permute-start.18 = (bf16[128,512]{1,0:T(8,128)(2,1)S(1)}, bf16[128,512]{1,0:T(8,128)(2,1)S(1)}, u32[]{:S(2)}, u32[]{:S(2)}) collective-permute-start(bf16[128,512]{1,0:T(8,128)(2,1)S(1)} %collective-permute-done.14.refs_1_), channel_id=1, source_target_pairs={{0,1},{1,0},{2,3},{3,2},{4,5},{5,4},{6,7},{7,6},{8,9},{9,8},{10,11... | collective-permute-start | bytes 393224 | tf_op jit(solution)/shard_map/ppermute | solution.py:278
  83.1 1.3 %collective-permute-start.19 = (bf16[128,512]{1,0:T(8,128)(2,1)S(1)}, bf16[128,512]{1,0:T(8,128)(2,1)S(1)}, u32[]{:S(2)}, u32[]{:S(2)}) collective-permute-start(bf16[128,512]{1,0:T(8,128)(2,1)S(1)} %collective-permute-done.15.refs_2_), channel_id=1, source_target_pairs={{0,1},{1,0},{2,3},{3,2},{4,5},{5,4},{6,7},{7,6},{8,9},{9,8},{10,11... | collective-permute-start | bytes 393224 | tf_op jit(solution)/shard_map/ppermute | solution.py:278
  83.1 1.5 %collective-permute-start.20 = (bf16[128,512]{1,0:T(8,128)(2,1)S(1)}, bf16[128,512]{1,0:T(8,128)(2,1)S(1)}, u32[]{:S(2)}, u32[]{:S(2)}) collective-permute-start(bf16[128,512]{1,0:T(8,128)(2,1)S(1)} %collective-permute-done.16.refs_3_), channel_id=1, source_target_pairs={{0,1},{1,0},{2,3},{3,2},{4,5},{5,4},{6,7},{7,6},{8,9},{9,8},{10,11... | collective-permute-start | bytes 393224 | tf_op jit(solution)/shard_map/ppermute | solution.py:278

commit v4 on v3

--- a/solution.py
+++ b/solution.py
@@ -65,44 +65,30 @@
 
 
 def pick_kernel(band, chips, counts, wanted_ref, *refs):
-    pieces, outs, held = refs[: 2 * chips], refs[2 * chips : -1], refs[-1]
+    pieces, outs, held = refs[: 2 * chips], list(refs[2 * chips : -1]), refs[-1]
     me = lax.axis_index("seq")
     core = lax.axis_index("rep")
     for number, piece in enumerate(pieces):
         held[number] = piece[: held.shape[1], :]
-    start = 2 * 2 * band
+    near = outs.pop()
+    start = sum(counts) * 2 * band
     for piece in (pieces[2], pieces[chips + 2]):
         passed = piece[held.shape[1] :, :]
-        outs[1][start : start + passed.shape[0], :] = passed
+        near[start : start + passed.shape[0], :] = passed
         start += passed.shape[0]
     for far in range(chips):
+        targets = [(near, 0), (near, counts[0])] if far == 1 else [(outs.pop(0), 0), (outs.pop(0), 0)]
         for slot in range(2):
             chosen = wanted_ref[me ^ far, slot]
             device = chosen // 2
             number = ((device // 2) ^ me) + chips * ((device % 2) ^ core)
             tile = 0
-            for chunk, count in enumerate(counts):
-                out = outs[chunk * chips + far]
+            for (out, base), count in zip(targets, counts):
                 for one in range(count):
                     start = pl.multiple_of(tile * 2 * band + (chosen % 2) * band, 16)
-                    row = one * 2 * band + slot * band
+                    row = (base + one) * 2 * band + slot * band
                     out[row : row + band, :] = held[number, pl.ds(start, band), :]
                     tile += 1
-
-
-def combine_kernel(keep_ref, received_ref, *outs):
-    for number, out in enumerate(outs):
-        out[...] = (keep_ref[number] + received_ref[number].astype(jnp.float32)).astype(out.dtype)
-
-
-def finish_kernel(*refs):
-    mine, theirs, out_ref = refs[: len(refs) // 2], refs[len(refs) // 2 : -1], refs[-1]
-    core = lax.axis_index("rep")
-    for parts, place in ((mine, core), (theirs, 1 - core)):
-        total = parts[0][...]
-        for part in parts[1:]:
-            total = total + part[...].astype(jnp.float32)
-        out_ref[place] = total.T
 
 
 def attend_kernel(band, heads, total_rows, bands, first, last, xor, row_count, length_ref, tree_ref, *refs):
@@ -141,8 +127,8 @@
             [(piece, piece.shape[0] - share) for piece in parts] for parts in (own_parts, other_parts)
         )
         if xor:
-            own_parts.append((pair_rows[1], 2 * high))
-            other_parts.append((pair_rows[1], 2 * high + share))
+            own_parts.append((pair_rows[1], (2 + 2 * heads) * high))
+            other_parts.append((pair_rows[1], (2 + 2 * heads) * high + share))
 
         @pl.when(core == 0)
         def _():
@@ -192,7 +178,10 @@
                 ref[one, pl.ds(at, band), head * size : (head + 1) * size] = value[start : start + band, :]
 
     def rows_of(index):
-        parts = [ref[index * high : (index + 1) * high, :] for ref in head_rows]
+        parts = []
+        for which, ref in zip(bands, head_rows):
+            at = (index + 2 if xor and which == 1 else index) * high
+            parts.append(ref[at : at + high, :])
         return parts[0] if len(parts) == 1 else jnp.concatenate(parts, axis=0)
 
     key_total, value_total = (None, None) if first else (key_before[...], value_before[...])
@@ -264,6 +253,10 @@
         out[...] = (keep_ref[number] + received_ref[number].astype(jnp.float32)).astype(out.dtype)
 
 
+def add_kernel(part_ref, passed_ref, out_ref):
+    out_ref[...] = (part_ref[...] + passed_ref[...].astype(jnp.float32)).astype(out_ref.dtype)
+
+
 def finish_kernel(*refs):
     mine, theirs, out_ref = refs[: len(refs) // 2], refs[len(refs) // 2 : -1], refs[-1]
     core = lax.axis_index("rep")
@@ -320,21 +313,19 @@
         )(*sources, prompt_keys, prompt_values)
         mine = spread(packed)
         theirs = [swap_cores(piece) for piece in mine]
+        row_counts = [count * high for count in counts] * (chips - 1) + [length + 2 * share]
         picked = pl.pallas_call(
             functools.partial(pick_kernel, band, chips, counts),
-            out_shape=[
-                jax.ShapeDtypeStruct((count * high + (2 * share if (number, far) == (0, 1) else 0), size), bf16)
-                for number, count in enumerate(counts)
-                for far in range(chips)
-            ],
+            out_shape=[jax.ShapeDtypeStruct((one, size), bf16) for one in row_counts],
             in_specs=[SMEM] + [VMEM] * (2 * chips),
-            out_specs=[VMEM] * (chips * len(counts)),
+            out_specs=[VMEM] * len(row_counts),
             scratch_shapes=[pltpu.VMEM((2 * chips, len(tiles) * high, size), bf16)],
             compiler_params=SMALL,
             name="pick",
-        )(wanted, *mine, *theirs)
-        head_rows = spread(picked[chips:])
-        pair_rows = spread(picked[:chips])
+        )(wanted, mine[0][:length], *mine[1:], *theirs)
+        near = to_far(picked[6], 1)
+        pair_rows = [picked[0], near, to_far(picked[2], 2), to_far(picked[4], 3)]
+        head_rows = [picked[1], near, to_far(picked[3], 2), to_far(picked[5], 3)]
         prompt_own, prompt_other = mine[:3], theirs[:3]
     else:
         piece = jnp.concatenate(sources, axis=2)
@@ -403,18 +394,27 @@
         block = (size, share)
         total = pl.pallas_call(
             combine_kernel,
-            out_shape=[jax.ShapeDtypeStruct(block, bf16 if far else jnp.float32) for far in range(chips)],
+            out_shape=[jax.ShapeDtypeStruct(block, dtype) for dtype in (f32, bf16, f32, bf16)],
             in_specs=[VMEM] * 2,
             out_specs=[VMEM] * chips,
             compiler_params=SMALL,
             name="combine",
         )(keep, received)
-        arrived = spread(total)
+        passed = to_far(total[3], 1)
+        across = pl.pallas_call(
+            add_kernel,
+            out_shape=jax.ShapeDtypeStruct(block, bf16),
+            in_specs=[VMEM] * 2,
+            out_specs=VMEM,
+            compiler_params=SMALL,
+            name="add",
+        )(total[2], passed)
+        arrived = [total[0], to_far(total[1], 1), to_far(across, 2)]
         swapped = [swap_cores(part) for part in arrived]
         prompt_grads = pl.pallas_call(
             finish_kernel,
             out_shape=jax.ShapeDtypeStruct((2, share, size), jnp.float32),
-            in_specs=[VMEM] * (2 * chips),
+            in_specs=[VMEM] * 6,
             out_specs=VMEM,
             compiler_params=SMALL,
             name="finish",

time: 85.8 us -> 82.4 us (0.960)
  starting transfers between devices: 22.9 us -> 18.1 us
  waiting for transfers between devices: 42.9 us -> 44.8 us
    ppermute x12 -> x11, starting transfers between devices: 21.9 us -> 17.6 us  [to_far(): lax.ppermute(value, 'seq', [(chip, chip ^ far) for chip in range(lax.axis...]
    ppermute x12 -> x11, waiting for transfers between devices: 39.3 us -> 41.3 us  [to_far(): lax.ppermute(value, 'seq', [(chip, chip ^ far) for chip in range(lax.axis...]
    unnamed x8, local copies, waits for them, and re-layouts: 0.98 us -> 0.02 us
    slice x0 -> x1, local copies, waits for them, and re-layouts: none -> 0.94 us  [per_device(): mine[0][:length]]
    ppermute x9 -> x8, waiting for transfers between devices: 3.58 us -> 3.56 us  [swap_cores(): return lax.ppermute(value, 'rep', [(0, 1), (1, 0)])]
  transfers between devices with their start and end apart: 21 -> 19, of which waited for: 11 -> 11; matrix products, arithmetic and copies ran while one was open for 1% -> 1% of each run, Pallas kernels for 7% -> 7%
where the time goes in v4:
time: 82.4 us; the launch traced here: 82.2 us
  waiting for transfers between devices  44.8 us (54%)
  starting transfers between devices  18.1 us (22%)
  Pallas kernels  17.5 us (21%)
  local copies, waits for them, and re-layouts  1.06 us (1%)
    ppermute x11, waiting for transfers between devices, to_far(): lax.ppermute(value, 'seq', [(chip, chip ^ far) for chip in range(lax.axis...  41.3 us
    ppermute x11, starting transfers between devices, to_far(): lax.ppermute(value, 'seq', [(chip, chip ^ far) for chip in range(lax.axis...  17.6 us
    pallas_call x2, Pallas kernels, per_device(): pl.pallas_call(functools.partial(attend_kernel, band, heads, rows, bands,...  13.1 us
    ppermute x8, waiting for transfers between devices, swap_cores(): return lax.ppermute(value, 'rep', [(0, 1), (1, 0)])  3.56 us
    pallas_call x1, Pallas kernels, per_device(): pl.pallas_call(functools.partial(pack_kernel, band, tiles), out_shape=[ja...  2.34 us
  transfers between devices with their start and end apart: 19, of which 11 were waited for; matrix products, arithmetic and copies ran while one was open for 1% of the time, Pallas kernels for 7%

profile of v4, /device:TPU:0, one launch (start us, length us, event | category | flops | bytes accessed | tf_op | source)
XLA Modules:
  0.0 82.2 jit_solution(9067806177293040159)
XLA Ops:
  0.6 0.0 copy-start.3
  0.6 2.3 %pack.1 = (bf16[1280,128]{1,0:T(8,128)(2,1)}, bf16[1280,128]{1,0:T(8,128)(2,1)}, bf16[1280,128]{1,0:T(8,128)(2,1)}, bf16[768,128]{1,0:T(8,128)(2,1)}) custom-call(bf16[2,128,128]{2,1,0:T(8,128)(2,1)} %k_hbm.1, bf16[2,128,128]{2,1,0:T(8,128)(2,1)} %v_hbm.1, bf16[2,128,640]{2,1,0:T(8,128)(2,1)} %q_hbm.1, bf16[2,128,640]{2,1,0:T(8,128)(2,1)} %g_hbm.1, ...), custom_call_target="tpu_custom_call" | custom-call | tf_op jit(solution)/shard_map/pack/pallas_call | solution.py:305
  3.0 3.1 %collective-permute-start = (bf16[1280,128]{1,0:T(8,128)(2,1)}, bf16[1280,128]{1,0:T(8,128)(2,1)S(1)}, u32[]{:S(2)}, u32[]{:S(2)}) collective-permute-start(bf16[1280,128]{1,0:T(8,128)(2,1)} %get-tuple-element.33), channel_id=1, source_target_pairs={{0,4},{4,0},{8,12},{12,8},{1,5},{5,1},{9,13},{13,9},{2,6},{6,2},{1... | collective-permute-start | bytes 983048 | tf_op jit(solution)/shard_map/ppermute | solution.py:275
  6.1 2.6 %collective-permute-start.1 = (bf16[1280,128]{1,0:T(8,128)(2,1)}, bf16[1280,128]{1,0:T(8,128)(2,1)S(1)}, u32[]{:S(2)}, u32[]{:S(2)}) collective-permute-start(bf16[1280,128]{1,0:T(8,128)(2,1)} %get-tuple-element.34), channel_id=1, source_target_pairs={{0,8},{4,12},{8,0},{12,4},{1,9},{5,13},{9,1},{13,5},{2,10},{6,14},... | collective-permute-start | bytes 983048 | tf_op jit(solution)/shard_map/ppermute | solution.py:275
  8.7 0.0 collective-permute-start.2
  8.7 0.0 collective-permute-start.3
  8.7 11.6 %collective-permute-done.refs_1_.refs_7_ = bf16[1280,128]{1,0:T(8,128)(2,1)S(1)} collective-permute-done((bf16[1280,128]{1,0:T(8,128)(2,1)}, bf16[1280,128]{1,0:T(8,128)(2,1)S(1)}, u32[]{:S(2)}, u32[]{:S(2)}) %collective-permute-start) | collective-permute-done | bytes 327712 | tf_op jit(solution)/shard_map/ppermute | solution.py:275
  20.3 0.0 collective-permute-start.4
  20.3 8.8 %collective-permute-done.1.refs_2_.refs_8_ = bf16[1280,128]{1,0:T(8,128)(2,1)S(1)} collective-permute-done((bf16[1280,128]{1,0:T(8,128)(2,1)}, bf16[1280,128]{1,0:T(8,128)(2,1)S(1)}, u32[]{:S(2)}, u32[]{:S(2)}) %collective-permute-start.1) | collective-permute-done | bytes 327712 | tf_op jit(solution)/shard_map/ppermute | solution.py:275
  29.1 0.0 collective-permute-start.5
  29.1 0.0 collective-permute-done.2.refs_3_
  29.1 0.5 collective-permute-start.6
  29.6 0.9 %slice.3.refs_0_ = bf16[768,128]{1,0:T(8,128)(2,1)S(1)} slice(bf16[1280,128]{1,0:T(8,128)(2,1)} %get-tuple-element.32.refs_6_), slice={[0:768], [0:128]} | slice | bytes 393216 | tf_op jit(solution)/shard_map/slice | solution.py:325
  30.5 0.0 copy-start
  30.5 0.0 copy-start.1
  30.5 0.0 copy-start.2
  30.6 0.0 copy-done.3
  30.6 0.1 reshape.13
  30.7 0.0 collective-permute-done.3.refs_4_.refs_9_
  30.7 0.3 collective-permute-done.6.refs_7_
  31.0 0.0 collective-permute-done.4.refs_5_.refs_10_
  31.0 0.0 collective-permute-done.5.refs_6_.refs_11_
  31.0 0.9 %pick.1 = (bf16[128,128]{1,0:T(8,128)(2,1)S(1)}, bf16[640,128]{1,0:T(8,128)(2,1)S(1)}, bf16[128,128]{1,0:T(8,128)(2,1)S(1)}, bf16[640,128]{1,0:T(8,128)(2,1)S(1)...) custom-call(s32[4,2]{1,0:T(4,128)S(1)} %bitcast.1, ...), custom_call_target="tpu_custom_call" | custom-call | tf_op jit(solution)/shard_map/pick/pallas_call | solution.py:317
  31.8 3.0 %collective-permute-start.9 = (bf16[1792,128]{1,0:T(8,128)(2,1)S(1)}, bf16[1792,128]{1,0:T(8,128)(2,1)S(1)}, u32[]{:S(2)}, u32[]{:S(2)}) collective-permute-start(bf16[1792,128]{1,0:T(8,128)(2,1)S(1)} %get-tuple-element.39), channel_id=1, source_target_pairs={{0,4},{4,0},{8,12},{12,8},{1,5},{5,1},{9,13},{13,9},{2,6},{6,2},{1... | collective-permute-start | bytes 1376264 | tf_op jit(solution)/shard_map/ppermute | solution.py:275
  34.8 1.1 %collective-permute-start.10 = (bf16[128,128]{1,0:T(8,128)(2,1)S(1)}, bf16[128,128]{1,0:T(8,128)(2,1)S(1)}, u32[]{:S(2)}, u32[]{:S(2)}) collective-permute-start(bf16[128,128]{1,0:T(8,128)(2,1)S(1)} %get-tuple-element.41), channel_id=1, source_target_pairs={{0,8},{4,12},{8,0},{12,4},{1,9},{5,13},{9,1},{13,5},{2,10},{6,14},... | collective-permute-start | bytes 98312 | tf_op jit(solution)/shard_map/ppermute | solution.py:275
  35.9 1.4 %collective-permute-start.11 = (bf16[128,128]{1,0:T(8,128)(2,1)S(1)}, bf16[128,128]{1,0:T(8,128)(2,1)S(1)}, u32[]{:S(2)}, u32[]{:S(2)}) collective-permute-start(bf16[128,128]{1,0:T(8,128)(2,1)S(1)} %get-tuple-element.42), channel_id=1, source_target_pairs={{0,12},{4,8},{8,4},{12,0},{1,13},{5,9},{9,5},{13,1},{2,14},{6,10},... | collective-permute-start | bytes 98312 | tf_op jit(solution)/shard_map/ppermute | solution.py:275
  37.3 2.0 %collective-permute-start.7 = (bf16[640,128]{1,0:T(8,128)(2,1)S(1)}, bf16[640,128]{1,0:T(8,128)(2,1)S(1)}, u32[]{:S(2)}, u32[]{:S(2)}) collective-permute-start(bf16[640,128]{1,0:T(8,128)(2,1)S(1)} %get-tuple-element.36), channel_id=1, source_target_pairs={{0,8},{4,12},{8,0},{12,4},{1,9},{5,13},{9,1},{13,5},{2,10},{6,14},... | collective-permute-start | bytes 491528 | tf_op jit(solution)/shard_map/ppermute | solution.py:275
  39.3 1.4 %collective-permute-start.8 = (bf16[640,128]{1,0:T(8,128)(2,1)S(1)}, bf16[640,128]{1,0:T(8,128)(2,1)S(1)}, u32[]{:S(2)}, u32[]{:S(2)}) collective-permute-start(bf16[640,128]{1,0:T(8,128)(2,1)S(1)} %get-tuple-element.37), channel_id=1, source_target_pairs={{0,12},{4,8},{8,4},{12,0},{1,13},{5,9},{9,5},{13,1},{2,14},{6,10},... | collective-permute-start | bytes 491528 | tf_op jit(solution)/shard_map/ppermute | solution.py:275
  40.6 5.7 %collective-permute-done.10.refs_4_ = bf16[128,128]{1,0:T(8,128)(2,1)S(1)} collective-permute-done((bf16[128,128]{1,0:T(8,128)(2,1)S(1)}, bf16[128,128]{1,0:T(8,128)(2,1)S(1)}, u32[]{:S(2)}, u32[]{:S(2)}) %collective-permute-start.10) | collective-permute-done | bytes 32800 | tf_op jit(solution)/shard_map/ppermute | solution.py:275
  46.4 3.6 %collective-permute-done.11.refs_5_ = bf16[128,128]{1,0:T(8,128)(2,1)S(1)} collective-permute-done((bf16[128,128]{1,0:T(8,128)(2,1)S(1)}, bf16[128,128]{1,0:T(8,128)(2,1)S(1)}, u32[]{:S(2)}, u32[]{:S(2)}) %collective-permute-start.11) | collective-permute-done | bytes 32800 | tf_op jit(solution)/shard_map/ppermute | solution.py:275
  50.0 0.6 collective-permute-done.9.refs_1_.refs_3_
  50.6 0.0 copy-done
  50.6 0.0 copy-done.1
  50.6 0.0 copy-done.2
  50.6 6.0 %attend.2 = (bf16[5,128,128]{2,1,0:T(8,128)(2,1)S(1)}, bf16[5,128,128]{2,1,0:T(8,128)(2,1)S(1)}, bf16[2304,128]{1,0:T(8,128)(2,1)S(1)}, bf16[2304,128]{1,0:T(8,1...) custom-call(s32[2]{0:T(128)S(1)} %copy-done.2, s32[2,2]{1,0:T(2,128)S(1)} %copy-done.1, ...), custom_call_target="tpu_custom_call" | custom-call | flops 4529848320 | bytes 1048576 | tf_op jit(solution)/shard_map/attend/pallas_call | solution.py:366
  56.6 0.0 collective-permute-done.7.refs_0_
  56.6 0.0 collective-permute-done.8.refs_1_
  56.7 7.1 %attend.3 = (bf16[2,128,640]{2,1,0:T(8,128)(2,1)}, bf16[2,128,640]{2,1,0:T(8,128)(2,1)}, bf16[2,128,128]{2,1,0:T(8,128)(2,1)}, bf16[2,128,128]{2,1,0:T(8,128)(2,...) custom-call(s32[2]{0:T(128)S(1)} %copy-done.2, s32[2,2]{1,0:T(2,128)S(1)} %copy-done.1, ...), custom_call_target="tpu_custom_call" | custom-call | flops 4529848320 | bytes 1048576 | tf_op jit(solution)/shard_map/attend/pallas_call | solution.py:366
  63.7 0.0 collective-permute-start.12
  63.7 1.9 %collective-permute-done.12.received_ref = bf16[4,128,512]{2,1,0:T(8,128)(2,1)S(1)} collective-permute-done((bf16[4,128,512]{2,1,0:T(8,128)(2,1)S(1)}, bf16[4,128,512]{2,1,0:T(8,128)(2,1)S(1)}, u32[]{:S(2)}, u32[]{:S(2)}) %collective-permute-start.12) | collective-permute-done | bytes 524320 | tf_op jit(solution)/shard_map/ppermute | solution.py:271
  65.7 0.1 combine.1
  65.8 0.1 collective-permute-start.14
  65.9 2.0 %collective-permute-start.13 = (bf16[128,512]{1,0:T(8,128)(2,1)S(1)}, bf16[128,512]{1,0:T(8,128)(2,1)S(1)}, u32[]{:S(2)}, u32[]{:S(2)}) collective-permute-start(bf16[128,512]{1,0:T(8,128)(2,1)S(1)} %get-tuple-element.56), channel_id=1, source_target_pairs={{0,4},{4,0},{8,12},{12,8},{1,5},{5,1},{9,13},{13,9},{2,6},{6,2},{1... | collective-permute-start | bytes 393224 | tf_op jit(solution)/shard_map/ppermute | solution.py:275
  67.9 0.0 collective-permute-start.16
  67.9 4.3 %collective-permute-done.14.passed_ref = bf16[128,512]{1,0:T(8,128)(2,1)S(1)} collective-permute-done((bf16[128,512]{1,0:T(8,128)(2,1)S(1)}, bf16[128,512]{1,0:T(8,128)(2,1)S(1)}, u32[]{:S(2)}, u32[]{:S(2)}) %collective-permute-start.14) | collective-permute-done | bytes 131104 | tf_op jit(solution)/shard_map/ppermute | solution.py:275
  72.2 1.0 %collective-permute-start.15 = (bf16[128,512]{1,0:T(8,128)(2,1)S(1)}, bf16[128,512]{1,0:T(8,128)(2,1)S(1)}, u32[]{:S(2)}, u32[]{:S(2)}) collective-permute-start(bf16[128,512]{1,0:T(8,128)(2,1)S(1)} %add.6), channel_id=1, source_target_pairs={{0,8},{4,12},{8,0},{12,4},{1,9},{5,13},{9,1},{13,5},{2,10},{6,14},... | collective-permute-start | bytes 393224 | tf_op jit(solution)/shard_map/ppermute | solution.py:275
  73.3 0.9 %collective-permute-done.13.refs_1_ = bf16[128,512]{1,0:T(8,128)(2,1)S(1)} collective-permute-done((bf16[128,512]{1,0:T(8,128)(2,1)S(1)}, bf16[128,512]{1,0:T(8,128)(2,1)S(1)}, u32[]{:S(2)}, u32[]{:S(2)}) %collective-permute-start.13) | collective-permute-done | bytes 131104 | tf_op jit(solution)/shard_map/ppermute | solution.py:275
  74.2 0.0 collective-permute-start.17
  74.2 5.7 %collective-permute-done.15.refs_2_ = bf16[128,512]{1,0:T(8,128)(2,1)S(1)} collective-permute-done((bf16[128,512]{1,0:T(8,128)(2,1)S(1)}, bf16[128,512]{1,0:T(8,128)(2,1)S(1)}, u32[]{:S(2)}, u32[]{:S(2)}) %collective-permute-start.15) | collective-permute-done | bytes 131104 | tf_op jit(solution)/shard_map/ppermute | solution.py:275
  79.9 0.0 collective-permute-start.18
  79.9 0.0 collective-permute-done.16.refs_3_
  79.9 0.0 collective-permute-done.17.refs_4_
  79.9 1.3 %collective-permute-done.18.refs_5_ = bf16[128,512]{1,0:T(8,128)(2,1)S(1)} collective-permute-done((bf16[128,512]{1,0:T(8,128)(2,1)S(1)}, bf16[128,512]{1,0:T(8,128)(2,1)S(1)}, u32[]{:S(2)}, u32[]{:S(2)}) %collective-permute-start.18) | collective-permute-done | bytes 131104 | tf_op jit(solution)/shard_map/ppermute | solution.py:271
  81.2 1.0 %finish.1 = f32[2,512,128]{2,1,0:T(8,128)} custom-call(f32[128,512]{1,0:T(8,128)S(1)} %get-tuple-element.55.refs_0_, bf16[128,512]{1,0:T(8,128)(2,1)S(1)} %collective-permute-done.13.refs_1_, bf16[128,512]{1,0:T(8,128)(2,1)S(1)} %collective-permute-done.15.refs_2_, f32[128,512]{1,0:T(8,128)S(1)} %collective-permute-done.16.refs_3_, ...), custom_call_target="tpu_custom_call" | custom-call | tf_op jit(solution)/shard_map/finish/pallas_call | solution.py:414
  (2 shorter events, 0.0 us)
Async XLA Ops:
  0.6 29.9 %copy-start.3 = (s32[16]{0:T(128)S(1)}, s32[16]{0:T(128)}, u32[]{:S(2)}) copy-start(s32[16]{0:T(128)} %param.15) | copy-start | bytes 196
  3.0 17.3 %collective-permute-start = (bf16[1280,128]{1,0:T(8,128)(2,1)}, bf16[1280,128]{1,0:T(8,128)(2,1)S(1)}, u32[]{:S(2)}, u32[]{:S(2)}) collective-permute-start(bf16[1280,128]{1,0:T(8,128)(2,1)} %get-tuple-element.33), channel_id=1, source_target_pairs={{0,4},{4,0},{8,12},{12,8},{1,5},{5,1},{9,13},{13,9},{2,6},{6,2},{1... | collective-permute-start | bytes 983048 | tf_op jit(solution)/shard_map/ppermute | solution.py:275
  6.1 23.0 %collective-permute-start.1 = (bf16[1280,128]{1,0:T(8,128)(2,1)}, bf16[1280,128]{1,0:T(8,128)(2,1)S(1)}, u32[]{:S(2)}, u32[]{:S(2)}) collective-permute-start(bf16[1280,128]{1,0:T(8,128)(2,1)} %get-tuple-element.34), channel_id=1, source_target_pairs={{0,8},{4,12},{8,0},{12,4},{1,9},{5,13},{9,1},{13,5},{2,10},{6,14},... | collective-permute-start | bytes 983048 | tf_op jit(solution)/shard_map/ppermute | solution.py:275
  8.7 20.4 %collective-permute-start.2 = (bf16[768,128]{1,0:T(8,128)(2,1)}, bf16[768,128]{1,0:T(8,128)(2,1)S(1)}, u32[]{:S(2)}, u32[]{:S(2)}) collective-permute-start(bf16[768,128]{1,0:T(8,128)(2,1)} %get-tuple-element.35), channel_id=1, source_target_pairs={{0,12},{4,8},{8,4},{12,0},{1,13},{5,9},{9,5},{13,1},{2,14},{6,10},... | collective-permute-start | bytes 589832 | tf_op jit(solution)/shard_map/ppermute | solution.py:275
  8.7 22.0 %collective-permute-start.3 = (bf16[1280,128]{1,0:T(8,128)(2,1)}, bf16[1280,128]{1,0:T(8,128)(2,1)S(1)}, u32[]{:S(2)}, u32[]{:S(2)}) collective-permute-start(bf16[1280,128]{1,0:T(8,128)(2,1)} %get-tuple-element.32.refs_6_), channel_id=1, source_target_pairs={{0,1},{1,0},{2,3},{3,2},{4,5},{5,4},{6,7},{7,6},{8,9},{9,8},{10,11... | collective-permute-start | bytes 983048 | tf_op jit(solution)/shard_map/ppermute | solution.py:271
  20.3 10.7 %collective-permute-start.4 = (bf16[1280,128]{1,0:T(8,128)(2,1)S(1)}, bf16[1280,128]{1,0:T(8,128)(2,1)S(1)}, u32[]{:S(2)}, u32[]{:S(2)}) collective-permute-start(bf16[1280,128]{1,0:T(8,128)(2,1)S(1)} %collective-permute-done.refs_1_.refs_7_), channel_id=1, source_target_pairs={{0,1},{1,0},{2,3},{3,2},{4,5},{5,4},{6,7},{7,6},{8,9},{9,8},{10,11... | collective-permute-start | bytes 983048 | tf_op jit(solution)/shard_map/ppermute | solution.py:271
  29.1 1.9 %collective-permute-start.5 = (bf16[1280,128]{1,0:T(8,128)(2,1)S(1)}, bf16[1280,128]{1,0:T(8,128)(2,1)S(1)}, u32[]{:S(2)}, u32[]{:S(2)}) collective-permute-start(bf16[1280,128]{1,0:T(8,128)(2,1)S(1)} %collective-permute-done.1.refs_2_.refs_8_), channel_id=1, source_target_pairs={{0,1},{1,0},{2,3},{3,2},{4,5},{5,4},{6,7},{7,6},{8,9},{9,8},{10,11... | collective-permute-start | bytes 983048 | tf_op jit(solution)/shard_map/ppermute | solution.py:271
  29.1 1.9 %collective-permute-start.6 = (bf16[768,128]{1,0:T(8,128)(2,1)S(1)}, bf16[768,128]{1,0:T(8,128)(2,1)S(1)}, u32[]{:S(2)}, u32[]{:S(2)}) collective-permute-start(bf16[768,128]{1,0:T(8,128)(2,1)S(1)} %collective-permute-done.2.refs_3_), channel_id=1, source_target_pairs={{0,1},{1,0},{2,3},{3,2},{4,5},{5,4},{6,7},{7,6},{8,9},{9,8},{10,11... | collective-permute-start | bytes 589832 | tf_op jit(solution)/shard_map/ppermute | solution.py:271
  30.5 20.1 %copy-start = (bf16[1280,128]{1,0:T(8,128)(2,1)S(1)}, bf16[1280,128]{1,0:T(8,128)(2,1)}, u32[]{:S(2)}) copy-start(bf16[1280,128]{1,0:T(8,128)(2,1)} %get-tuple-element.32.refs_6_) | copy-start | bytes 983044
  30.5 20.1 %copy-start.1 = (s32[2,2]{1,0:T(2,128)S(1)}, s32[2,2]{1,0:T(2,128)}, u32[]{:S(2)}) copy-start(s32[2,2]{1,0:T(2,128)} %tree_ref.3) | copy-start | bytes 52
  30.5 20.1 %copy-start.2 = (s32[2]{0:T(128)S(1)}, s32[2]{0:T(128)}, u32[]{:S(2)}) copy-start(s32[2]{0:T(128)} %length_ref.3) | copy-start | bytes 28
  31.8 18.7 %collective-permute-start.9 = (bf16[1792,128]{1,0:T(8,128)(2,1)S(1)}, bf16[1792,128]{1,0:T(8,128)(2,1)S(1)}, u32[]{:S(2)}, u32[]{:S(2)}) collective-permute-start(bf16[1792,128]{1,0:T(8,128)(2,1)S(1)} %get-tuple-element.39), channel_id=1, source_target_pairs={{0,4},{4,0},{8,12},{12,8},{1,5},{5,1},{9,13},{13,9},{2,6},{6,2},{1... | collective-permute-start | bytes 1376264 | tf_op jit(solution)/shard_map/ppermute | solution.py:275
  34.8 11.6 %collective-permute-start.10 = (bf16[128,128]{1,0:T(8,128)(2,1)S(1)}, bf16[128,128]{1,0:T(8,128)(2,1)S(1)}, u32[]{:S(2)}, u32[]{:S(2)}) collective-permute-start(bf16[128,128]{1,0:T(8,128)(2,1)S(1)} %get-tuple-element.41), channel_id=1, source_target_pairs={{0,8},{4,12},{8,0},{12,4},{1,9},{5,13},{9,1},{13,5},{2,10},{6,14},... | collective-permute-start | bytes 98312 | tf_op jit(solution)/shard_map/ppermute | solution.py:275
  35.9 14.1 %collective-permute-start.11 = (bf16[128,128]{1,0:T(8,128)(2,1)S(1)}, bf16[128,128]{1,0:T(8,128)(2,1)S(1)}, u32[]{:S(2)}, u32[]{:S(2)}) collective-permute-start(bf16[128,128]{1,0:T(8,128)(2,1)S(1)} %get-tuple-element.42), channel_id=1, source_target_pairs={{0,12},{4,8},{8,4},{12,0},{1,13},{5,9},{9,5},{13,1},{2,14},{6,10},... | collective-permute-start | bytes 98312 | tf_op jit(solution)/shard_map/ppermute | solution.py:275
  37.3 19.4 %collective-permute-start.7 = (bf16[640,128]{1,0:T(8,128)(2,1)S(1)}, bf16[640,128]{1,0:T(8,128)(2,1)S(1)}, u32[]{:S(2)}, u32[]{:S(2)}) collective-permute-start(bf16[640,128]{1,0:T(8,128)(2,1)S(1)} %get-tuple-element.36), channel_id=1, source_target_pairs={{0,8},{4,12},{8,0},{12,4},{1,9},{5,13},{9,1},{13,5},{2,10},{6,14},... | collective-permute-start | bytes 491528 | tf_op jit(solution)/shard_map/ppermute | solution.py:275
  39.3 17.4 %collective-permute-start.8 = (bf16[640,128]{1,0:T(8,128)(2,1)S(1)}, bf16[640,128]{1,0:T(8,128)(2,1)S(1)}, u32[]{:S(2)}, u32[]{:S(2)}) collective-permute-start(bf16[640,128]{1,0:T(8,128)(2,1)S(1)} %get-tuple-element.37), channel_id=1, source_target_pairs={{0,12},{4,8},{8,4},{12,0},{1,13},{5,9},{9,5},{13,1},{2,14},{6,10},... | collective-permute-start | bytes 491528 | tf_op jit(solution)/shard_map/ppermute | solution.py:275
  63.7 1.9 %collective-permute-start.12 = (bf16[4,128,512]{2,1,0:T(8,128)(2,1)S(1)}, bf16[4,128,512]{2,1,0:T(8,128)(2,1)S(1)}, u32[]{:S(2)}, u32[]{:S(2)}) collective-permute-start(bf16[4,128,512]{2,1,0:T(8,128)(2,1)S(1)} %get-tuple-element.54), channel_id=1, source_target_pairs={{0,1},{1,0},{2,3},{3,2},{4,5},{5,4},{6,7},{7,6},{8,9},{9,8},{10,11... | collective-permute-start | bytes 1572872 | tf_op jit(solution)/shard_map/ppermute | solution.py:271
  65.8 6.4 %collective-permute-start.14 = (bf16[128,512]{1,0:T(8,128)(2,1)S(1)}, bf16[128,512]{1,0:T(8,128)(2,1)S(1)}, u32[]{:S(2)}, u32[]{:S(2)}) collective-permute-start(bf16[128,512]{1,0:T(8,128)(2,1)S(1)} %get-tuple-element.58), channel_id=1, source_target_pairs={{0,4},{4,0},{8,12},{12,8},{1,5},{5,1},{9,13},{13,9},{2,6},{6,2},{1... | collective-permute-start | bytes 393224 | tf_op jit(solution)/shard_map/ppermute | solution.py:275
  65.9 8.3 %collective-permute-start.13 = (bf16[128,512]{1,0:T(8,128)(2,1)S(1)}, bf16[128,512]{1,0:T(8,128)(2,1)S(1)}, u32[]{:S(2)}, u32[]{:S(2)}) collective-permute-start(bf16[128,512]{1,0:T(8,128)(2,1)S(1)} %get-tuple-element.56), channel_id=1, source_target_pairs={{0,4},{4,0},{8,12},{12,8},{1,5},{5,1},{9,13},{13,9},{2,6},{6,2},{1... | collective-permute-start | bytes 393224 | tf_op jit(solution)/shard_map/ppermute | solution.py:275
  67.9 12.0 %collective-permute-start.16 = (f32[128,512]{1,0:T(8,128)S(1)}, f32[128,512]{1,0:T(8,128)S(1)}, u32[]{:S(2)}, u32[]{:S(2)}) collective-permute-start(f32[128,512]{1,0:T(8,128)S(1)} %get-tuple-element.55.refs_0_), channel_id=1, source_target_pairs={{0,1},{1,0},{2,3},{3,2},{4,5},{5,4},{6,7},{7,6},{8,9},{9,8},{10,11... | collective-permute-start | bytes 786440 | tf_op jit(solution)/shard_map/ppermute | solution.py:271
  72.2 7.7 %collective-permute-start.15 = (bf16[128,512]{1,0:T(8,128)(2,1)S(1)}, bf16[128,512]{1,0:T(8,128)(2,1)S(1)}, u32[]{:S(2)}, u32[]{:S(2)}) collective-permute-start(bf16[128,512]{1,0:T(8,128)(2,1)S(1)} %add.6), channel_id=1, source_target_pairs={{0,8},{4,12},{8,0},{12,4},{1,9},{5,13},{9,1},{13,5},{2,10},{6,14},... | collective-permute-start | bytes 393224 | tf_op jit(solution)/shard_map/ppermute | solution.py:275
  74.2 5.7 %collective-permute-start.17 = (bf16[128,512]{1,0:T(8,128)(2,1)S(1)}, bf16[128,512]{1,0:T(8,128)(2,1)S(1)}, u32[]{:S(2)}, u32[]{:S(2)}) collective-permute-start(bf16[128,512]{1,0:T(8,128)(2,1)S(1)} %collective-permute-done.13.refs_1_), channel_id=1, source_target_pairs={{0,1},{1,0},{2,3},{3,2},{4,5},{5,4},{6,7},{7,6},{8,9},{9,8},{10,11... | collective-permute-start | bytes 393224 | tf_op jit(solution)/shard_map/ppermute | solution.py:271
  79.9 1.3 %collective-permute-start.18 = (bf16[128,512]{1,0:T(8,128)(2,1)S(1)}, bf16[128,512]{1,0:T(8,128)(2,1)S(1)}, u32[]{:S(2)}, u32[]{:S(2)}) collective-permute-start(bf16[128,512]{1,0:T(8,128)(2,1)S(1)} %collective-permute-done.15.refs_2_), channel_id=1, source_target_pairs={{0,1},{1,0},{2,3},{3,2},{4,5},{5,4},{6,7},{7,6},{8,9},{9,8},{10,11... | collective-permute-start | bytes 393224 | tf_op jit(solution)/shard_map/ppermute | solution.py:271

commit v5 on v4

--- a/solution.py
+++ b/solution.py
@@ -104,7 +104,7 @@
         pair_rows = take(row_count)
         own_parts, other_parts = take(3 if xor else 1), take(3 if xor else 1)
     else:
-        keys, values, att_before, gq_before, key_before, value_before = take(6)
+        keys, values, key_before, value_before = take(4)
     att_ref, gq_ref = take(2)
     if first:
         keys, values = (refs.pop(-2), refs.pop(-1)) if last else take(2)
@@ -166,16 +166,6 @@
     live_bf = live.astype(jnp.bfloat16)
     all_keys = keys[...]
     all_values = values[...]
-
-    def put(ref, value, head, placed):
-        if not xor:
-            ref[head] = value
-            return
-        for number, which in enumerate(placed):
-            for one in range(2):
-                start = number * high + one * band
-                at = pl.multiple_of((which ^ me) * band, 16)
-                ref[one, pl.ds(at, band), head * size : (head + 1) * size] = value[start : start + band, :]
 
     def rows_of(index):
         parts = []
@@ -215,23 +205,15 @@
         value_total = value_part if value_total is None else value_total + value_part
         for head in range(count):
             for ref, result in ((att_ref, attended), (gq_ref, grad_query)):
-                result = result[head * rows : (head + 1) * rows, :]
-                if last:
-                    put(ref, result, start + head, bands)
-                else:
-                    ref[start + head] = result
+                ref[start + head] = result[head * rows : (head + 1) * rows, :]
         start += count
     if not last:
         refs[0][...] = key_total
         refs[1][...] = value_total
         return
-    if not first:
-        for head in range(heads):
-            for ref, before in ((att_ref, att_before), (gq_ref, gq_before)):
-                put(ref, before[head], head, range(bands[0]))
     gk_ref, gv_ref, keep_ref, send_ref = refs
-    for ref, result in ((gk_ref, key_total[:, prompt:] * scale), (gv_ref, value_total[:, prompt:])):
-        put(ref, result.T.astype(jnp.bfloat16), 0, range(row_count))
+    gk_ref[...] = key_total[:, prompt:] * scale
+    gv_ref[...] = value_total[:, prompt:]
 
     def fill_sums(key_ref, value_ref):
         for number in range(row_count):
@@ -246,6 +228,29 @@
     @pl.when(core != 0)
     def _():
         fill_sums(send_ref, keep_ref)
+
+
+def place_kernel(band, high, *refs):
+    *parts, gk_part, gv_part, att_ref, gq_ref, gk_ref, gv_ref = refs
+    me = lax.axis_index("seq")
+    size = gk_part.shape[0]
+
+    def put(ref, value, column, which):
+        for one in range(2):
+            at = pl.multiple_of((which ^ me) * band, 16)
+            ref[one, pl.ds(at, band), column * size : (column + 1) * size] = value[one * band : (one + 1) * band, :]
+
+    for ref, pieces in ((att_ref, parts[0::2]), (gq_ref, parts[1::2])):
+        for head in range(pieces[0].shape[0]):
+            which = 0
+            for piece in pieces:
+                for start in range(0, piece.shape[1], high):
+                    put(ref, piece[head, start : start + high, :], head, which)
+                    which += 1
+    for ref, part in ((gk_ref, gk_part), (gv_ref, gv_part)):
+        rows = part[...].T.astype(jnp.bfloat16)
+        for which in range(rows.shape[0] // high):
+            put(ref, rows[which * high : (which + 1) * high, :], 0, which)
 
 
 def combine_kernel(keep_ref, received_ref, *outs):
@@ -312,6 +317,7 @@
             name="pack",
         )(*sources, prompt_keys, prompt_values)
         mine = spread(packed)
+        own_rows, wanted, mine[1] = lax.optimization_barrier((mine[0][:length], wanted, mine[1]))
         theirs = [swap_cores(piece) for piece in mine]
         row_counts = [count * high for count in counts] * (chips - 1) + [length + 2 * share]
         picked = pl.pallas_call(
@@ -322,7 +328,7 @@
             scratch_shapes=[pltpu.VMEM((2 * chips, len(tiles) * high, size), bf16)],
             compiler_params=SMALL,
             name="pick",
-        )(wanted, mine[0][:length], *mine[1:], *theirs)
+        )(wanted, own_rows, *mine[1:], *theirs)
         near = to_far(picked[6], 1)
         pair_rows = [picked[0], near, to_far(picked[2], 2), to_far(picked[4], 3)]
         head_rows = [picked[1], near, to_far(picked[3], 2), to_far(picked[5], 3)]
@@ -347,21 +353,20 @@
     high = rows // row_count
     every = prompt + rows
     f32 = jnp.float32
-    wide = (slots, seg_length, heads * size) if xor else (heads, rows, size)
-    narrow = (slots, seg_length, size) if xor else (1, rows, size)
+    wide, narrow = (slots, seg_length, heads * size), (slots, seg_length, size)
     parts = [(0, 1), (2, 3)] if xor else [(0,)]
-    carried = []
+    carried, placed = [], []
     for bands in parts:
         first, last = bands is parts[0], bands is parts[-1]
         operands = [head_rows[one] for one in bands]
         operands += [*pair_rows, *prompt_own, *prompt_other] if first else carried
         pair_shapes = [jax.ShapeDtypeStruct((every, size), bf16)] * 2
+        out_shape = [jax.ShapeDtypeStruct((heads, high * len(bands), size), bf16)] * 2
         if last:
-            out_shape = [jax.ShapeDtypeStruct(shape, bf16) for shape in (wide, wide, narrow, narrow)]
+            out_shape += [jax.ShapeDtypeStruct((size, rows), f32)] * 2
             out_shape += [jax.ShapeDtypeStruct((row_count, size, prompt // row_count), dtype) for dtype in (f32, bf16)]
         else:
-            out_shape = [jax.ShapeDtypeStruct((heads, high * len(bands), size), bf16)] * 2 + pair_shapes
-            out_shape += [jax.ShapeDtypeStruct((size, every), f32)] * 2
+            out_shape += pair_shapes + [jax.ShapeDtypeStruct((size, every), f32)] * 2
         count = heads * high * len(bands) * every
         results = pl.pallas_call(
             functools.partial(attend_kernel, band, heads, rows, bands, first, last, xor, row_count),
@@ -375,19 +380,27 @@
             ),
             name="attend",
         )(lengths, tree_mask, *operands)
-        if not last:
-            att_part, gq_part, keys, values, key_part, value_part = results
-            carried = [keys, values, att_part, gq_part, key_part, value_part]
-    attended, grad_queries, grad_keys, grad_values, keep, send = results
-    if not xor:
+        placed += results[:2]
+        carried = results[2:]
+    placed += carried[:2]
+    keep, send = carried[2:]
+    if xor:
+        outputs = pl.pallas_call(
+            functools.partial(place_kernel, band, high),
+            out_shape=[jax.ShapeDtypeStruct(shape, bf16) for shape in (wide, wide, narrow, narrow)],
+            in_specs=[VMEM] * len(placed),
+            out_specs=[VMEM] * 4,
+            compiler_params=SMALL,
+            name="place",
+        )(*placed)
+    else:
 
         def restore(value):
             value = value.reshape(-1, chips, slots, band, size).transpose(2, 1, 3, 0, 4)
             return value.reshape(slots, seg_length, -1)
 
-        attended, grad_queries, grad_keys, grad_values = (
-            restore(value) for value in (attended, grad_queries, grad_keys, grad_values)
-        )
+        outputs = [restore(value) for value in placed[:2]]
+        outputs += [restore(value.T.astype(bf16)[None]) for value in placed[2:]]
 
     received = swap_cores(send)
     if xor:
@@ -400,7 +413,7 @@
             compiler_params=SMALL,
             name="combine",
         )(keep, received)
-        passed = to_far(total[3], 1)
+        passed, *outputs = lax.optimization_barrier((to_far(total[3], 1), *outputs))
         across = pl.pallas_call(
             add_kernel,
             out_shape=jax.ShapeDtypeStruct(block, bf16),
@@ -425,7 +438,7 @@
         own = jnp.sum(arrived.astype(jnp.float32), axis=0).T
         other = swap_cores(own)
         prompt_grads = jnp.stack([jnp.where(core == 0, own, other), jnp.where(core == 0, other, own)])
-    return attended, grad_queries, grad_keys, grad_values, prompt_grads
+    return *outputs, prompt_grads
 
 
 def solution(mesh):

time: 82.4 us -> 81.5 us (0.989)
  waiting for transfers between devices: 44.8 us -> 43.8 us
    ppermute x11, waiting for transfers between devices: 41.3 us -> 39.2 us  [to_far(): lax.ppermute(value, 'seq', [(chip, chip ^ far) for chip in range(lax.axis...]
    ppermute x8, waiting for transfers between devices: 3.56 us -> 4.55 us  [swap_cores(): return lax.ppermute(value, 'rep', [(0, 1), (1, 0)])]
    pallas_call x2, Pallas kernels: 13.1 us -> 12.2 us  [per_device(): pl.pallas_call(functools.partial(attend_kernel, band, heads, rows, bands,...]
    pallas_call x0 -> x1, Pallas kernels: none -> 0.95 us  [per_device(): pl.pallas_call(functools.partial(place_kernel, band, high), out_shape=[ja...]
  transfers between devices with their start and end apart: 19 -> 19, of which waited for: 11 -> 11; matrix products, arithmetic and copies ran while one was open for 1% -> 2% of each run, Pallas kernels for 7% -> 9%
where the time goes in v5:
time: 81.5 us; the launch traced here: 81.3 us
  waiting for transfers between devices  43.8 us (54%)
  starting transfers between devices  18.1 us (22%)
  Pallas kernels  17.5 us (21%)
  local copies, waits for them, and re-layouts  1.24 us (2%)
    ppermute x11, waiting for transfers between devices, to_far(): lax.ppermute(value, 'seq', [(chip, chip ^ far) for chip in range(lax.axis...  39.2 us
    ppermute x11, starting transfers between devices, to_far(): lax.ppermute(value, 'seq', [(chip, chip ^ far) for chip in range(lax.axis...  17.5 us
    pallas_call x2, Pallas kernels, per_device(): pl.pallas_call(functools.partial(attend_kernel, band, heads, rows, bands,...  12.2 us
    ppermute x8, waiting for transfers between devices, swap_cores(): return lax.ppermute(value, 'rep', [(0, 1), (1, 0)])  4.55 us
    pallas_call x1, Pallas kernels, per_device(): pl.pallas_call(functools.partial(pack_kernel, band, tiles), out_shape=[ja...  2.36 us
  transfers between devices with their start and end apart: 19, of which 11 were waited for; matrix products, arithmetic and copies ran while one was open for 2% of the time, Pallas kernels for 9%

profile of v5, /device:TPU:0, one launch (start us, length us, event | category | flops | bytes accessed | tf_op | source)
XLA Modules:
  0.0 81.3 jit_solution(13039726165780737233)
XLA Ops:
  0.6 0.0 copy-start.3
  0.6 2.4 %pack.1 = (bf16[1280,128]{1,0:T(8,128)(2,1)}, bf16[1280,128]{1,0:T(8,128)(2,1)}, bf16[1280,128]{1,0:T(8,128)(2,1)}, bf16[768,128]{1,0:T(8,128)(2,1)}) custom-call(bf16[2,128,128]{2,1,0:T(8,128)(2,1)} %k_hbm.1, bf16[2,128,128]{2,1,0:T(8,128)(2,1)} %v_hbm.1, bf16[2,128,640]{2,1,0:T(8,128)(2,1)} %q_hbm.1, bf16[2,128,640]{2,1,0:T(8,128)(2,1)} %g_hbm.1, ...), custom_call_target="tpu_custom_call" | custom-call | tf_op jit(solution)/shard_map/pack/pallas_call | solution.py:310
  3.0 3.1 %collective-permute-start = (bf16[1280,128]{1,0:T(8,128)(2,1)}, bf16[1280,128]{1,0:T(8,128)(2,1)S(1)}, u32[]{:S(2)}, u32[]{:S(2)}) collective-permute-start(bf16[1280,128]{1,0:T(8,128)(2,1)} %get-tuple-element.45), channel_id=1, source_target_pairs={{0,4},{4,0},{8,12},{12,8},{1,5},{5,1},{9,13},{13,9},{2,6},{6,2},{1... | collective-permute-start | bytes 983048 | tf_op jit(solution)/shard_map/ppermute | solution.py:280
  6.1 2.6 %collective-permute-start.1 = (bf16[1280,128]{1,0:T(8,128)(2,1)}, bf16[1280,128]{1,0:T(8,128)(2,1)S(1)}, u32[]{:S(2)}, u32[]{:S(2)}) collective-permute-start(bf16[1280,128]{1,0:T(8,128)(2,1)} %get-tuple-element.49), channel_id=1, source_target_pairs={{0,8},{4,12},{8,0},{12,4},{1,9},{5,13},{9,1},{13,5},{2,10},{6,14},... | collective-permute-start | bytes 983048 | tf_op jit(solution)/shard_map/ppermute | solution.py:280
  8.7 0.0 collective-permute-start.2
  8.7 0.0 collective-permute-start.3
  8.7 0.9 %slice.3.refs_0_ = bf16[768,128]{1,0:T(8,128)(2,1)S(1)} slice(bf16[1280,128]{1,0:T(8,128)(2,1)} %get-tuple-element.44.refs_6_), slice={[0:768], [0:128]} | slice | bytes 393216 | tf_op jit(solution)/shard_map/slice | solution.py:320
  9.6 0.0 copy-start
  9.7 0.0 copy-start.1
  9.7 0.0 copy-start.2
  9.7 0.0 copy-done.3
  9.7 0.1 reshape.13
  9.8 0.1 copy.16
  9.9 10.4 %collective-permute-done.refs_1_.refs_7_ = bf16[1280,128]{1,0:T(8,128)(2,1)S(1)} collective-permute-done((bf16[1280,128]{1,0:T(8,128)(2,1)}, bf16[1280,128]{1,0:T(8,128)(2,1)S(1)}, u32[]{:S(2)}, u32[]{:S(2)}) %collective-permute-start) | collective-permute-done | bytes 327712 | tf_op jit(solution)/shard_map/ppermute | solution.py:280
  20.3 0.0 collective-permute-start.4
  20.3 8.8 %collective-permute-done.1.refs_2_.refs_8_ = bf16[1280,128]{1,0:T(8,128)(2,1)S(1)} collective-permute-done((bf16[1280,128]{1,0:T(8,128)(2,1)}, bf16[1280,128]{1,0:T(8,128)(2,1)S(1)}, u32[]{:S(2)}, u32[]{:S(2)}) %collective-permute-start.1) | collective-permute-done | bytes 327712 | tf_op jit(solution)/shard_map/ppermute | solution.py:280
  29.1 0.0 collective-permute-start.5
  29.1 0.0 collective-permute-done.2.refs_3_
  29.1 0.5 collective-permute-start.6
  29.6 0.1 copy.17.wanted_ref
  29.7 0.0 collective-permute-done.3.refs_4_.refs_9_
  29.7 1.3 %collective-permute-done.6.refs_7_ = bf16[768,128]{1,0:T(8,128)(2,1)S(1)} collective-permute-done((bf16[768,128]{1,0:T(8,128)(2,1)S(1)}, bf16[768,128]{1,0:T(8,128)(2,1)S(1)}, u32[]{:S(2)}, u32[]{:S(2)}) %collective-permute-start.6) | collective-permute-done | bytes 196640 | tf_op jit(solution)/shard_map/ppermute | solution.py:276
  31.0 0.0 collective-permute-done.4.refs_5_.refs_10_
  31.0 0.0 collective-permute-done.5.refs_6_.refs_11_
  31.0 0.9 %pick.1 = (bf16[128,128]{1,0:T(8,128)(2,1)S(1)}, bf16[640,128]{1,0:T(8,128)(2,1)S(1)}, bf16[128,128]{1,0:T(8,128)(2,1)S(1)}, bf16[640,128]{1,0:T(8,128)(2,1)S(1)...) custom-call(s32[4,2]{1,0:T(4,128)S(1)} %copy.17.wanted_ref, ...), custom_call_target="tpu_custom_call" | custom-call | tf_op jit(solution)/shard_map/pick/pallas_call | solution.py:323
  31.9 3.0 %collective-permute-start.9 = (bf16[1792,128]{1,0:T(8,128)(2,1)S(1)}, bf16[1792,128]{1,0:T(8,128)(2,1)S(1)}, u32[]{:S(2)}, u32[]{:S(2)}) collective-permute-start(bf16[1792,128]{1,0:T(8,128)(2,1)S(1)} %get-tuple-element.54), channel_id=1, source_target_pairs={{0,4},{4,0},{8,12},{12,8},{1,5},{5,1},{9,13},{13,9},{2,6},{6,2},{1... | collective-permute-start | bytes 1376264 | tf_op jit(solution)/shard_map/ppermute | solution.py:280
  34.8 1.1 %collective-permute-start.10 = (bf16[128,128]{1,0:T(8,128)(2,1)S(1)}, bf16[128,128]{1,0:T(8,128)(2,1)S(1)}, u32[]{:S(2)}, u32[]{:S(2)}) collective-permute-start(bf16[128,128]{1,0:T(8,128)(2,1)S(1)} %get-tuple-element.56), channel_id=1, source_target_pairs={{0,8},{4,12},{8,0},{12,4},{1,9},{5,13},{9,1},{13,5},{2,10},{6,14},... | collective-permute-start | bytes 98312 | tf_op jit(solution)/shard_map/ppermute | solution.py:280
  35.9 1.4 %collective-permute-start.11 = (bf16[128,128]{1,0:T(8,128)(2,1)S(1)}, bf16[128,128]{1,0:T(8,128)(2,1)S(1)}, u32[]{:S(2)}, u32[]{:S(2)}) collective-permute-start(bf16[128,128]{1,0:T(8,128)(2,1)S(1)} %get-tuple-element.57), channel_id=1, source_target_pairs={{0,12},{4,8},{8,4},{12,0},{1,13},{5,9},{9,5},{13,1},{2,14},{6,10},... | collective-permute-start | bytes 98312 | tf_op jit(solution)/shard_map/ppermute | solution.py:280
  37.3 2.0 %collective-permute-start.7 = (bf16[640,128]{1,0:T(8,128)(2,1)S(1)}, bf16[640,128]{1,0:T(8,128)(2,1)S(1)}, u32[]{:S(2)}, u32[]{:S(2)}) collective-permute-start(bf16[640,128]{1,0:T(8,128)(2,1)S(1)} %get-tuple-element.51), channel_id=1, source_target_pairs={{0,8},{4,12},{8,0},{12,4},{1,9},{5,13},{9,1},{13,5},{2,10},{6,14},... | collective-permute-start | bytes 491528 | tf_op jit(solution)/shard_map/ppermute | solution.py:280
  39.3 1.4 %collective-permute-start.8 = (bf16[640,128]{1,0:T(8,128)(2,1)S(1)}, bf16[640,128]{1,0:T(8,128)(2,1)S(1)}, u32[]{:S(2)}, u32[]{:S(2)}) collective-permute-start(bf16[640,128]{1,0:T(8,128)(2,1)S(1)} %get-tuple-element.52), channel_id=1, source_target_pairs={{0,12},{4,8},{8,4},{12,0},{1,13},{5,9},{9,5},{13,1},{2,14},{6,10},... | collective-permute-start | bytes 491528 | tf_op jit(solution)/shard_map/ppermute | solution.py:280
  40.7 5.7 %collective-permute-done.10.refs_4_ = bf16[128,128]{1,0:T(8,128)(2,1)S(1)} collective-permute-done((bf16[128,128]{1,0:T(8,128)(2,1)S(1)}, bf16[128,128]{1,0:T(8,128)(2,1)S(1)}, u32[]{:S(2)}, u32[]{:S(2)}) %collective-permute-start.10) | collective-permute-done | bytes 32800 | tf_op jit(solution)/shard_map/ppermute | solution.py:280
  46.4 3.6 %collective-permute-done.11.refs_5_ = bf16[128,128]{1,0:T(8,128)(2,1)S(1)} collective-permute-done((bf16[128,128]{1,0:T(8,128)(2,1)S(1)}, bf16[128,128]{1,0:T(8,128)(2,1)S(1)}, u32[]{:S(2)}, u32[]{:S(2)}) %collective-permute-start.11) | collective-permute-done | bytes 32800 | tf_op jit(solution)/shard_map/ppermute | solution.py:280
  50.0 0.5 collective-permute-done.9.refs_1_.refs_3_
  50.6 0.0 copy-done
  50.6 0.0 copy-done.1
  50.6 0.0 copy-done.2
  50.6 6.0 %attend.2 = (bf16[5,128,128]{2,1,0:T(8,128)(2,1)S(1)}, bf16[5,128,128]{2,1,0:T(8,128)(2,1)S(1)}, bf16[2304,128]{1,0:T(8,128)(2,1)S(1)}, bf16[2304,128]{1,0:T(8,1...) custom-call(s32[2]{0:T(128)S(1)} %copy-done.2, s32[2,2]{1,0:T(2,128)S(1)} %copy-done.1, ...), custom_call_target="tpu_custom_call" | custom-call | flops 4529848320 | bytes 1048576 | tf_op jit(solution)/shard_map/attend/pallas_call | solution.py:371
  56.6 0.0 collective-permute-done.7.refs_0_
  56.6 0.0 collective-permute-done.8.refs_1_
  56.6 6.1 %attend.3 = (bf16[5,128,128]{2,1,0:T(8,128)(2,1)S(1)}, bf16[5,128,128]{2,1,0:T(8,128)(2,1)S(1)}, f32[128,256]{1,0:T(8,128)S(1)}, f32[128,256]{1,0:T(8,128)S(1)},...) custom-call(s32[2]{0:T(128)S(1)} %copy-done.2, s32[2,2]{1,0:T(2,128)S(1)} %copy-done.1, ...), custom_call_target="tpu_custom_call" | custom-call | flops 4529848320 | bytes 1048576 | tf_op jit(solution)/shard_map/attend/pallas_call | solution.py:371
  62.8 0.1 collective-permute-start.12
  62.8 1.9 %collective-permute-done.12.received_ref = bf16[4,128,512]{2,1,0:T(8,128)(2,1)S(1)} collective-permute-done((bf16[4,128,512]{2,1,0:T(8,128)(2,1)S(1)}, bf16[4,128,512]{2,1,0:T(8,128)(2,1)S(1)}, u32[]{:S(2)}, u32[]{:S(2)}) %collective-permute-start.12) | collective-permute-done | bytes 524320 | tf_op jit(solution)/shard_map/ppermute | solution.py:276
  64.7 0.1 combine.1
  64.9 0.1 collective-permute-start.13
  64.9 0.9 %place.1 = (bf16[2,128,640]{2,1,0:T(8,128)(2,1)}, bf16[2,128,640]{2,1,0:T(8,128)(2,1)}, bf16[2,128,128]{2,1,0:T(8,128)(2,1)}, bf16[2,128,128]{2,1,0:T(8,128)(2,1)}) custom-call(bf16[5,128,128]{2,1,0:T(8,128)(2,1)S(1)} %get-tuple-element.65.refs_0_, bf16[5,128,128]{2,1,0:T(8,128)(2,1)S(1)} %get-tuple-element.66.refs_1_, ...), custom_call_target="tpu_custom_call" | custom-call | tf_op jit(solution)/shard_map/place/pallas_call | solution.py:388
  65.9 2.0 %collective-permute-start.14 = (bf16[128,512]{1,0:T(8,128)(2,1)S(1)}, bf16[128,512]{1,0:T(8,128)(2,1)S(1)}, u32[]{:S(2)}, u32[]{:S(2)}) collective-permute-start(bf16[128,512]{1,0:T(8,128)(2,1)S(1)} %get-tuple-element.80), channel_id=1, source_target_pairs={{0,4},{4,0},{8,12},{12,8},{1,5},{5,1},{9,13},{13,9},{2,6},{6,2},{1... | collective-permute-start | bytes 393224 | tf_op jit(solution)/shard_map/ppermute | solution.py:280
  67.9 0.0 collective-permute-start.16
  67.9 3.4 %collective-permute-done.13.passed_ref = bf16[128,512]{1,0:T(8,128)(2,1)S(1)} collective-permute-done((bf16[128,512]{1,0:T(8,128)(2,1)S(1)}, bf16[128,512]{1,0:T(8,128)(2,1)S(1)}, u32[]{:S(2)}, u32[]{:S(2)}) %collective-permute-start.13) | collective-permute-done | bytes 131104 | tf_op jit(solution)/shard_map/ppermute | solution.py:280
  71.3 0.9 %collective-permute-start.15 = (bf16[128,512]{1,0:T(8,128)(2,1)S(1)}, bf16[128,512]{1,0:T(8,128)(2,1)S(1)}, u32[]{:S(2)}, u32[]{:S(2)}) collective-permute-start(bf16[128,512]{1,0:T(8,128)(2,1)S(1)} %add.6), channel_id=1, source_target_pairs={{0,8},{4,12},{8,0},{12,4},{1,9},{5,13},{9,1},{13,5},{2,10},{6,14},... | collective-permute-start | bytes 393224 | tf_op jit(solution)/shard_map/ppermute | solution.py:280
  72.2 1.1 %collective-permute-done.14.refs_1_ = bf16[128,512]{1,0:T(8,128)(2,1)S(1)} collective-permute-done((bf16[128,512]{1,0:T(8,128)(2,1)S(1)}, bf16[128,512]{1,0:T(8,128)(2,1)S(1)}, u32[]{:S(2)}, u32[]{:S(2)}) %collective-permute-start.14) | collective-permute-done | bytes 131104 | tf_op jit(solution)/shard_map/ppermute | solution.py:280
  73.3 0.0 collective-permute-start.17
  73.3 5.7 %collective-permute-done.15.refs_2_ = bf16[128,512]{1,0:T(8,128)(2,1)S(1)} collective-permute-done((bf16[128,512]{1,0:T(8,128)(2,1)S(1)}, bf16[128,512]{1,0:T(8,128)(2,1)S(1)}, u32[]{:S(2)}, u32[]{:S(2)}) %collective-permute-start.15) | collective-permute-done | bytes 131104 | tf_op jit(solution)/shard_map/ppermute | solution.py:280
  79.0 0.0 collective-permute-start.18
  79.0 0.0 collective-permute-done.16.refs_3_
  79.0 0.0 collective-permute-done.17.refs_4_
  79.0 1.3 %collective-permute-done.18.refs_5_ = bf16[128,512]{1,0:T(8,128)(2,1)S(1)} collective-permute-done((bf16[128,512]{1,0:T(8,128)(2,1)S(1)}, bf16[128,512]{1,0:T(8,128)(2,1)S(1)}, u32[]{:S(2)}, u32[]{:S(2)}) %collective-permute-start.18) | collective-permute-done | bytes 131104 | tf_op jit(solution)/shard_map/ppermute | solution.py:276
  80.3 1.0 %finish.1 = f32[2,512,128]{2,1,0:T(8,128)} custom-call(f32[128,512]{1,0:T(8,128)S(1)} %get-tuple-element.79.refs_0_, bf16[128,512]{1,0:T(8,128)(2,1)S(1)} %collective-permute-done.14.refs_1_, bf16[128,512]{1,0:T(8,128)(2,1)S(1)} %collective-permute-done.15.refs_2_, f32[128,512]{1,0:T(8,128)S(1)} %collective-permute-done.16.refs_3_, ...), custom_call_target="tpu_custom_call" | custom-call | tf_op jit(solution)/shard_map/finish/pallas_call | solution.py:427
  (2 shorter events, 0.0 us)
Async XLA Ops:
  0.6 9.0 %copy-start.3 = (s32[16]{0:T(128)S(1)}, s32[16]{0:T(128)}, u32[]{:S(2)}) copy-start(s32[16]{0:T(128)} %param.15) | copy-start | bytes 196
  3.0 17.3 %collective-permute-start = (bf16[1280,128]{1,0:T(8,128)(2,1)}, bf16[1280,128]{1,0:T(8,128)(2,1)S(1)}, u32[]{:S(2)}, u32[]{:S(2)}) collective-permute-start(bf16[1280,128]{1,0:T(8,128)(2,1)} %get-tuple-element.45), channel_id=1, source_target_pairs={{0,4},{4,0},{8,12},{12,8},{1,5},{5,1},{9,13},{13,9},{2,6},{6,2},{1... | collective-permute-start | bytes 983048 | tf_op jit(solution)/shard_map/ppermute | solution.py:280
  6.1 23.0 %collective-permute-start.1 = (bf16[1280,128]{1,0:T(8,128)(2,1)}, bf16[1280,128]{1,0:T(8,128)(2,1)S(1)}, u32[]{:S(2)}, u32[]{:S(2)}) collective-permute-start(bf16[1280,128]{1,0:T(8,128)(2,1)} %get-tuple-element.49), channel_id=1, source_target_pairs={{0,8},{4,12},{8,0},{12,4},{1,9},{5,13},{9,1},{13,5},{2,10},{6,14},... | collective-permute-start | bytes 983048 | tf_op jit(solution)/shard_map/ppermute | solution.py:280
  8.7 20.4 %collective-permute-start.2 = (bf16[768,128]{1,0:T(8,128)(2,1)}, bf16[768,128]{1,0:T(8,128)(2,1)S(1)}, u32[]{:S(2)}, u32[]{:S(2)}) collective-permute-start(bf16[768,128]{1,0:T(8,128)(2,1)} %get-tuple-element.50), channel_id=1, source_target_pairs={{0,12},{4,8},{8,4},{12,0},{1,13},{5,9},{9,5},{13,1},{2,14},{6,10},... | collective-permute-start | bytes 589832 | tf_op jit(solution)/shard_map/ppermute | solution.py:280
  8.7 21.0 %collective-permute-start.3 = (bf16[1280,128]{1,0:T(8,128)(2,1)}, bf16[1280,128]{1,0:T(8,128)(2,1)S(1)}, u32[]{:S(2)}, u32[]{:S(2)}) collective-permute-start(bf16[1280,128]{1,0:T(8,128)(2,1)} %get-tuple-element.44.refs_6_), channel_id=1, source_target_pairs={{0,1},{1,0},{2,3},{3,2},{4,5},{5,4},{6,7},{7,6},{8,9},{9,8},{10,11... | collective-permute-start | bytes 983048 | tf_op jit(solution)/shard_map/ppermute | solution.py:276
  9.6 40.9 %copy-start = (bf16[1280,128]{1,0:T(8,128)(2,1)S(1)}, bf16[1280,128]{1,0:T(8,128)(2,1)}, u32[]{:S(2)}) copy-start(bf16[1280,128]{1,0:T(8,128)(2,1)} %get-tuple-element.44.refs_6_) | copy-start | bytes 983044
  9.7 40.9 %copy-start.1 = (s32[2,2]{1,0:T(2,128)S(1)}, s32[2,2]{1,0:T(2,128)}, u32[]{:S(2)}) copy-start(s32[2,2]{1,0:T(2,128)} %tree_ref.3) | copy-start | bytes 52
  9.7 40.9 %copy-start.2 = (s32[2]{0:T(128)S(1)}, s32[2]{0:T(128)}, u32[]{:S(2)}) copy-start(s32[2]{0:T(128)} %length_ref.3) | copy-start | bytes 28
  20.3 10.7 %collective-permute-start.4 = (bf16[1280,128]{1,0:T(8,128)(2,1)S(1)}, bf16[1280,128]{1,0:T(8,128)(2,1)S(1)}, u32[]{:S(2)}, u32[]{:S(2)}) collective-permute-start(bf16[1280,128]{1,0:T(8,128)(2,1)S(1)} %collective-permute-done.refs_1_.refs_7_), channel_id=1, source_target_pairs={{0,1},{1,0},{2,3},{3,2},{4,5},{5,4},{6,7},{7,6},{8,9},{9,8},{10,11... | collective-permute-start | bytes 983048 | tf_op jit(solution)/shard_map/ppermute | solution.py:276
  29.1 1.9 %collective-permute-start.5 = (bf16[1280,128]{1,0:T(8,128)(2,1)S(1)}, bf16[1280,128]{1,0:T(8,128)(2,1)S(1)}, u32[]{:S(2)}, u32[]{:S(2)}) collective-permute-start(bf16[1280,128]{1,0:T(8,128)(2,1)S(1)} %collective-permute-done.1.refs_2_.refs_8_), channel_id=1, source_target_pairs={{0,1},{1,0},{2,3},{3,2},{4,5},{5,4},{6,7},{7,6},{8,9},{9,8},{10,11... | collective-permute-start | bytes 983048 | tf_op jit(solution)/shard_map/ppermute | solution.py:276
  29.1 1.9 %collective-permute-start.6 = (bf16[768,128]{1,0:T(8,128)(2,1)S(1)}, bf16[768,128]{1,0:T(8,128)(2,1)S(1)}, u32[]{:S(2)}, u32[]{:S(2)}) collective-permute-start(bf16[768,128]{1,0:T(8,128)(2,1)S(1)} %collective-permute-done.2.refs_3_), channel_id=1, source_target_pairs={{0,1},{1,0},{2,3},{3,2},{4,5},{5,4},{6,7},{7,6},{8,9},{9,8},{10,11... | collective-permute-start | bytes 589832 | tf_op jit(solution)/shard_map/ppermute | solution.py:276
  31.9 18.7 %collective-permute-start.9 = (bf16[1792,128]{1,0:T(8,128)(2,1)S(1)}, bf16[1792,128]{1,0:T(8,128)(2,1)S(1)}, u32[]{:S(2)}, u32[]{:S(2)}) collective-permute-start(bf16[1792,128]{1,0:T(8,128)(2,1)S(1)} %get-tuple-element.54), channel_id=1, source_target_pairs={{0,4},{4,0},{8,12},{12,8},{1,5},{5,1},{9,13},{13,9},{2,6},{6,2},{1... | collective-permute-start | bytes 1376264 | tf_op jit(solution)/shard_map/ppermute | solution.py:280
  34.8 11.6 %collective-permute-start.10 = (bf16[128,128]{1,0:T(8,128)(2,1)S(1)}, bf16[128,128]{1,0:T(8,128)(2,1)S(1)}, u32[]{:S(2)}, u32[]{:S(2)}) collective-permute-start(bf16[128,128]{1,0:T(8,128)(2,1)S(1)} %get-tuple-element.56), channel_id=1, source_target_pairs={{0,8},{4,12},{8,0},{12,4},{1,9},{5,13},{9,1},{13,5},{2,10},{6,14},... | collective-permute-start | bytes 98312 | tf_op jit(solution)/shard_map/ppermute | solution.py:280
  35.9 14.1 %collective-permute-start.11 = (bf16[128,128]{1,0:T(8,128)(2,1)S(1)}, bf16[128,128]{1,0:T(8,128)(2,1)S(1)}, u32[]{:S(2)}, u32[]{:S(2)}) collective-permute-start(bf16[128,128]{1,0:T(8,128)(2,1)S(1)} %get-tuple-element.57), channel_id=1, source_target_pairs={{0,12},{4,8},{8,4},{12,0},{1,13},{5,9},{9,5},{13,1},{2,14},{6,10},... | collective-permute-start | bytes 98312 | tf_op jit(solution)/shard_map/ppermute | solution.py:280
  37.3 19.3 %collective-permute-start.7 = (bf16[640,128]{1,0:T(8,128)(2,1)S(1)}, bf16[640,128]{1,0:T(8,128)(2,1)S(1)}, u32[]{:S(2)}, u32[]{:S(2)}) collective-permute-start(bf16[640,128]{1,0:T(8,128)(2,1)S(1)} %get-tuple-element.51), channel_id=1, source_target_pairs={{0,8},{4,12},{8,0},{12,4},{1,9},{5,13},{9,1},{13,5},{2,10},{6,14},... | collective-permute-start | bytes 491528 | tf_op jit(solution)/shard_map/ppermute | solution.py:280
  39.3 17.3 %collective-permute-start.8 = (bf16[640,128]{1,0:T(8,128)(2,1)S(1)}, bf16[640,128]{1,0:T(8,128)(2,1)S(1)}, u32[]{:S(2)}, u32[]{:S(2)}) collective-permute-start(bf16[640,128]{1,0:T(8,128)(2,1)S(1)} %get-tuple-element.52), channel_id=1, source_target_pairs={{0,12},{4,8},{8,4},{12,0},{1,13},{5,9},{9,5},{13,1},{2,14},{6,10},... | collective-permute-start | bytes 491528 | tf_op jit(solution)/shard_map/ppermute | solution.py:280
  62.8 2.0 %collective-permute-start.12 = (bf16[4,128,512]{2,1,0:T(8,128)(2,1)S(1)}, bf16[4,128,512]{2,1,0:T(8,128)(2,1)S(1)}, u32[]{:S(2)}, u32[]{:S(2)}) collective-permute-start(bf16[4,128,512]{2,1,0:T(8,128)(2,1)S(1)} %get-tuple-element.63), channel_id=1, source_target_pairs={{0,1},{1,0},{2,3},{3,2},{4,5},{5,4},{6,7},{7,6},{8,9},{9,8},{10,11... | collective-permute-start | bytes 1572872 | tf_op jit(solution)/shard_map/ppermute | solution.py:276
  64.9 6.4 %collective-permute-start.13 = (bf16[128,512]{1,0:T(8,128)(2,1)S(1)}, bf16[128,512]{1,0:T(8,128)(2,1)S(1)}, u32[]{:S(2)}, u32[]{:S(2)}) collective-permute-start(bf16[128,512]{1,0:T(8,128)(2,1)S(1)} %get-tuple-element.64), channel_id=1, source_target_pairs={{0,4},{4,0},{8,12},{12,8},{1,5},{5,1},{9,13},{13,9},{2,6},{6,2},{1... | collective-permute-start | bytes 393224 | tf_op jit(solution)/shard_map/ppermute | solution.py:280
  65.9 7.4 %collective-permute-start.14 = (bf16[128,512]{1,0:T(8,128)(2,1)S(1)}, bf16[128,512]{1,0:T(8,128)(2,1)S(1)}, u32[]{:S(2)}, u32[]{:S(2)}) collective-permute-start(bf16[128,512]{1,0:T(8,128)(2,1)S(1)} %get-tuple-element.80), channel_id=1, source_target_pairs={{0,4},{4,0},{8,12},{12,8},{1,5},{5,1},{9,13},{13,9},{2,6},{6,2},{1... | collective-permute-start | bytes 393224 | tf_op jit(solution)/shard_map/ppermute | solution.py:280
  67.9 11.1 %collective-permute-start.16 = (f32[128,512]{1,0:T(8,128)S(1)}, f32[128,512]{1,0:T(8,128)S(1)}, u32[]{:S(2)}, u32[]{:S(2)}) collective-permute-start(f32[128,512]{1,0:T(8,128)S(1)} %get-tuple-element.79.refs_0_), channel_id=1, source_target_pairs={{0,1},{1,0},{2,3},{3,2},{4,5},{5,4},{6,7},{7,6},{8,9},{9,8},{10,11... | collective-permute-start | bytes 786440 | tf_op jit(solution)/shard_map/ppermute | solution.py:276
  71.3 7.7 %collective-permute-start.15 = (bf16[128,512]{1,0:T(8,128)(2,1)S(1)}, bf16[128,512]{1,0:T(8,128)(2,1)S(1)}, u32[]{:S(2)}, u32[]{:S(2)}) collective-permute-start(bf16[128,512]{1,0:T(8,128)(2,1)S(1)} %add.6), channel_id=1, source_target_pairs={{0,8},{4,12},{8,0},{12,4},{1,9},{5,13},{9,1},{13,5},{2,10},{6,14},... | collective-permute-start | bytes 393224 | tf_op jit(solution)/shard_map/ppermute | solution.py:280
  73.3 5.7 %collective-permute-start.17 = (bf16[128,512]{1,0:T(8,128)(2,1)S(1)}, bf16[128,512]{1,0:T(8,128)(2,1)S(1)}, u32[]{:S(2)}, u32[]{:S(2)}) collective-permute-start(bf16[128,512]{1,0:T(8,128)(2,1)S(1)} %collective-permute-done.14.refs_1_), channel_id=1, source_target_pairs={{0,1},{1,0},{2,3},{3,2},{4,5},{5,4},{6,7},{7,6},{8,9},{9,8},{10,11... | collective-permute-start | bytes 393224 | tf_op jit(solution)/shard_map/ppermute | solution.py:276
  79.0 1.3 %collective-permute-start.18 = (bf16[128,512]{1,0:T(8,128)(2,1)S(1)}, bf16[128,512]{1,0:T(8,128)(2,1)S(1)}, u32[]{:S(2)}, u32[]{:S(2)}) collective-permute-start(bf16[128,512]{1,0:T(8,128)(2,1)S(1)} %collective-permute-done.15.refs_2_), channel_id=1, source_target_pairs={{0,1},{1,0},{2,3},{3,2},{4,5},{5,4},{6,7},{7,6},{8,9},{9,8},{10,11... | collective-permute-start | bytes 393224 | tf_op jit(solution)/shard_map/ppermute | solution.py:276

commit v6 on v5

--- a/solution.py
+++ b/solution.py
@@ -23,14 +23,13 @@
     return lax.dot_general(left, right, dims, preferred_element_type=jnp.float32)
 
 
-def pack_kernel(band, tiles, k_hbm, v_hbm, q_hbm, g_hbm, pk_hbm, pv_hbm, *refs):
-    chips = len(refs) - 5
-    outs, held, sems = refs[:chips], refs[chips:-1], refs[-1]
+def pack_kernel(band, tiles, fars, k_hbm, v_hbm, q_hbm, g_hbm, pk_hbm, pv_hbm, *refs):
+    outs, held, sems = refs[: len(fars)], refs[len(fars) : -1], refs[-1]
     me = lax.axis_index("seq")
     core = lax.axis_index("rep")
     share, size = pk_hbm.shape
     rows = len(tiles) * 2 * band
-    targets = [out.at[pl.ds(rows, share), :] for out in outs[:3]]
+    targets = [out.at[pl.ds(rows, share), :] for far, out in zip(fars, outs) if far < 3]
     copies = [
         pltpu.make_async_copy(source, target, sems.at[number])
         for number, (source, target) in enumerate(zip((k_hbm, v_hbm, q_hbm, g_hbm), held))
@@ -39,7 +38,7 @@
         copy.start()
 
     def prompt_copies(source):
-        return [pltpu.make_async_copy(source, target, sems.at[4 + far]) for far, target in enumerate(targets)]
+        return [pltpu.make_async_copy(source, target, sems.at[4 + one]) for one, target in enumerate(targets)]
 
     @pl.when(core == 0)
     def _():
@@ -53,7 +52,7 @@
 
     for copy in copies:
         copy.wait()
-    for far, out in enumerate(outs):
+    for far, out in zip(fars, outs):
         start = pl.multiple_of((me ^ far) * band, 16)
         row = 0
         for source, tile in tiles:
@@ -258,10 +257,6 @@
         out[...] = (keep_ref[number] + received_ref[number].astype(jnp.float32)).astype(out.dtype)
 
 
-def add_kernel(part_ref, passed_ref, out_ref):
-    out_ref[...] = (part_ref[...] + passed_ref[...].astype(jnp.float32)).astype(out_ref.dtype)
-
-
 def finish_kernel(*refs):
     mine, theirs, out_ref = refs[: len(refs) // 2], refs[len(refs) // 2 : -1], refs[-1]
     core = lax.axis_index("rep")
@@ -307,15 +302,19 @@
         counts = [2, 2 * heads]
         high = slots * band
         length = len(tiles) * high
-        packed = pl.pallas_call(
-            functools.partial(pack_kernel, band, tiles),
-            out_shape=[jax.ShapeDtypeStruct((one, size), bf16) for one in [length + share] * 3 + [length] * (chips - 3)],
-            in_specs=[HBM] * 6,
-            out_specs=[VMEM] * chips,
-            scratch_shapes=[pltpu.VMEM(source.shape, bf16) for source in sources] + [pltpu.SemaphoreType.DMA((7,))],
-            compiler_params=FULL,
-            name="pack",
-        )(*sources, prompt_keys, prompt_values)
+        packed = {}
+        for fars in ((1, 2, 3), (0,)):
+            messages = pl.pallas_call(
+                functools.partial(pack_kernel, band, tiles, fars),
+                out_shape=[jax.ShapeDtypeStruct((length + share * (far < 3), size), bf16) for far in fars],
+                in_specs=[HBM] * 6,
+                out_specs=[VMEM] * len(fars),
+                scratch_shapes=[pltpu.VMEM(source.shape, bf16) for source in sources] + [pltpu.SemaphoreType.DMA((6,))],
+                compiler_params=FULL,
+                name="pack",
+            )(*sources, prompt_keys, prompt_values)
+            packed.update(zip(fars, messages))
+        packed = [packed[far] for far in range(chips)]
         mine = spread(packed)
         own_rows, wanted, mine[1] = lax.optimization_barrier((mine[0][:length], wanted, mine[1]))
         theirs = [swap_cores(piece) for piece in mine]
@@ -407,27 +406,19 @@
         block = (size, share)
         total = pl.pallas_call(
             combine_kernel,
-            out_shape=[jax.ShapeDtypeStruct(block, dtype) for dtype in (f32, bf16, f32, bf16)],
+            out_shape=[jax.ShapeDtypeStruct(block, dtype) for dtype in (f32, bf16, bf16, bf16)],
             in_specs=[VMEM] * 2,
             out_specs=[VMEM] * chips,
             compiler_params=SMALL,
             name="combine",
         )(keep, received)
-        passed, *outputs = lax.optimization_barrier((to_far(total[3], 1), *outputs))
-        across = pl.pallas_call(
-            add_kernel,
-            out_shape=jax.ShapeDtypeStruct(block, bf16),
-            in_specs=[VMEM] * 2,
-            out_specs=VMEM,
-            compiler_params=SMALL,
-            name="add",
-        )(total[2], passed)
-        arrived = [total[0], to_far(total[1], 1), to_far(across, 2)]
+        arrived = spread(total)
+        arrived[1], *outputs = lax.optimization_barrier((arrived[1], *outputs))
         swapped = [swap_cores(part) for part in arrived]
         prompt_grads = pl.pallas_call(
             finish_kernel,
             out_shape=jax.ShapeDtypeStruct((2, share, size), jnp.float32),
-            in_specs=[VMEM] * 6,
+            in_specs=[VMEM] * (2 * chips),
             out_specs=VMEM,
             compiler_params=SMALL,
             name="finish",

time: 81.5 us -> 80.4 us (0.987)
  waiting for transfers between devices: 43.8 us -> 38.9 us
  starting transfers between devices: 18.1 us -> 20.2 us
  Pallas kernels: 17.5 us -> 19.1 us
    ppermute x11, waiting for transfers between devices: 39.2 us -> 34.6 us  [to_far(): lax.ppermute(value, 'seq', [(chip, chip ^ far) for chip in range(lax.axis...]
    pallas_call x2, Pallas kernels: 2.38 us -> 4.15 us  [per_device(): pl.pallas_call(functools.partial(pack_kernel, band, tiles, fars), out_sha...]
    ppermute x11, starting transfers between devices: 17.5 us -> 19 us  [to_far(): lax.ppermute(value, 'seq', [(chip, chip ^ far) for chip in range(lax.axis...]
    ppermute x8 -> x9, waiting for transfers between devices: 4.55 us -> 4.22 us  [swap_cores(): return lax.ppermute(value, 'rep', [(0, 1), (1, 0)])]
  transfers between devices with their start and end apart: 19 -> 20, of which waited for: 11 -> 11; matrix products, arithmetic and copies ran while one was open for 2% -> 2% of each run, Pallas kernels for 9% -> 11%
where the time goes in v6:
time: 80.4 us; the launch traced here: 80.2 us
  waiting for transfers between devices  38.9 us (48%)
  starting transfers between devices  20.2 us (25%)
  Pallas kernels  19.1 us (24%)
  local copies, waits for them, and re-layouts  1.25 us (2%)
  between operations  0.81 us (1%)
    ppermute x11, waiting for transfers between devices, to_far(): lax.ppermute(value, 'seq', [(chip, chip ^ far) for chip in range(lax.axis...  34.6 us
    ppermute x11, starting transfers between devices, to_far(): lax.ppermute(value, 'seq', [(chip, chip ^ far) for chip in range(lax.axis...  19 us
    pallas_call x2, Pallas kernels, per_device(): pl.pallas_call(functools.partial(attend_kernel, band, heads, rows, bands,...  12.1 us
    ppermute x9, waiting for transfers between devices, swap_cores(): return lax.ppermute(value, 'rep', [(0, 1), (1, 0)])  4.22 us
    pallas_call x2, Pallas kernels, per_device(): pl.pallas_call(functools.partial(pack_kernel, band, tiles, fars), out_sha...  4.15 us
  transfers between devices with their start and end apart: 20, of which 11 were waited for; matrix products, arithmetic and copies ran while one was open for 2% of the time, Pallas kernels for 11%

profile of v6, /device:TPU:0, one launch (start us, length us, event | category | flops | bytes accessed | tf_op | source)
XLA Modules:
  0.0 80.2 jit_solution(9421444961024835212)
XLA Ops:
  0.6 0.0 copy-start.3
  0.6 2.2 %pack.3 = (bf16[1280,128]{1,0:T(8,128)(2,1)}, bf16[1280,128]{1,0:T(8,128)(2,1)}, bf16[768,128]{1,0:T(8,128)(2,1)}) custom-call(bf16[2,128,128]{2,1,0:T(8,128)(2,1)} %k_hbm.3, bf16[2,128,128]{2,1,0:T(8,128)(2,1)} %v_hbm.3, bf16[2,128,640]{2,1,0:T(8,128)(2,1)} %q_hbm.3, bf16[2,128,640]{2,1,0:T(8,128)(2,1)} %g_hbm.3, bf16[512,128]{1,0:T(8,128)(2,1)} %pk_hbm.3, ...), custom_call_target="tpu_custom_call" | custom-call | tf_op jit(solution)/shard_map/pack/pallas_call | solution.py:307
  2.8 0.0 copy-start.4
  2.9 3.1 %collective-permute-start = (bf16[1280,128]{1,0:T(8,128)(2,1)}, bf16[1280,128]{1,0:T(8,128)(2,1)S(1)}, u32[]{:S(2)}, u32[]{:S(2)}) collective-permute-start(bf16[1280,128]{1,0:T(8,128)(2,1)} %get-tuple-element.43), channel_id=1, source_target_pairs={{0,4},{4,0},{8,12},{12,8},{1,5},{5,1},{9,13},{13,9},{2,6},{6,2},{1... | collective-permute-start | bytes 983048 | tf_op jit(solution)/shard_map/ppermute | solution.py:275
  5.9 2.6 %collective-permute-start.1 = (bf16[1280,128]{1,0:T(8,128)(2,1)}, bf16[1280,128]{1,0:T(8,128)(2,1)S(1)}, u32[]{:S(2)}, u32[]{:S(2)}) collective-permute-start(bf16[1280,128]{1,0:T(8,128)(2,1)} %get-tuple-element.47), channel_id=1, source_target_pairs={{0,8},{4,12},{8,0},{12,4},{1,9},{5,13},{9,1},{13,5},{2,10},{6,14},... | collective-permute-start | bytes 983048 | tf_op jit(solution)/shard_map/ppermute | solution.py:275
  8.5 2.0 %pack.2.refs_6_ = bf16[1280,128]{1,0:T(8,128)(2,1)} custom-call(bf16[2,128,128]{2,1,0:T(8,128)(2,1)} %k_hbm.3, bf16[2,128,128]{2,1,0:T(8,128)(2,1)} %v_hbm.3, bf16[2,128,640]{2,1,0:T(8,128)(2,1)} %q_hbm.3, bf16[2,128,640]{2,1,0:T(8,128)(2,1)} %g_hbm.3, bf16[512,128]{1,0:T(8,128)(2,1)} %pk_hbm.3, bf16[512,128]{1,0:T(8,128)(2,1)} %pv_hbm.3), custom_call_target="tpu_custom_call" | custom-call | tf_op jit(solution)/shard_map/pack/pallas_call | solution.py:307
  10.5 0.1 collective-permute-start.3
  10.6 0.0 copy-done.4
  10.6 0.1 collective-permute-start.2
  10.7 0.9 %slice.4.refs_0_ = bf16[768,128]{1,0:T(8,128)(2,1)S(1)} slice(bf16[1280,128]{1,0:T(8,128)(2,1)} %pack.2.refs_6_), slice={[0:768], [0:128]} | slice | bytes 393216 | tf_op jit(solution)/shard_map/slice | solution.py:319
  11.6 0.0 copy-start
  11.6 0.0 copy-start.1
  11.6 0.0 copy-start.2
  11.7 0.0 copy-done.3
  11.7 0.1 reshape.13
  11.8 0.1 copy.16
  11.9 8.3 %collective-permute-done.refs_1_.refs_7_ = bf16[1280,128]{1,0:T(8,128)(2,1)S(1)} collective-permute-done((bf16[1280,128]{1,0:T(8,128)(2,1)}, bf16[1280,128]{1,0:T(8,128)(2,1)S(1)}, u32[]{:S(2)}, u32[]{:S(2)}) %collective-permute-start) | collective-permute-done | bytes 327712 | tf_op jit(solution)/shard_map/ppermute | solution.py:275
  20.1 0.0 collective-permute-start.4
  20.1 8.8 %collective-permute-done.1.refs_2_.refs_8_ = bf16[1280,128]{1,0:T(8,128)(2,1)S(1)} collective-permute-done((bf16[1280,128]{1,0:T(8,128)(2,1)}, bf16[1280,128]{1,0:T(8,128)(2,1)S(1)}, u32[]{:S(2)}, u32[]{:S(2)}) %collective-permute-start.1) | collective-permute-done | bytes 327712 | tf_op jit(solution)/shard_map/ppermute | solution.py:275
  28.9 0.0 collective-permute-start.5
  28.9 0.0 collective-permute-done.2.refs_3_
  28.9 0.5 collective-permute-start.6
  29.4 0.1 copy.17.wanted_ref
  29.5 0.0 collective-permute-done.3.refs_4_.refs_9_
  29.5 1.3 %collective-permute-done.6.refs_7_ = bf16[768,128]{1,0:T(8,128)(2,1)S(1)} collective-permute-done((bf16[768,128]{1,0:T(8,128)(2,1)S(1)}, bf16[768,128]{1,0:T(8,128)(2,1)S(1)}, u32[]{:S(2)}, u32[]{:S(2)}) %collective-permute-start.6) | collective-permute-done | bytes 196640 | tf_op jit(solution)/shard_map/ppermute | solution.py:271
  30.8 0.0 collective-permute-done.4.refs_5_.refs_10_
  30.8 0.0 collective-permute-done.5.refs_6_.refs_11_
  30.8 0.9 %pick.1 = (bf16[128,128]{1,0:T(8,128)(2,1)S(1)}, bf16[640,128]{1,0:T(8,128)(2,1)S(1)}, bf16[128,128]{1,0:T(8,128)(2,1)S(1)}, bf16[640,128]{1,0:T(8,128)(2,1)S(1)...) custom-call(s32[4,2]{1,0:T(4,128)S(1)} %copy.17.wanted_ref, ...), custom_call_target="tpu_custom_call" | custom-call | tf_op jit(solution)/shard_map/pick/pallas_call | solution.py:322
  31.7 3.0 %collective-permute-start.9 = (bf16[1792,128]{1,0:T(8,128)(2,1)S(1)}, bf16[1792,128]{1,0:T(8,128)(2,1)S(1)}, u32[]{:S(2)}, u32[]{:S(2)}) collective-permute-start(bf16[1792,128]{1,0:T(8,128)(2,1)S(1)} %get-tuple-element.52), channel_id=1, source_target_pairs={{0,4},{4,0},{8,12},{12,8},{1,5},{5,1},{9,13},{13,9},{2,6},{6,2},{1... | collective-permute-start | bytes 1376264 | tf_op jit(solution)/shard_map/ppermute | solution.py:275
  34.7 1.1 %collective-permute-start.10 = (bf16[128,128]{1,0:T(8,128)(2,1)S(1)}, bf16[128,128]{1,0:T(8,128)(2,1)S(1)}, u32[]{:S(2)}, u32[]{:S(2)}) collective-permute-start(bf16[128,128]{1,0:T(8,128)(2,1)S(1)} %get-tuple-element.54), channel_id=1, source_target_pairs={{0,8},{4,12},{8,0},{12,4},{1,9},{5,13},{9,1},{13,5},{2,10},{6,14},... | collective-permute-start | bytes 98312 | tf_op jit(solution)/shard_map/ppermute | solution.py:275
  35.8 1.4 %collective-permute-start.11 = (bf16[128,128]{1,0:T(8,128)(2,1)S(1)}, bf16[128,128]{1,0:T(8,128)(2,1)S(1)}, u32[]{:S(2)}, u32[]{:S(2)}) collective-permute-start(bf16[128,128]{1,0:T(8,128)(2,1)S(1)} %get-tuple-element.55), channel_id=1, source_target_pairs={{0,12},{4,8},{8,4},{12,0},{1,13},{5,9},{9,5},{13,1},{2,14},{6,10},... | collective-permute-start | bytes 98312 | tf_op jit(solution)/shard_map/ppermute | solution.py:275
  37.1 2.0 %collective-permute-start.7 = (bf16[640,128]{1,0:T(8,128)(2,1)S(1)}, bf16[640,128]{1,0:T(8,128)(2,1)S(1)}, u32[]{:S(2)}, u32[]{:S(2)}) collective-permute-start(bf16[640,128]{1,0:T(8,128)(2,1)S(1)} %get-tuple-element.49), channel_id=1, source_target_pairs={{0,8},{4,12},{8,0},{12,4},{1,9},{5,13},{9,1},{13,5},{2,10},{6,14},... | collective-permute-start | bytes 491528 | tf_op jit(solution)/shard_map/ppermute | solution.py:275
  39.2 1.4 %collective-permute-start.8 = (bf16[640,128]{1,0:T(8,128)(2,1)S(1)}, bf16[640,128]{1,0:T(8,128)(2,1)S(1)}, u32[]{:S(2)}, u32[]{:S(2)}) collective-permute-start(bf16[640,128]{1,0:T(8,128)(2,1)S(1)} %get-tuple-element.50), channel_id=1, source_target_pairs={{0,12},{4,8},{8,4},{12,0},{1,13},{5,9},{9,5},{13,1},{2,14},{6,10},... | collective-permute-start | bytes 491528 | tf_op jit(solution)/shard_map/ppermute | solution.py:275
  40.5 5.7 %collective-permute-done.10.refs_4_ = bf16[128,128]{1,0:T(8,128)(2,1)S(1)} collective-permute-done((bf16[128,128]{1,0:T(8,128)(2,1)S(1)}, bf16[128,128]{1,0:T(8,128)(2,1)S(1)}, u32[]{:S(2)}, u32[]{:S(2)}) %collective-permute-start.10) | collective-permute-done | bytes 32800 | tf_op jit(solution)/shard_map/ppermute | solution.py:275
  46.2 3.6 %collective-permute-done.11.refs_5_ = bf16[128,128]{1,0:T(8,128)(2,1)S(1)} collective-permute-done((bf16[128,128]{1,0:T(8,128)(2,1)S(1)}, bf16[128,128]{1,0:T(8,128)(2,1)S(1)}, u32[]{:S(2)}, u32[]{:S(2)}) %collective-permute-start.11) | collective-permute-done | bytes 32800 | tf_op jit(solution)/shard_map/ppermute | solution.py:275
  49.9 0.5 collective-permute-done.9.refs_1_.refs_3_
  50.4 0.0 copy-done
  50.4 0.0 copy-done.1
  50.4 0.0 copy-done.2
  50.4 6.0 %attend.2 = (bf16[5,128,128]{2,1,0:T(8,128)(2,1)S(1)}, bf16[5,128,128]{2,1,0:T(8,128)(2,1)S(1)}, bf16[2304,128]{1,0:T(8,128)(2,1)S(1)}, bf16[2304,128]{1,0:T(8,1...) custom-call(s32[2]{0:T(128)S(1)} %copy-done.2, s32[2,2]{1,0:T(2,128)S(1)} %copy-done.1, ...), custom_call_target="tpu_custom_call" | custom-call | flops 4529848320 | bytes 1048576 | tf_op jit(solution)/shard_map/attend/pallas_call | solution.py:370
  56.4 0.0 collective-permute-done.7.refs_0_
  56.4 0.0 collective-permute-done.8.refs_1_
  56.4 6.1 %attend.3 = (bf16[5,128,128]{2,1,0:T(8,128)(2,1)S(1)}, bf16[5,128,128]{2,1,0:T(8,128)(2,1)S(1)}, f32[128,256]{1,0:T(8,128)S(1)}, f32[128,256]{1,0:T(8,128)S(1)},...) custom-call(s32[2]{0:T(128)S(1)} %copy-done.2, s32[2,2]{1,0:T(2,128)S(1)} %copy-done.1, ...), custom_call_target="tpu_custom_call" | custom-call | flops 4529848320 | bytes 1048576 | tf_op jit(solution)/shard_map/attend/pallas_call | solution.py:370
  62.5 0.1 collective-permute-start.12
  62.6 1.9 %collective-permute-done.12.received_ref = bf16[4,128,512]{2,1,0:T(8,128)(2,1)S(1)} collective-permute-done((bf16[4,128,512]{2,1,0:T(8,128)(2,1)S(1)}, bf16[4,128,512]{2,1,0:T(8,128)(2,1)S(1)}, u32[]{:S(2)}, u32[]{:S(2)}) %collective-permute-start.12) | collective-permute-done | bytes 524320 | tf_op jit(solution)/shard_map/ppermute | solution.py:271
  64.5 0.1 combine.1
  64.6 0.1 collective-permute-start.13
  64.7 3.0 %collective-permute-start.14 = (bf16[128,512]{1,0:T(8,128)(2,1)S(1)}, bf16[128,512]{1,0:T(8,128)(2,1)S(1)}, u32[]{:S(2)}, u32[]{:S(2)}) collective-permute-start(bf16[128,512]{1,0:T(8,128)(2,1)S(1)} %get-tuple-element.79), channel_id=1, source_target_pairs={{0,8},{4,12},{8,0},{12,4},{1,9},{5,13},{9,1},{13,5},{2,10},{6,14},... | collective-permute-start | bytes 393224 | tf_op jit(solution)/shard_map/ppermute | solution.py:275
  67.7 0.0 collective-permute-start.16
  67.7 1.4 %collective-permute-start.15 = (bf16[128,512]{1,0:T(8,128)(2,1)S(1)}, bf16[128,512]{1,0:T(8,128)(2,1)S(1)}, u32[]{:S(2)}, u32[]{:S(2)}) collective-permute-start(bf16[128,512]{1,0:T(8,128)(2,1)S(1)} %get-tuple-element.80), channel_id=1, source_target_pairs={{0,12},{4,8},{8,4},{12,0},{1,13},{5,9},{9,5},{13,1},{2,14},{6,10},... | collective-permute-start | bytes 393224 | tf_op jit(solution)/shard_map/ppermute | solution.py:275
  69.0 0.9 %place.1 = (bf16[2,128,640]{2,1,0:T(8,128)(2,1)}, bf16[2,128,640]{2,1,0:T(8,128)(2,1)}, bf16[2,128,128]{2,1,0:T(8,128)(2,1)}, bf16[2,128,128]{2,1,0:T(8,128)(2,1)}) custom-call(bf16[5,128,128]{2,1,0:T(8,128)(2,1)S(1)} %get-tuple-element.63.refs_0_, bf16[5,128,128]{2,1,0:T(8,128)(2,1)S(1)} %get-tuple-element.64.refs_1_, ...), custom_call_target="tpu_custom_call" | custom-call | tf_op jit(solution)/shard_map/place/pallas_call | solution.py:387
  70.0 2.5 %collective-permute-done.13.refs_1_ = bf16[128,512]{1,0:T(8,128)(2,1)S(1)} collective-permute-done((bf16[128,512]{1,0:T(8,128)(2,1)S(1)}, bf16[128,512]{1,0:T(8,128)(2,1)S(1)}, u32[]{:S(2)}, u32[]{:S(2)}) %collective-permute-start.13) | collective-permute-done | bytes 131104 | tf_op jit(solution)/shard_map/ppermute | solution.py:275
  72.5 0.0 collective-permute-start.17
  72.5 5.2 %collective-permute-done.14.refs_2_ = bf16[128,512]{1,0:T(8,128)(2,1)S(1)} collective-permute-done((bf16[128,512]{1,0:T(8,128)(2,1)S(1)}, bf16[128,512]{1,0:T(8,128)(2,1)S(1)}, u32[]{:S(2)}, u32[]{:S(2)}) %collective-permute-start.14) | collective-permute-done | bytes 131104 | tf_op jit(solution)/shard_map/ppermute | solution.py:275
  77.7 0.0 collective-permute-start.18
  77.7 0.0 collective-permute-done.15.refs_3_
  77.7 0.5 collective-permute-start.19
  78.2 0.0 collective-permute-done.16.refs_4_
  78.2 0.0 collective-permute-done.17.refs_5_
  78.2 0.8 %collective-permute-done.18.refs_6_ = bf16[128,512]{1,0:T(8,128)(2,1)S(1)} collective-permute-done((bf16[128,512]{1,0:T(8,128)(2,1)S(1)}, bf16[128,512]{1,0:T(8,128)(2,1)S(1)}, u32[]{:S(2)}, u32[]{:S(2)}) %collective-permute-start.18) | collective-permute-done | bytes 131104 | tf_op jit(solution)/shard_map/ppermute | solution.py:271
  79.0 0.2 collective-permute-done.19.refs_7_
  79.2 1.0 %finish.1 = f32[2,512,128]{2,1,0:T(8,128)} custom-call(f32[128,512]{1,0:T(8,128)S(1)} %get-tuple-element.77.refs_0_, bf16[128,512]{1,0:T(8,128)(2,1)S(1)} %collective-permute-done.13.refs_1_, bf16[128,512]{1,0:T(8,128)(2,1)S(1)} %collective-permute-done.14.refs_2_, bf16[128,512]{1,0:T(8,128)(2,1)S(1)} %collective-permute-done.15.refs_3_, ...), custom_call_target="tpu_custom_call" | custom-call | tf_op jit(solution)/shard_map/finish/pallas_call | solution.py:418
  (1 shorter events, 0.0 us)
Async XLA Ops:
  0.6 11.0 %copy-start.3 = (s32[16]{0:T(128)S(1)}, s32[16]{0:T(128)}, u32[]{:S(2)}) copy-start(s32[16]{0:T(128)} %param.15) | copy-start | bytes 196
  2.8 7.7 %copy-start.4 = (bf16[768,128]{1,0:T(8,128)(2,1)S(1)}, bf16[768,128]{1,0:T(8,128)(2,1)}, u32[]{:S(2)}) copy-start(bf16[768,128]{1,0:T(8,128)(2,1)} %get-tuple-element.48) | copy-start | bytes 589828
  2.9 17.3 %collective-permute-start = (bf16[1280,128]{1,0:T(8,128)(2,1)}, bf16[1280,128]{1,0:T(8,128)(2,1)S(1)}, u32[]{:S(2)}, u32[]{:S(2)}) collective-permute-start(bf16[1280,128]{1,0:T(8,128)(2,1)} %get-tuple-element.43), channel_id=1, source_target_pairs={{0,4},{4,0},{8,12},{12,8},{1,5},{5,1},{9,13},{13,9},{2,6},{6,2},{1... | collective-permute-start | bytes 983048 | tf_op jit(solution)/shard_map/ppermute | solution.py:275
  5.9 23.0 %collective-permute-start.1 = (bf16[1280,128]{1,0:T(8,128)(2,1)}, bf16[1280,128]{1,0:T(8,128)(2,1)S(1)}, u32[]{:S(2)}, u32[]{:S(2)}) collective-permute-start(bf16[1280,128]{1,0:T(8,128)(2,1)} %get-tuple-element.47), channel_id=1, source_target_pairs={{0,8},{4,12},{8,0},{12,4},{1,9},{5,13},{9,1},{13,5},{2,10},{6,14},... | collective-permute-start | bytes 983048 | tf_op jit(solution)/shard_map/ppermute | solution.py:275
  10.5 19.0 %collective-permute-start.3 = (bf16[1280,128]{1,0:T(8,128)(2,1)}, bf16[1280,128]{1,0:T(8,128)(2,1)S(1)}, u32[]{:S(2)}, u32[]{:S(2)}) collective-permute-start(bf16[1280,128]{1,0:T(8,128)(2,1)} %pack.2.refs_6_), channel_id=1, source_target_pairs={{0,1},{1,0},{2,3},{3,2},{4,5},{5,4},{6,7},{7,6},{8,9},{9,8},{10,11... | collective-permute-start | bytes 983048 | tf_op jit(solution)/shard_map/ppermute | solution.py:271
  10.6 18.3 %collective-permute-start.2 = (bf16[768,128]{1,0:T(8,128)(2,1)S(1)}, bf16[768,128]{1,0:T(8,128)(2,1)S(1)}, u32[]{:S(2)}, u32[]{:S(2)}) collective-permute-start(bf16[768,128]{1,0:T(8,128)(2,1)S(1)} %copy-done.4), channel_id=1, source_target_pairs={{0,12},{4,8},{8,4},{12,0},{1,13},{5,9},{9,5},{13,1},{2,14},{6,10},... | collective-permute-start | bytes 589832 | tf_op jit(solution)/shard_map/ppermute | solution.py:275
  11.6 38.8 %copy-start = (bf16[1280,128]{1,0:T(8,128)(2,1)S(1)}, bf16[1280,128]{1,0:T(8,128)(2,1)}, u32[]{:S(2)}) copy-start(bf16[1280,128]{1,0:T(8,128)(2,1)} %pack.2.refs_6_) | copy-start | bytes 983044
  11.6 38.8 %copy-start.1 = (s32[2,2]{1,0:T(2,128)S(1)}, s32[2,2]{1,0:T(2,128)}, u32[]{:S(2)}) copy-start(s32[2,2]{1,0:T(2,128)} %tree_ref.3) | copy-start | bytes 52
  11.6 38.8 %copy-start.2 = (s32[2]{0:T(128)S(1)}, s32[2]{0:T(128)}, u32[]{:S(2)}) copy-start(s32[2]{0:T(128)} %length_ref.3) | copy-start | bytes 28
  20.1 10.7 %collective-permute-start.4 = (bf16[1280,128]{1,0:T(8,128)(2,1)S(1)}, bf16[1280,128]{1,0:T(8,128)(2,1)S(1)}, u32[]{:S(2)}, u32[]{:S(2)}) collective-permute-start(bf16[1280,128]{1,0:T(8,128)(2,1)S(1)} %collective-permute-done.refs_1_.refs_7_), channel_id=1, source_target_pairs={{0,1},{1,0},{2,3},{3,2},{4,5},{5,4},{6,7},{7,6},{8,9},{9,8},{10,11... | collective-permute-start | bytes 983048 | tf_op jit(solution)/shard_map/ppermute | solution.py:271
  28.9 1.9 %collective-permute-start.5 = (bf16[1280,128]{1,0:T(8,128)(2,1)S(1)}, bf16[1280,128]{1,0:T(8,128)(2,1)S(1)}, u32[]{:S(2)}, u32[]{:S(2)}) collective-permute-start(bf16[1280,128]{1,0:T(8,128)(2,1)S(1)} %collective-permute-done.1.refs_2_.refs_8_), channel_id=1, source_target_pairs={{0,1},{1,0},{2,3},{3,2},{4,5},{5,4},{6,7},{7,6},{8,9},{9,8},{10,11... | collective-permute-start | bytes 983048 | tf_op jit(solution)/shard_map/ppermute | solution.py:271
  28.9 1.9 %collective-permute-start.6 = (bf16[768,128]{1,0:T(8,128)(2,1)S(1)}, bf16[768,128]{1,0:T(8,128)(2,1)S(1)}, u32[]{:S(2)}, u32[]{:S(2)}) collective-permute-start(bf16[768,128]{1,0:T(8,128)(2,1)S(1)} %collective-permute-done.2.refs_3_), channel_id=1, source_target_pairs={{0,1},{1,0},{2,3},{3,2},{4,5},{5,4},{6,7},{7,6},{8,9},{9,8},{10,11... | collective-permute-start | bytes 589832 | tf_op jit(solution)/shard_map/ppermute | solution.py:271
  31.7 18.7 %collective-permute-start.9 = (bf16[1792,128]{1,0:T(8,128)(2,1)S(1)}, bf16[1792,128]{1,0:T(8,128)(2,1)S(1)}, u32[]{:S(2)}, u32[]{:S(2)}) collective-permute-start(bf16[1792,128]{1,0:T(8,128)(2,1)S(1)} %get-tuple-element.52), channel_id=1, source_target_pairs={{0,4},{4,0},{8,12},{12,8},{1,5},{5,1},{9,13},{13,9},{2,6},{6,2},{1... | collective-permute-start | bytes 1376264 | tf_op jit(solution)/shard_map/ppermute | solution.py:275
  34.7 11.6 %collective-permute-start.10 = (bf16[128,128]{1,0:T(8,128)(2,1)S(1)}, bf16[128,128]{1,0:T(8,128)(2,1)S(1)}, u32[]{:S(2)}, u32[]{:S(2)}) collective-permute-start(bf16[128,128]{1,0:T(8,128)(2,1)S(1)} %get-tuple-element.54), channel_id=1, source_target_pairs={{0,8},{4,12},{8,0},{12,4},{1,9},{5,13},{9,1},{13,5},{2,10},{6,14},... | collective-permute-start | bytes 98312 | tf_op jit(solution)/shard_map/ppermute | solution.py:275
  35.8 14.1 %collective-permute-start.11 = (bf16[128,128]{1,0:T(8,128)(2,1)S(1)}, bf16[128,128]{1,0:T(8,128)(2,1)S(1)}, u32[]{:S(2)}, u32[]{:S(2)}) collective-permute-start(bf16[128,128]{1,0:T(8,128)(2,1)S(1)} %get-tuple-element.55), channel_id=1, source_target_pairs={{0,12},{4,8},{8,4},{12,0},{1,13},{5,9},{9,5},{13,1},{2,14},{6,10},... | collective-permute-start | bytes 98312 | tf_op jit(solution)/shard_map/ppermute | solution.py:275
  37.1 19.3 %collective-permute-start.7 = (bf16[640,128]{1,0:T(8,128)(2,1)S(1)}, bf16[640,128]{1,0:T(8,128)(2,1)S(1)}, u32[]{:S(2)}, u32[]{:S(2)}) collective-permute-start(bf16[640,128]{1,0:T(8,128)(2,1)S(1)} %get-tuple-element.49), channel_id=1, source_target_pairs={{0,8},{4,12},{8,0},{12,4},{1,9},{5,13},{9,1},{13,5},{2,10},{6,14},... | collective-permute-start | bytes 491528 | tf_op jit(solution)/shard_map/ppermute | solution.py:275
  39.2 17.3 %collective-permute-start.8 = (bf16[640,128]{1,0:T(8,128)(2,1)S(1)}, bf16[640,128]{1,0:T(8,128)(2,1)S(1)}, u32[]{:S(2)}, u32[]{:S(2)}) collective-permute-start(bf16[640,128]{1,0:T(8,128)(2,1)S(1)} %get-tuple-element.50), channel_id=1, source_target_pairs={{0,12},{4,8},{8,4},{12,0},{1,13},{5,9},{9,5},{13,1},{2,14},{6,10},... | collective-permute-start | bytes 491528 | tf_op jit(solution)/shard_map/ppermute | solution.py:275
  62.5 2.0 %collective-permute-start.12 = (bf16[4,128,512]{2,1,0:T(8,128)(2,1)S(1)}, bf16[4,128,512]{2,1,0:T(8,128)(2,1)S(1)}, u32[]{:S(2)}, u32[]{:S(2)}) collective-permute-start(bf16[4,128,512]{2,1,0:T(8,128)(2,1)S(1)} %get-tuple-element.61), channel_id=1, source_target_pairs={{0,1},{1,0},{2,3},{3,2},{4,5},{5,4},{6,7},{7,6},{8,9},{9,8},{10,11... | collective-permute-start | bytes 1572872 | tf_op jit(solution)/shard_map/ppermute | solution.py:271
  64.6 7.9 %collective-permute-start.13 = (bf16[128,512]{1,0:T(8,128)(2,1)S(1)}, bf16[128,512]{1,0:T(8,128)(2,1)S(1)}, u32[]{:S(2)}, u32[]{:S(2)}) collective-permute-start(bf16[128,512]{1,0:T(8,128)(2,1)S(1)} %get-tuple-element.62), channel_id=1, source_target_pairs={{0,4},{4,0},{8,12},{12,8},{1,5},{5,1},{9,13},{13,9},{2,6},{6,2},{1... | collective-permute-start | bytes 393224 | tf_op jit(solution)/shard_map/ppermute | solution.py:275
  64.7 13.0 %collective-permute-start.14 = (bf16[128,512]{1,0:T(8,128)(2,1)S(1)}, bf16[128,512]{1,0:T(8,128)(2,1)S(1)}, u32[]{:S(2)}, u32[]{:S(2)}) collective-permute-start(bf16[128,512]{1,0:T(8,128)(2,1)S(1)} %get-tuple-element.79), channel_id=1, source_target_pairs={{0,8},{4,12},{8,0},{12,4},{1,9},{5,13},{9,1},{13,5},{2,10},{6,14},... | collective-permute-start | bytes 393224 | tf_op jit(solution)/shard_map/ppermute | solution.py:275
  67.7 10.5 %collective-permute-start.16 = (f32[128,512]{1,0:T(8,128)S(1)}, f32[128,512]{1,0:T(8,128)S(1)}, u32[]{:S(2)}, u32[]{:S(2)}) collective-permute-start(f32[128,512]{1,0:T(8,128)S(1)} %get-tuple-element.77.refs_0_), channel_id=1, source_target_pairs={{0,1},{1,0},{2,3},{3,2},{4,5},{5,4},{6,7},{7,6},{8,9},{9,8},{10,11... | collective-permute-start | bytes 786440 | tf_op jit(solution)/shard_map/ppermute | solution.py:271
  67.7 10.0 %collective-permute-start.15 = (bf16[128,512]{1,0:T(8,128)(2,1)S(1)}, bf16[128,512]{1,0:T(8,128)(2,1)S(1)}, u32[]{:S(2)}, u32[]{:S(2)}) collective-permute-start(bf16[128,512]{1,0:T(8,128)(2,1)S(1)} %get-tuple-element.80), channel_id=1, source_target_pairs={{0,12},{4,8},{8,4},{12,0},{1,13},{5,9},{9,5},{13,1},{2,14},{6,10},... | collective-permute-start | bytes 393224 | tf_op jit(solution)/shard_map/ppermute | solution.py:275
  72.5 5.7 %collective-permute-start.17 = (bf16[128,512]{1,0:T(8,128)(2,1)S(1)}, bf16[128,512]{1,0:T(8,128)(2,1)S(1)}, u32[]{:S(2)}, u32[]{:S(2)}) collective-permute-start(bf16[128,512]{1,0:T(8,128)(2,1)S(1)} %collective-permute-done.13.refs_1_), channel_id=1, source_target_pairs={{0,1},{1,0},{2,3},{3,2},{4,5},{5,4},{6,7},{7,6},{8,9},{9,8},{10,11... | collective-permute-start | bytes 393224 | tf_op jit(solution)/shard_map/ppermute | solution.py:271
  77.7 1.3 %collective-permute-start.18 = (bf16[128,512]{1,0:T(8,128)(2,1)S(1)}, bf16[128,512]{1,0:T(8,128)(2,1)S(1)}, u32[]{:S(2)}, u32[]{:S(2)}) collective-permute-start(bf16[128,512]{1,0:T(8,128)(2,1)S(1)} %collective-permute-done.14.refs_2_), channel_id=1, source_target_pairs={{0,1},{1,0},{2,3},{3,2},{4,5},{5,4},{6,7},{7,6},{8,9},{9,8},{10,11... | collective-permute-start | bytes 393224 | tf_op jit(solution)/shard_map/ppermute | solution.py:271
  77.7 1.5 %collective-permute-start.19 = (bf16[128,512]{1,0:T(8,128)(2,1)S(1)}, bf16[128,512]{1,0:T(8,128)(2,1)S(1)}, u32[]{:S(2)}, u32[]{:S(2)}) collective-permute-start(bf16[128,512]{1,0:T(8,128)(2,1)S(1)} %collective-permute-done.15.refs_3_), channel_id=1, source_target_pairs={{0,1},{1,0},{2,3},{3,2},{4,5},{5,4},{6,7},{7,6},{8,9},{9,8},{10,11... | collective-permute-start | bytes 393224 | tf_op jit(solution)/shard_map/ppermute | solution.py:271

commit v7 on v6

--- a/solution.py
+++ b/solution.py
@@ -257,14 +257,18 @@
         out[...] = (keep_ref[number] + received_ref[number].astype(jnp.float32)).astype(out.dtype)
 
 
-def finish_kernel(*refs):
-    mine, theirs, out_ref = refs[: len(refs) // 2], refs[len(refs) // 2 : -1], refs[-1]
+def finish_kernel(other, *refs):
+    *parts, out_hbm, held, sem = refs
     core = lax.axis_index("rep")
-    for parts, place in ((mine, core), (theirs, 1 - core)):
-        total = parts[0][...]
-        for part in parts[1:]:
-            total = total + part[...].astype(jnp.float32)
-        out_ref[place] = total.T
+    if other:
+        parts = parts[1:]
+    total = parts[0][...]
+    for part in parts[1:]:
+        total = total + part[...].astype(jnp.float32)
+    held[...] = total.T
+    copy = pltpu.make_async_copy(held, out_hbm.at[1 - core if other else core], sem)
+    copy.start()
+    copy.wait()
 
 
 def swap_cores(value):
@@ -415,14 +419,18 @@
         arrived = spread(total)
         arrived[1], *outputs = lax.optimization_barrier((arrived[1], *outputs))
         swapped = [swap_cores(part) for part in arrived]
-        prompt_grads = pl.pallas_call(
-            finish_kernel,
-            out_shape=jax.ShapeDtypeStruct((2, share, size), jnp.float32),
-            in_specs=[VMEM] * (2 * chips),
-            out_specs=VMEM,
-            compiler_params=SMALL,
-            name="finish",
-        )(*arrived, *swapped)
+        prompt_grads = ()
+        for other, parts in enumerate((arrived, swapped)):
+            prompt_grads = pl.pallas_call(
+                functools.partial(finish_kernel, other),
+                out_shape=jax.ShapeDtypeStruct((2, share, size), jnp.float32),
+                in_specs=[HBM] * other + [VMEM] * chips,
+                out_specs=HBM,
+                scratch_shapes=[pltpu.VMEM((share, size), jnp.float32), pltpu.SemaphoreType.DMA],
+                input_output_aliases={0: 0} if other else {},
+                compiler_params=SMALL,
+                name="finish",
+            )(*([prompt_grads] if other else []), *parts)
     else:
         total = (keep + received.astype(jnp.float32)).reshape(size, chips, share).transpose(1, 0, 2).astype(bf16)
         arrived = lax.all_to_all(total, "seq", split_axis=0, concat_axis=0)

time: 80.4 us -> 80.2 us (level)
  waiting for transfers between devices: 38.9 us -> 38 us
    ppermute x9, waiting for transfers between devices: 4.22 us -> 3.35 us  [swap_cores(): return lax.ppermute(value, 'rep', [(0, 1), (1, 0)])]
    pallas_call x1 -> x2, Pallas kernels: 1 us -> 1.7 us  [per_device(): pl.pallas_call(functools.partial(finish_kernel, other), out_shape=jax.Sha...]
  transfers between devices with their start and end apart: 20 -> 20, of which waited for: 11 -> 10; matrix products, arithmetic and copies ran while one was open for 2% -> 2% of each run, Pallas kernels for 11% -> 12%
where the time goes in v7:
time: 80.2 us; the launch traced here: 80 us
  waiting for transfers between devices  38 us (47%)
  starting transfers between devices  20.2 us (25%)
  Pallas kernels  19.8 us (25%)
  local copies, waits for them, and re-layouts  1.25 us (2%)
  between operations  0.84 us (1%)
    ppermute x11, waiting for transfers between devices, to_far(): lax.ppermute(value, 'seq', [(chip, chip ^ far) for chip in range(lax.axis...  34.6 us
    ppermute x11, starting transfers between devices, to_far(): lax.ppermute(value, 'seq', [(chip, chip ^ far) for chip in range(lax.axis...  19 us
    pallas_call x2, Pallas kernels, per_device(): pl.pallas_call(functools.partial(attend_kernel, band, heads, rows, bands,...  12.1 us
    pallas_call x2, Pallas kernels, per_device(): pl.pallas_call(functools.partial(pack_kernel, band, tiles, fars), out_sha...  4.15 us
    ppermute x9, waiting for transfers between devices, swap_cores(): return lax.ppermute(value, 'rep', [(0, 1), (1, 0)])  3.35 us
    pallas_call x2, Pallas kernels, per_device(): pl.pallas_call(functools.partial(finish_kernel, other), out_shape=jax.Sha...  1.7 us
  transfers between devices with their start and end apart: 20, of which 10 were waited for; matrix products, arithmetic and copies ran while one was open for 2% of the time, Pallas kernels for 12%

profile of v7, /device:TPU:0, one launch (start us, length us, event | category | flops | bytes accessed | tf_op | source)
XLA Modules:
  0.0 80.0 jit_solution(15242025476550465876)
XLA Ops:
  0.6 0.0 copy-start.3
  0.6 2.2 %pack.3 = (bf16[1280,128]{1,0:T(8,128)(2,1)}, bf16[1280,128]{1,0:T(8,128)(2,1)}, bf16[768,128]{1,0:T(8,128)(2,1)}) custom-call(bf16[2,128,128]{2,1,0:T(8,128)(2,1)} %k_hbm.3, bf16[2,128,128]{2,1,0:T(8,128)(2,1)} %v_hbm.3, bf16[2,128,640]{2,1,0:T(8,128)(2,1)} %q_hbm.3, bf16[2,128,640]{2,1,0:T(8,128)(2,1)} %g_hbm.3, bf16[512,128]{1,0:T(8,128)(2,1)} %pk_hbm.3, ...), custom_call_target="tpu_custom_call" | custom-call | tf_op jit(solution)/shard_map/pack/pallas_call | solution.py:311
  2.8 0.0 copy-start.4
  2.9 3.1 %collective-permute-start = (bf16[1280,128]{1,0:T(8,128)(2,1)}, bf16[1280,128]{1,0:T(8,128)(2,1)S(1)}, u32[]{:S(2)}, u32[]{:S(2)}) collective-permute-start(bf16[1280,128]{1,0:T(8,128)(2,1)} %get-tuple-element.43), channel_id=1, source_target_pairs={{0,4},{4,0},{8,12},{12,8},{1,5},{5,1},{9,13},{13,9},{2,6},{6,2},{1... | collective-permute-start | bytes 983048 | tf_op jit(solution)/shard_map/ppermute | solution.py:279
  5.9 2.6 %collective-permute-start.1 = (bf16[1280,128]{1,0:T(8,128)(2,1)}, bf16[1280,128]{1,0:T(8,128)(2,1)S(1)}, u32[]{:S(2)}, u32[]{:S(2)}) collective-permute-start(bf16[1280,128]{1,0:T(8,128)(2,1)} %get-tuple-element.47), channel_id=1, source_target_pairs={{0,8},{4,12},{8,0},{12,4},{1,9},{5,13},{9,1},{13,5},{2,10},{6,14},... | collective-permute-start | bytes 983048 | tf_op jit(solution)/shard_map/ppermute | solution.py:279
  8.5 2.0 %pack.2.refs_6_ = bf16[1280,128]{1,0:T(8,128)(2,1)} custom-call(bf16[2,128,128]{2,1,0:T(8,128)(2,1)} %k_hbm.3, bf16[2,128,128]{2,1,0:T(8,128)(2,1)} %v_hbm.3, bf16[2,128,640]{2,1,0:T(8,128)(2,1)} %q_hbm.3, bf16[2,128,640]{2,1,0:T(8,128)(2,1)} %g_hbm.3, bf16[512,128]{1,0:T(8,128)(2,1)} %pk_hbm.3, bf16[512,128]{1,0:T(8,128)(2,1)} %pv_hbm.3), custom_call_target="tpu_custom_call" | custom-call | tf_op jit(solution)/shard_map/pack/pallas_call | solution.py:311
  10.5 0.1 collective-permute-start.3
  10.6 0.0 copy-done.4
  10.6 0.1 collective-permute-start.2
  10.7 0.9 %slice.4.refs_0_ = bf16[768,128]{1,0:T(8,128)(2,1)S(1)} slice(bf16[1280,128]{1,0:T(8,128)(2,1)} %pack.2.refs_6_), slice={[0:768], [0:128]} | slice | bytes 393216 | tf_op jit(solution)/shard_map/slice | solution.py:323
  11.6 0.0 copy-start
  11.6 0.0 copy-start.1
  11.6 0.0 copy-start.2
  11.7 0.0 copy-done.3
  11.7 0.1 reshape.13
  11.8 0.1 copy.17
  11.9 8.3 %collective-permute-done.refs_1_.refs_7_ = bf16[1280,128]{1,0:T(8,128)(2,1)S(1)} collective-permute-done((bf16[1280,128]{1,0:T(8,128)(2,1)}, bf16[1280,128]{1,0:T(8,128)(2,1)S(1)}, u32[]{:S(2)}, u32[]{:S(2)}) %collective-permute-start) | collective-permute-done | bytes 327712 | tf_op jit(solution)/shard_map/ppermute | solution.py:279
  20.1 0.0 collective-permute-start.4
  20.1 8.8 %collective-permute-done.1.refs_2_.refs_8_ = bf16[1280,128]{1,0:T(8,128)(2,1)S(1)} collective-permute-done((bf16[1280,128]{1,0:T(8,128)(2,1)}, bf16[1280,128]{1,0:T(8,128)(2,1)S(1)}, u32[]{:S(2)}, u32[]{:S(2)}) %collective-permute-start.1) | collective-permute-done | bytes 327712 | tf_op jit(solution)/shard_map/ppermute | solution.py:279
  28.9 0.0 collective-permute-start.5
  28.9 0.0 collective-permute-done.2.refs_3_
  28.9 0.5 collective-permute-start.6
  29.4 0.1 copy.18.wanted_ref
  29.5 0.0 collective-permute-done.3.refs_4_.refs_9_
  29.5 1.3 %collective-permute-done.6.refs_7_ = bf16[768,128]{1,0:T(8,128)(2,1)S(1)} collective-permute-done((bf16[768,128]{1,0:T(8,128)(2,1)S(1)}, bf16[768,128]{1,0:T(8,128)(2,1)S(1)}, u32[]{:S(2)}, u32[]{:S(2)}) %collective-permute-start.6) | collective-permute-done | bytes 196640 | tf_op jit(solution)/shard_map/ppermute | solution.py:275
  30.8 0.0 collective-permute-done.4.refs_5_.refs_10_
  30.8 0.0 collective-permute-done.5.refs_6_.refs_11_
  30.8 0.9 %pick.1 = (bf16[128,128]{1,0:T(8,128)(2,1)S(1)}, bf16[640,128]{1,0:T(8,128)(2,1)S(1)}, bf16[128,128]{1,0:T(8,128)(2,1)S(1)}, bf16[640,128]{1,0:T(8,128)(2,1)S(1)...) custom-call(s32[4,2]{1,0:T(4,128)S(1)} %copy.18.wanted_ref, ...), custom_call_target="tpu_custom_call" | custom-call | tf_op jit(solution)/shard_map/pick/pallas_call | solution.py:326
  31.7 3.0 %collective-permute-start.9 = (bf16[1792,128]{1,0:T(8,128)(2,1)S(1)}, bf16[1792,128]{1,0:T(8,128)(2,1)S(1)}, u32[]{:S(2)}, u32[]{:S(2)}) collective-permute-start(bf16[1792,128]{1,0:T(8,128)(2,1)S(1)} %get-tuple-element.52), channel_id=1, source_target_pairs={{0,4},{4,0},{8,12},{12,8},{1,5},{5,1},{9,13},{13,9},{2,6},{6,2},{1... | collective-permute-start | bytes 1376264 | tf_op jit(solution)/shard_map/ppermute | solution.py:279
  34.7 1.1 %collective-permute-start.10 = (bf16[128,128]{1,0:T(8,128)(2,1)S(1)}, bf16[128,128]{1,0:T(8,128)(2,1)S(1)}, u32[]{:S(2)}, u32[]{:S(2)}) collective-permute-start(bf16[128,128]{1,0:T(8,128)(2,1)S(1)} %get-tuple-element.54), channel_id=1, source_target_pairs={{0,8},{4,12},{8,0},{12,4},{1,9},{5,13},{9,1},{13,5},{2,10},{6,14},... | collective-permute-start | bytes 98312 | tf_op jit(solution)/shard_map/ppermute | solution.py:279
  35.8 1.4 %collective-permute-start.11 = (bf16[128,128]{1,0:T(8,128)(2,1)S(1)}, bf16[128,128]{1,0:T(8,128)(2,1)S(1)}, u32[]{:S(2)}, u32[]{:S(2)}) collective-permute-start(bf16[128,128]{1,0:T(8,128)(2,1)S(1)} %get-tuple-element.55), channel_id=1, source_target_pairs={{0,12},{4,8},{8,4},{12,0},{1,13},{5,9},{9,5},{13,1},{2,14},{6,10},... | collective-permute-start | bytes 98312 | tf_op jit(solution)/shard_map/ppermute | solution.py:279
  37.1 2.0 %collective-permute-start.7 = (bf16[640,128]{1,0:T(8,128)(2,1)S(1)}, bf16[640,128]{1,0:T(8,128)(2,1)S(1)}, u32[]{:S(2)}, u32[]{:S(2)}) collective-permute-start(bf16[640,128]{1,0:T(8,128)(2,1)S(1)} %get-tuple-element.49), channel_id=1, source_target_pairs={{0,8},{4,12},{8,0},{12,4},{1,9},{5,13},{9,1},{13,5},{2,10},{6,14},... | collective-permute-start | bytes 491528 | tf_op jit(solution)/shard_map/ppermute | solution.py:279
  39.2 1.4 %collective-permute-start.8 = (bf16[640,128]{1,0:T(8,128)(2,1)S(1)}, bf16[640,128]{1,0:T(8,128)(2,1)S(1)}, u32[]{:S(2)}, u32[]{:S(2)}) collective-permute-start(bf16[640,128]{1,0:T(8,128)(2,1)S(1)} %get-tuple-element.50), channel_id=1, source_target_pairs={{0,12},{4,8},{8,4},{12,0},{1,13},{5,9},{9,5},{13,1},{2,14},{6,10},... | collective-permute-start | bytes 491528 | tf_op jit(solution)/shard_map/ppermute | solution.py:279
  40.5 5.7 %collective-permute-done.10.refs_4_ = bf16[128,128]{1,0:T(8,128)(2,1)S(1)} collective-permute-done((bf16[128,128]{1,0:T(8,128)(2,1)S(1)}, bf16[128,128]{1,0:T(8,128)(2,1)S(1)}, u32[]{:S(2)}, u32[]{:S(2)}) %collective-permute-start.10) | collective-permute-done | bytes 32800 | tf_op jit(solution)/shard_map/ppermute | solution.py:279
  46.2 3.6 %collective-permute-done.11.refs_5_ = bf16[128,128]{1,0:T(8,128)(2,1)S(1)} collective-permute-done((bf16[128,128]{1,0:T(8,128)(2,1)S(1)}, bf16[128,128]{1,0:T(8,128)(2,1)S(1)}, u32[]{:S(2)}, u32[]{:S(2)}) %collective-permute-start.11) | collective-permute-done | bytes 32800 | tf_op jit(solution)/shard_map/ppermute | solution.py:279
  49.9 0.5 collective-permute-done.9.refs_1_.refs_3_
  50.4 0.0 copy-done
  50.4 0.0 copy-done.1
  50.4 0.0 copy-done.2
  50.4 6.0 %attend.2 = (bf16[5,128,128]{2,1,0:T(8,128)(2,1)S(1)}, bf16[5,128,128]{2,1,0:T(8,128)(2,1)S(1)}, bf16[2304,128]{1,0:T(8,128)(2,1)S(1)}, bf16[2304,128]{1,0:T(8,1...) custom-call(s32[2]{0:T(128)S(1)} %copy-done.2, s32[2,2]{1,0:T(2,128)S(1)} %copy-done.1, ...), custom_call_target="tpu_custom_call" | custom-call | flops 4529848320 | bytes 1048576 | tf_op jit(solution)/shard_map/attend/pallas_call | solution.py:374
  56.4 0.0 collective-permute-done.7.refs_0_
  56.4 0.0 collective-permute-done.8.refs_1_
  56.4 6.1 %attend.3 = (bf16[5,128,128]{2,1,0:T(8,128)(2,1)S(1)}, bf16[5,128,128]{2,1,0:T(8,128)(2,1)S(1)}, f32[128,256]{1,0:T(8,128)S(1)}, f32[128,256]{1,0:T(8,128)S(1)},...) custom-call(s32[2]{0:T(128)S(1)} %copy-done.2, s32[2,2]{1,0:T(2,128)S(1)} %copy-done.1, ...), custom_call_target="tpu_custom_call" | custom-call | flops 4529848320 | bytes 1048576 | tf_op jit(solution)/shard_map/attend/pallas_call | solution.py:374
  62.5 0.1 collective-permute-start.12
  62.6 1.9 %collective-permute-done.12.received_ref = bf16[4,128,512]{2,1,0:T(8,128)(2,1)S(1)} collective-permute-done((bf16[4,128,512]{2,1,0:T(8,128)(2,1)S(1)}, bf16[4,128,512]{2,1,0:T(8,128)(2,1)S(1)}, u32[]{:S(2)}, u32[]{:S(2)}) %collective-permute-start.12) | collective-permute-done | bytes 524320 | tf_op jit(solution)/shard_map/ppermute | solution.py:275
  64.5 0.1 combine.1
  64.6 0.1 collective-permute-start.13
  64.7 3.0 %collective-permute-start.14 = (bf16[128,512]{1,0:T(8,128)(2,1)S(1)}, bf16[128,512]{1,0:T(8,128)(2,1)S(1)}, u32[]{:S(2)}, u32[]{:S(2)}) collective-permute-start(bf16[128,512]{1,0:T(8,128)(2,1)S(1)} %get-tuple-element.79), channel_id=1, source_target_pairs={{0,8},{4,12},{8,0},{12,4},{1,9},{5,13},{9,1},{13,5},{2,10},{6,14},... | collective-permute-start | bytes 393224 | tf_op jit(solution)/shard_map/ppermute | solution.py:279
  67.7 0.0 collective-permute-start.16
  67.7 1.4 %collective-permute-start.15 = (bf16[128,512]{1,0:T(8,128)(2,1)S(1)}, bf16[128,512]{1,0:T(8,128)(2,1)S(1)}, u32[]{:S(2)}, u32[]{:S(2)}) collective-permute-start(bf16[128,512]{1,0:T(8,128)(2,1)S(1)} %get-tuple-element.80), channel_id=1, source_target_pairs={{0,12},{4,8},{8,4},{12,0},{1,13},{5,9},{9,5},{13,1},{2,14},{6,10},... | collective-permute-start | bytes 393224 | tf_op jit(solution)/shard_map/ppermute | solution.py:279
  69.0 0.9 %place.1 = (bf16[2,128,640]{2,1,0:T(8,128)(2,1)}, bf16[2,128,640]{2,1,0:T(8,128)(2,1)}, bf16[2,128,128]{2,1,0:T(8,128)(2,1)}, bf16[2,128,128]{2,1,0:T(8,128)(2,1)}) custom-call(bf16[5,128,128]{2,1,0:T(8,128)(2,1)S(1)} %get-tuple-element.63.refs_0_, bf16[5,128,128]{2,1,0:T(8,128)(2,1)S(1)} %get-tuple-element.64.refs_1_, ...), custom_call_target="tpu_custom_call" | custom-call | tf_op jit(solution)/shard_map/place/pallas_call | solution.py:391
  70.0 2.5 %collective-permute-done.13.refs_1_ = bf16[128,512]{1,0:T(8,128)(2,1)S(1)} collective-permute-done((bf16[128,512]{1,0:T(8,128)(2,1)S(1)}, bf16[128,512]{1,0:T(8,128)(2,1)S(1)}, u32[]{:S(2)}, u32[]{:S(2)}) %collective-permute-start.13) | collective-permute-done | bytes 131104 | tf_op jit(solution)/shard_map/ppermute | solution.py:279
  72.5 0.0 collective-permute-start.17
  72.5 5.2 %collective-permute-done.14.refs_2_ = bf16[128,512]{1,0:T(8,128)(2,1)S(1)} collective-permute-done((bf16[128,512]{1,0:T(8,128)(2,1)S(1)}, bf16[128,512]{1,0:T(8,128)(2,1)S(1)}, u32[]{:S(2)}, u32[]{:S(2)}) %collective-permute-start.14) | collective-permute-done | bytes 131104 | tf_op jit(solution)/shard_map/ppermute | solution.py:279
  77.7 0.0 collective-permute-start.18
  77.7 0.0 collective-permute-done.15.refs_3_
  77.7 0.5 collective-permute-start.19
  78.2 0.8 %finish.2.refs_0_ = f32[2,512,128]{2,1,0:T(8,128)} custom-call(f32[128,512]{1,0:T(8,128)S(1)} %get-tuple-element.77.refs_0_, bf16[128,512]{1,0:T(8,128)(2,1)S(1)} %collective-permute-done.13.refs_1_, bf16[128,512]{1,0:T(8,128)(2,1)S(1)} %collective-permute-done.14.refs_2_, bf16[128,512]{1,0:T(8,128)(2,1)S(1)} %collective-permute-done.15.refs_3_), custom_call_target="tpu_custom_call" | custom-call | tf_op jit(solution)/shard_map/finish/pallas_call | solution.py:424
  79.0 0.0 collective-permute-done.16.refs_1_
  79.0 0.0 collective-permute-done.17.refs_2_
  79.0 0.0 collective-permute-done.18.refs_3_
  79.1 0.1 collective-permute-done.19.refs_4_
  79.2 0.8 %finish.3 = f32[2,512,128]{2,1,0:T(8,128)} custom-call(f32[2,512,128]{2,1,0:T(8,128)} %finish.2.refs_0_, f32[128,512]{1,0:T(8,128)S(1)} %collective-permute-done.16.refs_1_, bf16[128,512]{1,0:T(8,128)(2,1)S(1)} %collective-permute-done.17.refs_2_, bf16[128,512]{1,0:T(8,128)(2,1)S(1)} %collective-permute-done.18.refs_3_, ...), custom_call_target="tpu_custom_call", output_to_operand_aliasing={{}: (0, {})} | custom-call | tf_op jit(solution)/shard_map/finish/pallas_call | solution.py:424
  (1 shorter events, 0.0 us)
Async XLA Ops:
  0.6 11.0 %copy-start.3 = (s32[16]{0:T(128)S(1)}, s32[16]{0:T(128)}, u32[]{:S(2)}) copy-start(s32[16]{0:T(128)} %param.15) | copy-start | bytes 196
  2.8 7.7 %copy-start.4 = (bf16[768,128]{1,0:T(8,128)(2,1)S(1)}, bf16[768,128]{1,0:T(8,128)(2,1)}, u32[]{:S(2)}) copy-start(bf16[768,128]{1,0:T(8,128)(2,1)} %get-tuple-element.48) | copy-start | bytes 589828
  2.9 17.3 %collective-permute-start = (bf16[1280,128]{1,0:T(8,128)(2,1)}, bf16[1280,128]{1,0:T(8,128)(2,1)S(1)}, u32[]{:S(2)}, u32[]{:S(2)}) collective-permute-start(bf16[1280,128]{1,0:T(8,128)(2,1)} %get-tuple-element.43), channel_id=1, source_target_pairs={{0,4},{4,0},{8,12},{12,8},{1,5},{5,1},{9,13},{13,9},{2,6},{6,2},{1... | collective-permute-start | bytes 983048 | tf_op jit(solution)/shard_map/ppermute | solution.py:279
  5.9 23.0 %collective-permute-start.1 = (bf16[1280,128]{1,0:T(8,128)(2,1)}, bf16[1280,128]{1,0:T(8,128)(2,1)S(1)}, u32[]{:S(2)}, u32[]{:S(2)}) collective-permute-start(bf16[1280,128]{1,0:T(8,128)(2,1)} %get-tuple-element.47), channel_id=1, source_target_pairs={{0,8},{4,12},{8,0},{12,4},{1,9},{5,13},{9,1},{13,5},{2,10},{6,14},... | collective-permute-start | bytes 983048 | tf_op jit(solution)/shard_map/ppermute | solution.py:279
  10.5 19.0 %collective-permute-start.3 = (bf16[1280,128]{1,0:T(8,128)(2,1)}, bf16[1280,128]{1,0:T(8,128)(2,1)S(1)}, u32[]{:S(2)}, u32[]{:S(2)}) collective-permute-start(bf16[1280,128]{1,0:T(8,128)(2,1)} %pack.2.refs_6_), channel_id=1, source_target_pairs={{0,1},{1,0},{2,3},{3,2},{4,5},{5,4},{6,7},{7,6},{8,9},{9,8},{10,11... | collective-permute-start | bytes 983048 | tf_op jit(solution)/shard_map/ppermute | solution.py:275
  10.6 18.3 %collective-permute-start.2 = (bf16[768,128]{1,0:T(8,128)(2,1)S(1)}, bf16[768,128]{1,0:T(8,128)(2,1)S(1)}, u32[]{:S(2)}, u32[]{:S(2)}) collective-permute-start(bf16[768,128]{1,0:T(8,128)(2,1)S(1)} %copy-done.4), channel_id=1, source_target_pairs={{0,12},{4,8},{8,4},{12,0},{1,13},{5,9},{9,5},{13,1},{2,14},{6,10},... | collective-permute-start | bytes 589832 | tf_op jit(solution)/shard_map/ppermute | solution.py:279
  11.6 38.8 %copy-start = (bf16[1280,128]{1,0:T(8,128)(2,1)S(1)}, bf16[1280,128]{1,0:T(8,128)(2,1)}, u32[]{:S(2)}) copy-start(bf16[1280,128]{1,0:T(8,128)(2,1)} %pack.2.refs_6_) | copy-start | bytes 983044
  11.6 38.8 %copy-start.1 = (s32[2,2]{1,0:T(2,128)S(1)}, s32[2,2]{1,0:T(2,128)}, u32[]{:S(2)}) copy-start(s32[2,2]{1,0:T(2,128)} %tree_ref.3) | copy-start | bytes 52
  11.6 38.8 %copy-start.2 = (s32[2]{0:T(128)S(1)}, s32[2]{0:T(128)}, u32[]{:S(2)}) copy-start(s32[2]{0:T(128)} %length_ref.3) | copy-start | bytes 28
  20.1 10.7 %collective-permute-start.4 = (bf16[1280,128]{1,0:T(8,128)(2,1)S(1)}, bf16[1280,128]{1,0:T(8,128)(2,1)S(1)}, u32[]{:S(2)}, u32[]{:S(2)}) collective-permute-start(bf16[1280,128]{1,0:T(8,128)(2,1)S(1)} %collective-permute-done.refs_1_.refs_7_), channel_id=1, source_target_pairs={{0,1},{1,0},{2,3},{3,2},{4,5},{5,4},{6,7},{7,6},{8,9},{9,8},{10,11... | collective-permute-start | bytes 983048 | tf_op jit(solution)/shard_map/ppermute | solution.py:275
  28.9 1.9 %collective-permute-start.5 = (bf16[1280,128]{1,0:T(8,128)(2,1)S(1)}, bf16[1280,128]{1,0:T(8,128)(2,1)S(1)}, u32[]{:S(2)}, u32[]{:S(2)}) collective-permute-start(bf16[1280,128]{1,0:T(8,128)(2,1)S(1)} %collective-permute-done.1.refs_2_.refs_8_), channel_id=1, source_target_pairs={{0,1},{1,0},{2,3},{3,2},{4,5},{5,4},{6,7},{7,6},{8,9},{9,8},{10,11... | collective-permute-start | bytes 983048 | tf_op jit(solution)/shard_map/ppermute | solution.py:275
  28.9 1.9 %collective-permute-start.6 = (bf16[768,128]{1,0:T(8,128)(2,1)S(1)}, bf16[768,128]{1,0:T(8,128)(2,1)S(1)}, u32[]{:S(2)}, u32[]{:S(2)}) collective-permute-start(bf16[768,128]{1,0:T(8,128)(2,1)S(1)} %collective-permute-done.2.refs_3_), channel_id=1, source_target_pairs={{0,1},{1,0},{2,3},{3,2},{4,5},{5,4},{6,7},{7,6},{8,9},{9,8},{10,11... | collective-permute-start | bytes 589832 | tf_op jit(solution)/shard_map/ppermute | solution.py:275
  31.7 18.7 %collective-permute-start.9 = (bf16[1792,128]{1,0:T(8,128)(2,1)S(1)}, bf16[1792,128]{1,0:T(8,128)(2,1)S(1)}, u32[]{:S(2)}, u32[]{:S(2)}) collective-permute-start(bf16[1792,128]{1,0:T(8,128)(2,1)S(1)} %get-tuple-element.52), channel_id=1, source_target_pairs={{0,4},{4,0},{8,12},{12,8},{1,5},{5,1},{9,13},{13,9},{2,6},{6,2},{1... | collective-permute-start | bytes 1376264 | tf_op jit(solution)/shard_map/ppermute | solution.py:279
  34.7 11.6 %collective-permute-start.10 = (bf16[128,128]{1,0:T(8,128)(2,1)S(1)}, bf16[128,128]{1,0:T(8,128)(2,1)S(1)}, u32[]{:S(2)}, u32[]{:S(2)}) collective-permute-start(bf16[128,128]{1,0:T(8,128)(2,1)S(1)} %get-tuple-element.54), channel_id=1, source_target_pairs={{0,8},{4,12},{8,0},{12,4},{1,9},{5,13},{9,1},{13,5},{2,10},{6,14},... | collective-permute-start | bytes 98312 | tf_op jit(solution)/shard_map/ppermute | solution.py:279
  35.8 14.1 %collective-permute-start.11 = (bf16[128,128]{1,0:T(8,128)(2,1)S(1)}, bf16[128,128]{1,0:T(8,128)(2,1)S(1)}, u32[]{:S(2)}, u32[]{:S(2)}) collective-permute-start(bf16[128,128]{1,0:T(8,128)(2,1)S(1)} %get-tuple-element.55), channel_id=1, source_target_pairs={{0,12},{4,8},{8,4},{12,0},{1,13},{5,9},{9,5},{13,1},{2,14},{6,10},... | collective-permute-start | bytes 98312 | tf_op jit(solution)/shard_map/ppermute | solution.py:279
  37.1 19.3 %collective-permute-start.7 = (bf16[640,128]{1,0:T(8,128)(2,1)S(1)}, bf16[640,128]{1,0:T(8,128)(2,1)S(1)}, u32[]{:S(2)}, u32[]{:S(2)}) collective-permute-start(bf16[640,128]{1,0:T(8,128)(2,1)S(1)} %get-tuple-element.49), channel_id=1, source_target_pairs={{0,8},{4,12},{8,0},{12,4},{1,9},{5,13},{9,1},{13,5},{2,10},{6,14},... | collective-permute-start | bytes 491528 | tf_op jit(solution)/shard_map/ppermute | solution.py:279
  39.2 17.3 %collective-permute-start.8 = (bf16[640,128]{1,0:T(8,128)(2,1)S(1)}, bf16[640,128]{1,0:T(8,128)(2,1)S(1)}, u32[]{:S(2)}, u32[]{:S(2)}) collective-permute-start(bf16[640,128]{1,0:T(8,128)(2,1)S(1)} %get-tuple-element.50), channel_id=1, source_target_pairs={{0,12},{4,8},{8,4},{12,0},{1,13},{5,9},{9,5},{13,1},{2,14},{6,10},... | collective-permute-start | bytes 491528 | tf_op jit(solution)/shard_map/ppermute | solution.py:279
  62.5 2.0 %collective-permute-start.12 = (bf16[4,128,512]{2,1,0:T(8,128)(2,1)S(1)}, bf16[4,128,512]{2,1,0:T(8,128)(2,1)S(1)}, u32[]{:S(2)}, u32[]{:S(2)}) collective-permute-start(bf16[4,128,512]{2,1,0:T(8,128)(2,1)S(1)} %get-tuple-element.61), channel_id=1, source_target_pairs={{0,1},{1,0},{2,3},{3,2},{4,5},{5,4},{6,7},{7,6},{8,9},{9,8},{10,11... | collective-permute-start | bytes 1572872 | tf_op jit(solution)/shard_map/ppermute | solution.py:275
  64.6 7.9 %collective-permute-start.13 = (bf16[128,512]{1,0:T(8,128)(2,1)S(1)}, bf16[128,512]{1,0:T(8,128)(2,1)S(1)}, u32[]{:S(2)}, u32[]{:S(2)}) collective-permute-start(bf16[128,512]{1,0:T(8,128)(2,1)S(1)} %get-tuple-element.62), channel_id=1, source_target_pairs={{0,4},{4,0},{8,12},{12,8},{1,5},{5,1},{9,13},{13,9},{2,6},{6,2},{1... | collective-permute-start | bytes 393224 | tf_op jit(solution)/shard_map/ppermute | solution.py:279
  64.7 13.0 %collective-permute-start.14 = (bf16[128,512]{1,0:T(8,128)(2,1)S(1)}, bf16[128,512]{1,0:T(8,128)(2,1)S(1)}, u32[]{:S(2)}, u32[]{:S(2)}) collective-permute-start(bf16[128,512]{1,0:T(8,128)(2,1)S(1)} %get-tuple-element.79), channel_id=1, source_target_pairs={{0,8},{4,12},{8,0},{12,4},{1,9},{5,13},{9,1},{13,5},{2,10},{6,14},... | collective-permute-start | bytes 393224 | tf_op jit(solution)/shard_map/ppermute | solution.py:279
  67.7 11.4 %collective-permute-start.16 = (f32[128,512]{1,0:T(8,128)S(1)}, f32[128,512]{1,0:T(8,128)S(1)}, u32[]{:S(2)}, u32[]{:S(2)}) collective-permute-start(f32[128,512]{1,0:T(8,128)S(1)} %get-tuple-element.77.refs_0_), channel_id=1, source_target_pairs={{0,1},{1,0},{2,3},{3,2},{4,5},{5,4},{6,7},{7,6},{8,9},{9,8},{10,11... | collective-permute-start | bytes 786440 | tf_op jit(solution)/shard_map/ppermute | solution.py:275
  67.7 10.0 %collective-permute-start.15 = (bf16[128,512]{1,0:T(8,128)(2,1)S(1)}, bf16[128,512]{1,0:T(8,128)(2,1)S(1)}, u32[]{:S(2)}, u32[]{:S(2)}) collective-permute-start(bf16[128,512]{1,0:T(8,128)(2,1)S(1)} %get-tuple-element.80), channel_id=1, source_target_pairs={{0,12},{4,8},{8,4},{12,0},{1,13},{5,9},{9,5},{13,1},{2,14},{6,10},... | collective-permute-start | bytes 393224 | tf_op jit(solution)/shard_map/ppermute | solution.py:279
  72.5 6.6 %collective-permute-start.17 = (bf16[128,512]{1,0:T(8,128)(2,1)S(1)}, bf16[128,512]{1,0:T(8,128)(2,1)S(1)}, u32[]{:S(2)}, u32[]{:S(2)}) collective-permute-start(bf16[128,512]{1,0:T(8,128)(2,1)S(1)} %collective-permute-done.13.refs_1_), channel_id=1, source_target_pairs={{0,1},{1,0},{2,3},{3,2},{4,5},{5,4},{6,7},{7,6},{8,9},{9,8},{10,11... | collective-permute-start | bytes 393224 | tf_op jit(solution)/shard_map/ppermute | solution.py:275
  77.7 1.4 %collective-permute-start.18 = (bf16[128,512]{1,0:T(8,128)(2,1)S(1)}, bf16[128,512]{1,0:T(8,128)(2,1)S(1)}, u32[]{:S(2)}, u32[]{:S(2)}) collective-permute-start(bf16[128,512]{1,0:T(8,128)(2,1)S(1)} %collective-permute-done.14.refs_2_), channel_id=1, source_target_pairs={{0,1},{1,0},{2,3},{3,2},{4,5},{5,4},{6,7},{7,6},{8,9},{9,8},{10,11... | collective-permute-start | bytes 393224 | tf_op jit(solution)/shard_map/ppermute | solution.py:275
  77.7 1.5 %collective-permute-start.19 = (bf16[128,512]{1,0:T(8,128)(2,1)S(1)}, bf16[128,512]{1,0:T(8,128)(2,1)S(1)}, u32[]{:S(2)}, u32[]{:S(2)}) collective-permute-start(bf16[128,512]{1,0:T(8,128)(2,1)S(1)} %collective-permute-done.15.refs_3_), channel_id=1, source_target_pairs={{0,1},{1,0},{2,3},{3,2},{4,5},{5,4},{6,7},{7,6},{8,9},{9,8},{10,11... | collective-permute-start | bytes 393224 | tf_op jit(solution)/shard_map/ppermute | solution.py:275

commit v8 on v7

--- a/solution.py
+++ b/solution.py
@@ -314,7 +314,7 @@
                 in_specs=[HBM] * 6,
                 out_specs=[VMEM] * len(fars),
                 scratch_shapes=[pltpu.VMEM(source.shape, bf16) for source in sources] + [pltpu.SemaphoreType.DMA((6,))],
-                compiler_params=FULL,
+                compiler_params=FULL if len(fars) > 1 else SMALL,
                 name="pack",
             )(*sources, prompt_keys, prompt_values)
             packed.update(zip(fars, messages))

time: 80.2 us -> 80.5 us (level)
  local copies, waits for them, and re-layouts: 1.25 us -> 4.03 us
  waiting for transfers between devices: 38 us -> 36.1 us
  Pallas kernels: 19.8 us -> 18.6 us
    unnamed x10 -> x20, local copies, waits for them, and re-layouts: 0.03 us -> 3.74 us
    ppermute x11, waiting for transfers between devices: 34.6 us -> 32.8 us  [to_far(): lax.ppermute(value, 'seq', [(chip, chip ^ far) for chip in range(lax.axis...]
    pallas_call x2, Pallas kernels: 4.15 us -> 2.85 us  [per_device(): pl.pallas_call(functools.partial(pack_kernel, band, tiles, fars), out_sha...]
    slice x1, local copies, waits for them, and re-layouts: 0.94 us -> 0.01 us  [per_device(): mine[0][:length]]
  transfers between devices with their start and end apart: 20 -> 20, of which waited for: 10 -> 10; matrix products, arithmetic and copies ran while one was open for 2% -> 0% of each run, Pallas kernels for 12% -> 10%
where the time goes in v8:
time: 80.5 us; the launch traced here: 80.2 us
  waiting for transfers between devices  36.1 us (45%)
  starting transfers between devices  20.6 us (26%)
  Pallas kernels  18.6 us (23%)
  local copies, waits for them, and re-layouts  4.03 us (5%)
  between operations  0.82 us (1%)
    ppermute x11, waiting for transfers between devices, to_far(): lax.ppermute(value, 'seq', [(chip, chip ^ far) for chip in range(lax.axis...  32.8 us
    ppermute x11, starting transfers between devices, to_far(): lax.ppermute(value, 'seq', [(chip, chip ^ far) for chip in range(lax.axis...  19.5 us
    pallas_call x2, Pallas kernels, per_device(): pl.pallas_call(functools.partial(attend_kernel, band, heads, rows, bands,...  12.2 us
    unnamed x20, local copies, waits for them, and re-layouts  3.74 us
    ppermute x9, waiting for transfers between devices, swap_cores(): return lax.ppermute(value, 'rep', [(0, 1), (1, 0)])  3.35 us
    pallas_call x2, Pallas kernels, per_device(): pl.pallas_call(functools.partial(pack_kernel, band, tiles, fars), out_sha...  2.85 us
    pallas_call x2, Pallas kernels, per_device(): pl.pallas_call(functools.partial(finish_kernel, other), out_shape=jax.Sha...  1.7 us
  transfers between devices with their start and end apart: 20, of which 10 were waited for; matrix products, arithmetic and copies ran while one was open for 0% of the time, Pallas kernels for 10%

profile of v8, /device:TPU:0, one launch (start us, length us, event | category | flops | bytes accessed | tf_op | source)
XLA Modules:
  0.0 80.2 jit_solution(12084674503550931186)
XLA Ops:
  0.6 0.0 copy-start.1
  0.6 0.0 copy-start
  0.7 0.0 copy-start.8
  0.7 2.2 %pack.3 = (bf16[1280,128]{1,0:T(8,128)(2,1)}, bf16[1280,128]{1,0:T(8,128)(2,1)}, bf16[768,128]{1,0:T(8,128)(2,1)}) custom-call(bf16[2,128,128]{2,1,0:T(8,128)(2,1)} %k_hbm.3, bf16[2,128,128]{2,1,0:T(8,128)(2,1)} %v_hbm.3, bf16[2,128,640]{2,1,0:T(8,128)(2,1)} %q_hbm.3, bf16[2,128,640]{2,1,0:T(8,128)(2,1)} %g_hbm.3, bf16[512,128]{1,0:T(8,128)(2,1)} %pk_hbm.3, ...), custom_call_target="tpu_custom_call" | custom-call | tf_op jit(solution)/shard_map/pack/pallas_call | solution.py:311
  2.9 3.1 %collective-permute-start = (bf16[1280,128]{1,0:T(8,128)(2,1)}, bf16[1280,128]{1,0:T(8,128)(2,1)S(1)}, u32[]{:S(2)}, u32[]{:S(2)}) collective-permute-start(bf16[1280,128]{1,0:T(8,128)(2,1)} %get-tuple-element.43), channel_id=1, source_target_pairs={{0,4},{4,0},{8,12},{12,8},{1,5},{5,1},{9,13},{13,9},{2,6},{6,2},{1... | collective-permute-start | bytes 983048 | tf_op jit(solution)/shard_map/ppermute | solution.py:279
  6.0 2.6 %collective-permute-start.1 = (bf16[1280,128]{1,0:T(8,128)(2,1)}, bf16[1280,128]{1,0:T(8,128)(2,1)S(1)}, u32[]{:S(2)}, u32[]{:S(2)}) collective-permute-start(bf16[1280,128]{1,0:T(8,128)(2,1)} %get-tuple-element.47), channel_id=1, source_target_pairs={{0,8},{4,12},{8,0},{12,4},{1,9},{5,13},{9,1},{13,5},{2,10},{6,14},... | collective-permute-start | bytes 983048 | tf_op jit(solution)/shard_map/ppermute | solution.py:279
  8.6 0.0 copy-done.1
  8.6 0.0 copy-done
  8.6 0.9 %copy-done.2 = bf16[512,128]{1,0:T(8,128)(2,1)S(1)} copy-done((bf16[512,128]{1,0:T(8,128)(2,1)S(1)}, bf16[512,128]{1,0:T(8,128)(2,1)}, u32[]{:S(2)}) %copy-start.2) | copy-done | bytes 131096
  9.5 0.9 %copy-done.3 = bf16[512,128]{1,0:T(8,128)(2,1)S(1)} copy-done((bf16[512,128]{1,0:T(8,128)(2,1)S(1)}, bf16[512,128]{1,0:T(8,128)(2,1)}, u32[]{:S(2)}) %copy-start.3) | copy-done | bytes 131096
  10.4 0.8 %copy-done.4 = bf16[2,128,128]{2,1,0:T(8,128)(2,1)S(1)} copy-done((bf16[2,128,128]{2,1,0:T(8,128)(2,1)S(1)}, bf16[2,128,128]{2,1,0:T(8,128)(2,1)}, u32[]{:S(2)}) %copy-start.4) | copy-done | bytes 65560
  11.2 0.8 %copy-done.5 = bf16[2,128,128]{2,1,0:T(8,128)(2,1)S(1)} copy-done((bf16[2,128,128]{2,1,0:T(8,128)(2,1)S(1)}, bf16[2,128,128]{2,1,0:T(8,128)(2,1)}, u32[]{:S(2)}) %copy-start.5) | copy-done | bytes 65560
  12.1 0.6 pack.2.refs_6_
  12.7 0.1 collective-permute-start.3
  12.8 0.2 copy-done.9
  13.0 0.0 collective-permute-start.2
  13.0 0.0 copy-start.6
  13.0 0.0 copy-start.7
  13.1 0.1 reshape.13
  13.2 0.1 copy.17
  13.3 7.2 %collective-permute-done.refs_1_.refs_7_ = bf16[1280,128]{1,0:T(8,128)(2,1)S(1)} collective-permute-done((bf16[1280,128]{1,0:T(8,128)(2,1)}, bf16[1280,128]{1,0:T(8,128)(2,1)S(1)}, u32[]{:S(2)}, u32[]{:S(2)}) %collective-permute-start) | collective-permute-done | bytes 327712 | tf_op jit(solution)/shard_map/ppermute | solution.py:279
  20.4 0.0 collective-permute-start.4
  20.4 8.0 %collective-permute-done.1.refs_2_.refs_8_ = bf16[1280,128]{1,0:T(8,128)(2,1)S(1)} collective-permute-done((bf16[1280,128]{1,0:T(8,128)(2,1)}, bf16[1280,128]{1,0:T(8,128)(2,1)S(1)}, u32[]{:S(2)}, u32[]{:S(2)}) %collective-permute-start.1) | collective-permute-done | bytes 327712 | tf_op jit(solution)/shard_map/ppermute | solution.py:279
  28.5 0.0 collective-permute-start.5
  28.5 0.0 collective-permute-done.2.refs_3_
  28.5 0.5 collective-permute-start.6
  29.0 0.1 copy.18.wanted_ref
  29.1 0.0 collective-permute-done.3.refs_4_.refs_9_
  29.1 1.3 %collective-permute-done.6.refs_7_ = bf16[768,128]{1,0:T(8,128)(2,1)S(1)} collective-permute-done((bf16[768,128]{1,0:T(8,128)(2,1)S(1)}, bf16[768,128]{1,0:T(8,128)(2,1)S(1)}, u32[]{:S(2)}, u32[]{:S(2)}) %collective-permute-start.6) | collective-permute-done | bytes 196640 | tf_op jit(solution)/shard_map/ppermute | solution.py:275
  30.4 0.0 collective-permute-done.4.refs_5_.refs_10_
  30.4 0.0 collective-permute-done.5.refs_6_.refs_11_
  30.4 0.9 %pick.1 = (bf16[128,128]{1,0:T(8,128)(2,1)S(1)}, bf16[640,128]{1,0:T(8,128)(2,1)S(1)}, bf16[128,128]{1,0:T(8,128)(2,1)S(1)}, bf16[640,128]{1,0:T(8,128)(2,1)S(1)...) custom-call(s32[4,2]{1,0:T(4,128)S(1)} %copy.18.wanted_ref, ...), custom_call_target="tpu_custom_call" | custom-call | tf_op jit(solution)/shard_map/pick/pallas_call | solution.py:326
  31.2 3.5 %collective-permute-start.9 = (bf16[1792,128]{1,0:T(8,128)(2,1)S(1)}, bf16[1792,128]{1,0:T(8,128)(2,1)S(1)}, u32[]{:S(2)}, u32[]{:S(2)}) collective-permute-start(bf16[1792,128]{1,0:T(8,128)(2,1)S(1)} %get-tuple-element.52), channel_id=1, source_target_pairs={{0,4},{4,0},{8,12},{12,8},{1,5},{5,1},{9,13},{13,9},{2,6},{6,2},{1... | collective-permute-start | bytes 1376264 | tf_op jit(solution)/shard_map/ppermute | solution.py:279
  34.7 1.1 %collective-permute-start.10 = (bf16[128,128]{1,0:T(8,128)(2,1)S(1)}, bf16[128,128]{1,0:T(8,128)(2,1)S(1)}, u32[]{:S(2)}, u32[]{:S(2)}) collective-permute-start(bf16[128,128]{1,0:T(8,128)(2,1)S(1)} %get-tuple-element.54), channel_id=1, source_target_pairs={{0,8},{4,12},{8,0},{12,4},{1,9},{5,13},{9,1},{13,5},{2,10},{6,14},... | collective-permute-start | bytes 98312 | tf_op jit(solution)/shard_map/ppermute | solution.py:279
  35.8 1.4 %collective-permute-start.11 = (bf16[128,128]{1,0:T(8,128)(2,1)S(1)}, bf16[128,128]{1,0:T(8,128)(2,1)S(1)}, u32[]{:S(2)}, u32[]{:S(2)}) collective-permute-start(bf16[128,128]{1,0:T(8,128)(2,1)S(1)} %get-tuple-element.55), channel_id=1, source_target_pairs={{0,12},{4,8},{8,4},{12,0},{1,13},{5,9},{9,5},{13,1},{2,14},{6,10},... | collective-permute-start | bytes 98312 | tf_op jit(solution)/shard_map/ppermute | solution.py:279
  37.2 2.0 %collective-permute-start.7 = (bf16[640,128]{1,0:T(8,128)(2,1)S(1)}, bf16[640,128]{1,0:T(8,128)(2,1)S(1)}, u32[]{:S(2)}, u32[]{:S(2)}) collective-permute-start(bf16[640,128]{1,0:T(8,128)(2,1)S(1)} %get-tuple-element.49), channel_id=1, source_target_pairs={{0,8},{4,12},{8,0},{12,4},{1,9},{5,13},{9,1},{13,5},{2,10},{6,14},... | collective-permute-start | bytes 491528 | tf_op jit(solution)/shard_map/ppermute | solution.py:279
  39.2 1.4 %collective-permute-start.8 = (bf16[640,128]{1,0:T(8,128)(2,1)S(1)}, bf16[640,128]{1,0:T(8,128)(2,1)S(1)}, u32[]{:S(2)}, u32[]{:S(2)}) collective-permute-start(bf16[640,128]{1,0:T(8,128)(2,1)S(1)} %get-tuple-element.50), channel_id=1, source_target_pairs={{0,12},{4,8},{8,4},{12,0},{1,13},{5,9},{9,5},{13,1},{2,14},{6,10},... | collective-permute-start | bytes 491528 | tf_op jit(solution)/shard_map/ppermute | solution.py:279
  40.6 5.7 %collective-permute-done.10.refs_4_ = bf16[128,128]{1,0:T(8,128)(2,1)S(1)} collective-permute-done((bf16[128,128]{1,0:T(8,128)(2,1)S(1)}, bf16[128,128]{1,0:T(8,128)(2,1)S(1)}, u32[]{:S(2)}, u32[]{:S(2)}) %collective-permute-start.10) | collective-permute-done | bytes 32800 | tf_op jit(solution)/shard_map/ppermute | solution.py:279
  46.3 3.6 %collective-permute-done.11.refs_5_ = bf16[128,128]{1,0:T(8,128)(2,1)S(1)} collective-permute-done((bf16[128,128]{1,0:T(8,128)(2,1)S(1)}, bf16[128,128]{1,0:T(8,128)(2,1)S(1)}, u32[]{:S(2)}, u32[]{:S(2)}) %collective-permute-start.11) | collective-permute-done | bytes 32800 | tf_op jit(solution)/shard_map/ppermute | solution.py:279
  49.9 0.5 collective-permute-done.9.refs_1_.refs_3_
  50.5 6.0 %attend.2 = (bf16[5,128,128]{2,1,0:T(8,128)(2,1)S(1)}, bf16[5,128,128]{2,1,0:T(8,128)(2,1)S(1)}, bf16[2304,128]{1,0:T(8,128)(2,1)S(1)}, bf16[2304,128]{1,0:T(8,1...) custom-call(s32[2]{0:T(128)S(1)} %copy-done.7, s32[2,2]{1,0:T(2,128)S(1)} %copy-done.6, ...), custom_call_target="tpu_custom_call" | custom-call | flops 4529848320 | bytes 1048576 | tf_op jit(solution)/shard_map/attend/pallas_call | solution.py:374
  56.5 0.0 collective-permute-done.7.refs_0_
  56.5 0.0 collective-permute-done.8.refs_1_
  56.5 6.2 %attend.3 = (bf16[5,128,128]{2,1,0:T(8,128)(2,1)S(1)}, bf16[5,128,128]{2,1,0:T(8,128)(2,1)S(1)}, f32[128,256]{1,0:T(8,128)S(1)}, f32[128,256]{1,0:T(8,128)S(1)},...) custom-call(s32[2]{0:T(128)S(1)} %copy-done.7, s32[2,2]{1,0:T(2,128)S(1)} %copy-done.6, ...), custom_call_target="tpu_custom_call" | custom-call | flops 4529848320 | bytes 1048576 | tf_op jit(solution)/shard_map/attend/pallas_call | solution.py:374
  62.7 0.1 collective-permute-start.12
  62.7 1.9 %collective-permute-done.12.received_ref = bf16[4,128,512]{2,1,0:T(8,128)(2,1)S(1)} collective-permute-done((bf16[4,128,512]{2,1,0:T(8,128)(2,1)S(1)}, bf16[4,128,512]{2,1,0:T(8,128)(2,1)S(1)}, u32[]{:S(2)}, u32[]{:S(2)}) %collective-permute-start.12) | collective-permute-done | bytes 524320 | tf_op jit(solution)/shard_map/ppermute | solution.py:275
  64.6 0.1 combine.1
  64.8 0.1 collective-permute-start.13
  64.8 3.0 %collective-permute-start.14 = (bf16[128,512]{1,0:T(8,128)(2,1)S(1)}, bf16[128,512]{1,0:T(8,128)(2,1)S(1)}, u32[]{:S(2)}, u32[]{:S(2)}) collective-permute-start(bf16[128,512]{1,0:T(8,128)(2,1)S(1)} %get-tuple-element.79), channel_id=1, source_target_pairs={{0,8},{4,12},{8,0},{12,4},{1,9},{5,13},{9,1},{13,5},{2,10},{6,14},... | collective-permute-start | bytes 393224 | tf_op jit(solution)/shard_map/ppermute | solution.py:279
  67.9 0.0 collective-permute-start.16
  67.9 1.4 %collective-permute-start.15 = (bf16[128,512]{1,0:T(8,128)(2,1)S(1)}, bf16[128,512]{1,0:T(8,128)(2,1)S(1)}, u32[]{:S(2)}, u32[]{:S(2)}) collective-permute-start(bf16[128,512]{1,0:T(8,128)(2,1)S(1)} %get-tuple-element.80), channel_id=1, source_target_pairs={{0,12},{4,8},{8,4},{12,0},{1,13},{5,9},{9,5},{13,1},{2,14},{6,10},... | collective-permute-start | bytes 393224 | tf_op jit(solution)/shard_map/ppermute | solution.py:279
  69.2 0.9 %place.1 = (bf16[2,128,640]{2,1,0:T(8,128)(2,1)}, bf16[2,128,640]{2,1,0:T(8,128)(2,1)}, bf16[2,128,128]{2,1,0:T(8,128)(2,1)}, bf16[2,128,128]{2,1,0:T(8,128)(2,1)}) custom-call(bf16[5,128,128]{2,1,0:T(8,128)(2,1)S(1)} %get-tuple-element.63.refs_0_, bf16[5,128,128]{2,1,0:T(8,128)(2,1)S(1)} %get-tuple-element.64.refs_1_, ...), custom_call_target="tpu_custom_call" | custom-call | tf_op jit(solution)/shard_map/place/pallas_call | solution.py:391
  70.2 2.5 %collective-permute-done.13.refs_1_ = bf16[128,512]{1,0:T(8,128)(2,1)S(1)} collective-permute-done((bf16[128,512]{1,0:T(8,128)(2,1)S(1)}, bf16[128,512]{1,0:T(8,128)(2,1)S(1)}, u32[]{:S(2)}, u32[]{:S(2)}) %collective-permute-start.13) | collective-permute-done | bytes 131104 | tf_op jit(solution)/shard_map/ppermute | solution.py:279
  72.7 0.0 collective-permute-start.17
  72.7 5.2 %collective-permute-done.14.refs_2_ = bf16[128,512]{1,0:T(8,128)(2,1)S(1)} collective-permute-done((bf16[128,512]{1,0:T(8,128)(2,1)S(1)}, bf16[128,512]{1,0:T(8,128)(2,1)S(1)}, u32[]{:S(2)}, u32[]{:S(2)}) %collective-permute-start.14) | collective-permute-done | bytes 131104 | tf_op jit(solution)/shard_map/ppermute | solution.py:279
  77.8 0.0 collective-permute-start.18
  77.8 0.0 collective-permute-done.15.refs_3_
  77.8 0.5 collective-permute-start.19
  78.3 0.8 %finish.2.refs_0_ = f32[2,512,128]{2,1,0:T(8,128)} custom-call(f32[128,512]{1,0:T(8,128)S(1)} %get-tuple-element.77.refs_0_, bf16[128,512]{1,0:T(8,128)(2,1)S(1)} %collective-permute-done.13.refs_1_, bf16[128,512]{1,0:T(8,128)(2,1)S(1)} %collective-permute-done.14.refs_2_, bf16[128,512]{1,0:T(8,128)(2,1)S(1)} %collective-permute-done.15.refs_3_), custom_call_target="tpu_custom_call" | custom-call | tf_op jit(solution)/shard_map/finish/pallas_call | solution.py:424
  79.2 0.0 collective-permute-done.16.refs_1_
  79.2 0.0 collective-permute-done.17.refs_2_
  79.2 0.0 collective-permute-done.18.refs_3_
  79.2 0.1 collective-permute-done.19.refs_4_
  79.4 0.8 %finish.3 = f32[2,512,128]{2,1,0:T(8,128)} custom-call(f32[2,512,128]{2,1,0:T(8,128)} %finish.2.refs_0_, f32[128,512]{1,0:T(8,128)S(1)} %collective-permute-done.16.refs_1_, bf16[128,512]{1,0:T(8,128)(2,1)S(1)} %collective-permute-done.17.refs_2_, bf16[128,512]{1,0:T(8,128)(2,1)S(1)} %collective-permute-done.18.refs_3_, ...), custom_call_target="tpu_custom_call", output_to_operand_aliasing={{}: (0, {})} | custom-call | tf_op jit(solution)/shard_map/finish/pallas_call | solution.py:424
  (10 shorter events, 0.0 us)
Async XLA Ops:
  0.6 8.0 %copy-start.1 = (bf16[2,128,640]{2,1,0:T(8,128)(2,1)S(1)}, bf16[2,128,640]{2,1,0:T(8,128)(2,1)}, u32[]{:S(2)}) copy-start(bf16[2,128,640]{2,1,0:T(8,128)(2,1)} %g_hbm.3) | copy-start | bytes 983044
  0.6 7.9 %copy-start = (bf16[2,128,640]{2,1,0:T(8,128)(2,1)S(1)}, bf16[2,128,640]{2,1,0:T(8,128)(2,1)}, u32[]{:S(2)}) copy-start(bf16[2,128,640]{2,1,0:T(8,128)(2,1)} %q_hbm.3) | copy-start | bytes 983044
  0.7 12.4 %copy-start.8 = (s32[16]{0:T(128)S(1)}, s32[16]{0:T(128)}, u32[]{:S(2)}) copy-start(s32[16]{0:T(128)} %param.15) | copy-start | bytes 196
  2.9 17.5 %collective-permute-start = (bf16[1280,128]{1,0:T(8,128)(2,1)}, bf16[1280,128]{1,0:T(8,128)(2,1)S(1)}, u32[]{:S(2)}, u32[]{:S(2)}) collective-permute-start(bf16[1280,128]{1,0:T(8,128)(2,1)} %get-tuple-element.43), channel_id=1, source_target_pairs={{0,4},{4,0},{8,12},{12,8},{1,5},{5,1},{9,13},{13,9},{2,6},{6,2},{1... | collective-permute-start | bytes 983048 | tf_op jit(solution)/shard_map/ppermute | solution.py:279
  6.0 22.5 %collective-permute-start.1 = (bf16[1280,128]{1,0:T(8,128)(2,1)}, bf16[1280,128]{1,0:T(8,128)(2,1)S(1)}, u32[]{:S(2)}, u32[]{:S(2)}) collective-permute-start(bf16[1280,128]{1,0:T(8,128)(2,1)} %get-tuple-element.47), channel_id=1, source_target_pairs={{0,8},{4,12},{8,0},{12,4},{1,9},{5,13},{9,1},{13,5},{2,10},{6,14},... | collective-permute-start | bytes 983048 | tf_op jit(solution)/shard_map/ppermute | solution.py:279
  8.6 0.9 %copy-start.2 = (bf16[512,128]{1,0:T(8,128)(2,1)S(1)}, bf16[512,128]{1,0:T(8,128)(2,1)}, u32[]{:S(2)}) copy-start(bf16[512,128]{1,0:T(8,128)(2,1)} %pk_hbm.3) | copy-start | bytes 393220
  9.5 0.9 %copy-start.3 = (bf16[512,128]{1,0:T(8,128)(2,1)S(1)}, bf16[512,128]{1,0:T(8,128)(2,1)}, u32[]{:S(2)}) copy-start(bf16[512,128]{1,0:T(8,128)(2,1)} %pv_hbm.3) | copy-start | bytes 393220
  10.4 0.8 %copy-start.4 = (bf16[2,128,128]{2,1,0:T(8,128)(2,1)S(1)}, bf16[2,128,128]{2,1,0:T(8,128)(2,1)}, u32[]{:S(2)}) copy-start(bf16[2,128,128]{2,1,0:T(8,128)(2,1)} %k_hbm.3) | copy-start | bytes 196612
  11.2 0.8 %copy-start.5 = (bf16[2,128,128]{2,1,0:T(8,128)(2,1)S(1)}, bf16[2,128,128]{2,1,0:T(8,128)(2,1)}, u32[]{:S(2)}) copy-start(bf16[2,128,128]{2,1,0:T(8,128)(2,1)} %v_hbm.3) | copy-start | bytes 196612
  12.1 0.9 %copy-start.9 = (bf16[768,128]{1,0:T(8,128)(2,1)S(1)}, bf16[768,128]{1,0:T(8,128)(2,1)}, u32[]{:S(2)}) copy-start(bf16[768,128]{1,0:T(8,128)(2,1)} %get-tuple-element.48) | copy-start | bytes 589828
  12.7 16.4 %collective-permute-start.3 = (bf16[1280,128]{1,0:T(8,128)(2,1)S(1)}, bf16[1280,128]{1,0:T(8,128)(2,1)S(1)}, u32[]{:S(2)}, u32[]{:S(2)}) collective-permute-start(bf16[1280,128]{1,0:T(8,128)(2,1)S(1)} %pack.2.refs_6_), channel_id=1, source_target_pairs={{0,1},{1,0},{2,3},{3,2},{4,5},{5,4},{6,7},{7,6},{8,9},{9,8},{10,11... | collective-permute-start | bytes 983048 | tf_op jit(solution)/shard_map/ppermute | solution.py:275
  13.0 15.5 %collective-permute-start.2 = (bf16[768,128]{1,0:T(8,128)(2,1)S(1)}, bf16[768,128]{1,0:T(8,128)(2,1)S(1)}, u32[]{:S(2)}, u32[]{:S(2)}) collective-permute-start(bf16[768,128]{1,0:T(8,128)(2,1)S(1)} %copy-done.9), channel_id=1, source_target_pairs={{0,12},{4,8},{8,4},{12,0},{1,13},{5,9},{9,5},{13,1},{2,14},{6,10},... | collective-permute-start | bytes 589832 | tf_op jit(solution)/shard_map/ppermute | solution.py:279
  13.0 37.4 %copy-start.6 = (s32[2,2]{1,0:T(2,128)S(1)}, s32[2,2]{1,0:T(2,128)}, u32[]{:S(2)}) copy-start(s32[2,2]{1,0:T(2,128)} %tree_ref.3) | copy-start | bytes 52
  13.0 37.4 %copy-start.7 = (s32[2]{0:T(128)S(1)}, s32[2]{0:T(128)}, u32[]{:S(2)}) copy-start(s32[2]{0:T(128)} %length_ref.3) | copy-start | bytes 28
  20.4 9.9 %collective-permute-start.4 = (bf16[1280,128]{1,0:T(8,128)(2,1)S(1)}, bf16[1280,128]{1,0:T(8,128)(2,1)S(1)}, u32[]{:S(2)}, u32[]{:S(2)}) collective-permute-start(bf16[1280,128]{1,0:T(8,128)(2,1)S(1)} %collective-permute-done.refs_1_.refs_7_), channel_id=1, source_target_pairs={{0,1},{1,0},{2,3},{3,2},{4,5},{5,4},{6,7},{7,6},{8,9},{9,8},{10,11... | collective-permute-start | bytes 983048 | tf_op jit(solution)/shard_map/ppermute | solution.py:275
  28.5 1.9 %collective-permute-start.5 = (bf16[1280,128]{1,0:T(8,128)(2,1)S(1)}, bf16[1280,128]{1,0:T(8,128)(2,1)S(1)}, u32[]{:S(2)}, u32[]{:S(2)}) collective-permute-start(bf16[1280,128]{1,0:T(8,128)(2,1)S(1)} %collective-permute-done.1.refs_2_.refs_8_), channel_id=1, source_target_pairs={{0,1},{1,0},{2,3},{3,2},{4,5},{5,4},{6,7},{7,6},{8,9},{9,8},{10,11... | collective-permute-start | bytes 983048 | tf_op jit(solution)/shard_map/ppermute | solution.py:275
  28.5 1.9 %collective-permute-start.6 = (bf16[768,128]{1,0:T(8,128)(2,1)S(1)}, bf16[768,128]{1,0:T(8,128)(2,1)S(1)}, u32[]{:S(2)}, u32[]{:S(2)}) collective-permute-start(bf16[768,128]{1,0:T(8,128)(2,1)S(1)} %collective-permute-done.2.refs_3_), channel_id=1, source_target_pairs={{0,1},{1,0},{2,3},{3,2},{4,5},{5,4},{6,7},{7,6},{8,9},{9,8},{10,11... | collective-permute-start | bytes 589832 | tf_op jit(solution)/shard_map/ppermute | solution.py:275
  31.2 19.2 %collective-permute-start.9 = (bf16[1792,128]{1,0:T(8,128)(2,1)S(1)}, bf16[1792,128]{1,0:T(8,128)(2,1)S(1)}, u32[]{:S(2)}, u32[]{:S(2)}) collective-permute-start(bf16[1792,128]{1,0:T(8,128)(2,1)S(1)} %get-tuple-element.52), channel_id=1, source_target_pairs={{0,4},{4,0},{8,12},{12,8},{1,5},{5,1},{9,13},{13,9},{2,6},{6,2},{1... | collective-permute-start | bytes 1376264 | tf_op jit(solution)/shard_map/ppermute | solution.py:279
  34.7 11.6 %collective-permute-start.10 = (bf16[128,128]{1,0:T(8,128)(2,1)S(1)}, bf16[128,128]{1,0:T(8,128)(2,1)S(1)}, u32[]{:S(2)}, u32[]{:S(2)}) collective-permute-start(bf16[128,128]{1,0:T(8,128)(2,1)S(1)} %get-tuple-element.54), channel_id=1, source_target_pairs={{0,8},{4,12},{8,0},{12,4},{1,9},{5,13},{9,1},{13,5},{2,10},{6,14},... | collective-permute-start | bytes 98312 | tf_op jit(solution)/shard_map/ppermute | solution.py:279
  35.8 14.1 %collective-permute-start.11 = (bf16[128,128]{1,0:T(8,128)(2,1)S(1)}, bf16[128,128]{1,0:T(8,128)(2,1)S(1)}, u32[]{:S(2)}, u32[]{:S(2)}) collective-permute-start(bf16[128,128]{1,0:T(8,128)(2,1)S(1)} %get-tuple-element.55), channel_id=1, source_target_pairs={{0,12},{4,8},{8,4},{12,0},{1,13},{5,9},{9,5},{13,1},{2,14},{6,10},... | collective-permute-start | bytes 98312 | tf_op jit(solution)/shard_map/ppermute | solution.py:279
  37.2 19.3 %collective-permute-start.7 = (bf16[640,128]{1,0:T(8,128)(2,1)S(1)}, bf16[640,128]{1,0:T(8,128)(2,1)S(1)}, u32[]{:S(2)}, u32[]{:S(2)}) collective-permute-start(bf16[640,128]{1,0:T(8,128)(2,1)S(1)} %get-tuple-element.49), channel_id=1, source_target_pairs={{0,8},{4,12},{8,0},{12,4},{1,9},{5,13},{9,1},{13,5},{2,10},{6,14},... | collective-permute-start | bytes 491528 | tf_op jit(solution)/shard_map/ppermute | solution.py:279
  39.2 17.3 %collective-permute-start.8 = (bf16[640,128]{1,0:T(8,128)(2,1)S(1)}, bf16[640,128]{1,0:T(8,128)(2,1)S(1)}, u32[]{:S(2)}, u32[]{:S(2)}) collective-permute-start(bf16[640,128]{1,0:T(8,128)(2,1)S(1)} %get-tuple-element.50), channel_id=1, source_target_pairs={{0,12},{4,8},{8,4},{12,0},{1,13},{5,9},{9,5},{13,1},{2,14},{6,10},... | collective-permute-start | bytes 491528 | tf_op jit(solution)/shard_map/ppermute | solution.py:279
  62.7 2.0 %collective-permute-start.12 = (bf16[4,128,512]{2,1,0:T(8,128)(2,1)S(1)}, bf16[4,128,512]{2,1,0:T(8,128)(2,1)S(1)}, u32[]{:S(2)}, u32[]{:S(2)}) collective-permute-start(bf16[4,128,512]{2,1,0:T(8,128)(2,1)S(1)} %get-tuple-element.61), channel_id=1, source_target_pairs={{0,1},{1,0},{2,3},{3,2},{4,5},{5,4},{6,7},{7,6},{8,9},{9,8},{10,11... | collective-permute-start | bytes 1572872 | tf_op jit(solution)/shard_map/ppermute | solution.py:275
  64.8 7.9 %collective-permute-start.13 = (bf16[128,512]{1,0:T(8,128)(2,1)S(1)}, bf16[128,512]{1,0:T(8,128)(2,1)S(1)}, u32[]{:S(2)}, u32[]{:S(2)}) collective-permute-start(bf16[128,512]{1,0:T(8,128)(2,1)S(1)} %get-tuple-element.62), channel_id=1, source_target_pairs={{0,4},{4,0},{8,12},{12,8},{1,5},{5,1},{9,13},{13,9},{2,6},{6,2},{1... | collective-permute-start | bytes 393224 | tf_op jit(solution)/shard_map/ppermute | solution.py:279
  64.8 13.0 %collective-permute-start.14 = (bf16[128,512]{1,0:T(8,128)(2,1)S(1)}, bf16[128,512]{1,0:T(8,128)(2,1)S(1)}, u32[]{:S(2)}, u32[]{:S(2)}) collective-permute-start(bf16[128,512]{1,0:T(8,128)(2,1)S(1)} %get-tuple-element.79), channel_id=1, source_target_pairs={{0,8},{4,12},{8,0},{12,4},{1,9},{5,13},{9,1},{13,5},{2,10},{6,14},... | collective-permute-start | bytes 393224 | tf_op jit(solution)/shard_map/ppermute | solution.py:279
  67.9 11.4 %collective-permute-start.16 = (f32[128,512]{1,0:T(8,128)S(1)}, f32[128,512]{1,0:T(8,128)S(1)}, u32[]{:S(2)}, u32[]{:S(2)}) collective-permute-start(f32[128,512]{1,0:T(8,128)S(1)} %get-tuple-element.77.refs_0_), channel_id=1, source_target_pairs={{0,1},{1,0},{2,3},{3,2},{4,5},{5,4},{6,7},{7,6},{8,9},{9,8},{10,11... | collective-permute-start | bytes 786440 | tf_op jit(solution)/shard_map/ppermute | solution.py:275
  67.9 10.0 %collective-permute-start.15 = (bf16[128,512]{1,0:T(8,128)(2,1)S(1)}, bf16[128,512]{1,0:T(8,128)(2,1)S(1)}, u32[]{:S(2)}, u32[]{:S(2)}) collective-permute-start(bf16[128,512]{1,0:T(8,128)(2,1)S(1)} %get-tuple-element.80), channel_id=1, source_target_pairs={{0,12},{4,8},{8,4},{12,0},{1,13},{5,9},{9,5},{13,1},{2,14},{6,10},... | collective-permute-start | bytes 393224 | tf_op jit(solution)/shard_map/ppermute | solution.py:279
  72.7 6.6 %collective-permute-start.17 = (bf16[128,512]{1,0:T(8,128)(2,1)S(1)}, bf16[128,512]{1,0:T(8,128)(2,1)S(1)}, u32[]{:S(2)}, u32[]{:S(2)}) collective-permute-start(bf16[128,512]{1,0:T(8,128)(2,1)S(1)} %collective-permute-done.13.refs_1_), channel_id=1, source_target_pairs={{0,1},{1,0},{2,3},{3,2},{4,5},{5,4},{6,7},{7,6},{8,9},{9,8},{10,11... | collective-permute-start | bytes 393224 | tf_op jit(solution)/shard_map/ppermute | solution.py:275
  77.8 1.4 %collective-permute-start.18 = (bf16[128,512]{1,0:T(8,128)(2,1)S(1)}, bf16[128,512]{1,0:T(8,128)(2,1)S(1)}, u32[]{:S(2)}, u32[]{:S(2)}) collective-permute-start(bf16[128,512]{1,0:T(8,128)(2,1)S(1)} %collective-permute-done.14.refs_2_), channel_id=1, source_target_pairs={{0,1},{1,0},{2,3},{3,2},{4,5},{5,4},{6,7},{7,6},{8,9},{9,8},{10,11... | collective-permute-start | bytes 393224 | tf_op jit(solution)/shard_map/ppermute | solution.py:275
  77.8 1.5 %collective-permute-start.19 = (bf16[128,512]{1,0:T(8,128)(2,1)S(1)}, bf16[128,512]{1,0:T(8,128)(2,1)S(1)}, u32[]{:S(2)}, u32[]{:S(2)}) collective-permute-start(bf16[128,512]{1,0:T(8,128)(2,1)S(1)} %collective-permute-done.15.refs_3_), channel_id=1, source_target_pairs={{0,1},{1,0},{2,3},{3,2},{4,5},{5,4},{6,7},{7,6},{8,9},{9,8},{10,11... | collective-permute-start | bytes 393224 | tf_op jit(solution)/shard_map/ppermute | solution.py:275
